TPU v7x, 32 devices: a whole 2x2x4 slice. The times are simulated.
32 devices in a mesh: vir: 8 (over z, x), ph: 2 (over y), vec: 2 (over core).
Axes of the slice: x: 2, y: 2, z: 4, core: 2. Of those that a mesh axis runs over, the one named last changes fastest.
Arguments:
- vv_factor: bfloat16 [1024, 1024, 1024], P(('ph', 'vec'), 'vir'), may hold values from -0.1875 to 0.1875
- ladder_amp: bfloat16 [1024, 1024, 256], P(None, 'vir'), may hold values from -0.1875 to 0.1875
- cycle_amp: bfloat16 [1024, 32, 128], P(('vir', 'ph'), None, 'vec'), may hold values from -0.015625 to 0.015625
- ov_slots: bfloat16 [2048, 1024, 128], P(('vir', 'ph'), None, 'vec'), may hold values from -6 to 6
- owner_of: int32 [1024], P(('vir', 'ph')), may hold values from 0 to 1, as said below
- slot_of: int32 [1024], P(('vir', 'ph')), may hold values from 0 to 127, as said below
- ov_pairs: bfloat16 [1024, 8, 1024], P(('ph', 'vec'), None, 'vir'), may hold values from -0.1875 to 0.1875
- eps_vir: float32 [1024], replicated, may hold values from 0.5 to 3
- eps_occ: float32 [128], replicated, may hold values from -3 to -0.5
Outputs:
- residual: bfloat16 [1024, 256], P('vir', ('ph', 'vec'))
- update: float32 [1024, 256], P('vir', ('ph', 'vec'))
Inputs may be any that keep to these rules, and one draw needn't show every extreme that they name: `owner_of`: within each run of 128 consecutive blocks (one vir index) one owner holds exactly 128 blocks and no owner more. `slot_of`: distinct among the blocks of one run with the same owner.
All inputs are finite; a program needn't handle non-finite values.
Results may differ from a plain program's by a relative error of at most 0.0055.
Values may be sent and summed in bfloat16 or wider, within the bound.
No kernel may reach another device: no remote copies, remote signals or barrier semaphores. Data moves between devices by JAX's collectives and lax.ppermute only.
A program may use at most 320 MiB of HBM per device.

v0:
```python
import functools

import jax
import jax.numpy as jnp
from jax import lax
from jax.experimental import pallas as pl
from jax.experimental.pallas import tpu as pltpu
from jax.sharding import PartitionSpec as P

LANES = 128
bf16, f32 = jnp.bfloat16, jnp.float32


def plain(
    vv_factor, ladder_amp, cycle_amp, ov_slots, owner_of, slot_of, ov_pairs, eps_vir, eps_occ
):
    chol_local, slab_width, virtuals = vv_factor.shape
    pair_count = ladder_amp.shape[2]
    row_piece = vv_factor[:, :, 0]
    factor_row = lax.all_gather(row_piece, "vir", axis=1, tiled=True)
    half = jnp.dot(
        factor_row,
        ladder_amp.reshape(virtuals, slab_width * pair_count),
        preferred_element_type=jnp.float32,
    )
    half = half.astype(jnp.bfloat16).reshape(chol_local * slab_width, pair_count)
    flat_factor = vv_factor.reshape(chol_local * slab_width, virtuals)
    block_local, occ_rows, block_part = cycle_amp.shape
    owner_total = lax.axis_size("ph")
    targets = owner_of[None, :] == jnp.arange(owner_total, dtype=jnp.int32)[:, None]
    outgoing = jnp.where(targets[:, :, None, None], cycle_amp[None], jnp.zeros((), jnp.bfloat16))
    places = jnp.where(targets, slot_of[None, :], 0)
    arrived, arrived_slots = (
        lax.all_to_all(outgoing, "ph", split_axis=0, concat_axis=0, tiled=True),
        lax.all_to_all(places, "ph", split_axis=0, concat_axis=0, tiled=True),
    )
    capacity = ov_slots.shape[0]
    picks = (
        arrived_slots.reshape(-1)[:, None] == jnp.arange(capacity, dtype=jnp.int32)[None, :]
    ).astype(jnp.bfloat16)
    arranged = jnp.einsum(
        "ns,niw->siw",
        picks,
        arrived.reshape(-1, occ_rows, block_part),
        preferred_element_type=jnp.float32,
    )
    arranged = arranged.astype(jnp.bfloat16)
    cycle_part = jnp.einsum("siw,spw->ip", arranged, ov_slots, preferred_element_type=jnp.float32)
    near_groups = lax.axis_size("ph") * lax.axis_size("vec")
    summed = lax.psum(cycle_part, ("vir", "ph", "vec"))
    vector_share = summed.shape[1] // near_groups
    own_share = lax.dynamic_slice_in_dim(
        summed, lax.axis_index(("ph", "vec")) * vector_share, vector_share, 1
    )
    coupling = own_share.astype(jnp.bfloat16)
    second_count = ov_pairs.shape[1]
    cycle_term = jnp.einsum("ip,pjb->bij", coupling, ov_pairs, preferred_element_type=jnp.float32)
    cycle_term = cycle_term.reshape(slab_width, occ_rows * second_count)
    slab_start = lax.axis_index("vir") * slab_width
    slab = (
        lax.psum_scatter(
            lax.dot_general(
                flat_factor, half, (((0,), (0,)), ((), ())), preferred_element_type=jnp.float32
            ),
            "vir",
            scatter_dimension=0,
            tiled=True,
        )
        + cycle_term
    )
    result = lax.psum_scatter(slab, ("ph", "vec"), scatter_dimension=1, tiled=True)
    residual = result.astype(jnp.bfloat16)
    share_width = result.shape[1]
    pair_index = lax.axis_index(("ph", "vec")) * share_width + jnp.arange(
        share_width, dtype=jnp.int32
    )
    occ_count = eps_occ.shape[0]
    occ_ids = jnp.arange(occ_count, dtype=jnp.int32)[None, :]
    first_occ = jnp.sum(
        jnp.where((pair_index // second_count)[:, None] == occ_ids, eps_occ[None, :], 0.0), 1
    )
    second_occ = jnp.sum(
        jnp.where((pair_index % second_count)[:, None] == occ_ids, eps_occ[None, :], 0.0), 1
    )
    slab_energy = lax.dynamic_slice_in_dim(eps_vir, slab_start, slab_width, 0)
    denominator = (eps_vir[0] + slab_energy)[:, None] - first_occ[None, :] - second_occ[None, :]
    update = residual.astype(jnp.float32) / denominator
    return (residual, update)


def shifted(x, axes, k):
    n = lax.axis_size(axes)
    return lax.ppermute(x, axes, [(i, (i + k) % n) for i in range(n)])


def round_robin(x, axes):
    return [x] + [shifted(x, axes, k) for k in range(1, lax.axis_size(axes))]


def row_kernel(*refs):
    (*x_refs, out_ref, acc) = refs
    step, rows = pl.program_id(1), x_refs[0].shape[0]
    lane = lax.broadcasted_iota(jnp.int32, acc.shape, 1)

    @pl.when(step == 0)
    def _():
        acc[...] = jnp.zeros_like(acc)

    part = jnp.zeros(acc.shape, f32)
    for q, ref in enumerate(x_refs):
        for p in range(rows):
            shift = q * rows + p
            column = ref[p].astype(f32)
            part = jnp.where(lane == shift, pltpu.roll(column, shift, 1) if shift else column, part)
    rows = rows * len(x_refs)
    part = pltpu.roll(part, step * rows, 1)
    acc[...] = jnp.where(lane // rows == step, part, acc[...])

    @pl.when(step == pl.num_programs(1) - 1)
    def _():
        piece = acc[...].T.astype(bf16)
        for k in range(out_ref.shape[0]):
            out_ref[k] = piece


def own_row(vv_factor, copies):
    chol, slab, _ = vv_factor.shape
    rows, sides = 16, 4
    steps = LANES // (rows * sides)

    def side(q):
        return pl.BlockSpec((rows, slab, LANES), lambda g, k: ((g * steps + k) * sides + q, 0, 0))

    return pl.pallas_call(
        row_kernel,
        grid=(chol // LANES, steps),
        in_specs=[side(q) for q in range(sides)],
        out_specs=pl.BlockSpec((copies, LANES, slab), lambda g, k: (0, g, 0)),
        out_shape=jax.ShapeDtypeStruct((copies, chol, slab), bf16),
        scratch_shapes=[pltpu.VMEM((slab, LANES), f32)],
        compiler_params=pltpu.CompilerParams(vmem_limit_bytes=32 << 20),
        cost_estimate=pl.CostEstimate(
            flops=2 * chol * slab * LANES, bytes_accessed=2 * chol * slab * LANES, transcendentals=0
        ),
    )(*[vv_factor] * sides)


def cycle_kernel(shares, place_ref, code_ref, *refs):
    (*amp_refs, ov_ref, out_ref, amps, acc, block_of) = refs
    step = pl.program_id(0)
    blocks, slots = code_ref.shape[0], block_of.shape[0]
    own, width = 2 * amp_refs[0].shape[0], amps.shape[2]

    @pl.when(step == 0)
    def _():
        for k, ref in enumerate(amp_refs):
            for h in range(2):
                amps[pl.ds(k * own + h * (own // 2), own // 2)] = ref[
                    :, :, h * width : (h + 1) * width
                ]
        amps[blocks] = jnp.zeros(amps.shape[1:], bf16)
        acc[...] = jnp.zeros_like(acc)
        first = place_ref[0] * slots

        @pl.loop(0, slots)
        def _(s):
            block_of[s] = blocks

        @pl.loop(0, blocks)
        def _(n):
            slot = code_ref[n] - first

            @pl.when((slot >= 0) & (slot < slots))
            def _():
                block_of[slot] = n

    here, _, chol = ov_ref.shape
    left = jnp.concatenate([amps[block_of[step * here + s]] for s in range(here)], axis=1)
    right = ov_ref[...].reshape(here * width, chol)
    acc[...] += jnp.dot(left, right, preferred_element_type=f32)

    @pl.when(step == pl.num_programs(0) - 1)
    def _():
        share = chol // shares
        for k in range(out_ref.shape[0]):
            start = k % shares * share
            out_ref[k] = acc[:, start : start + share]


def cycle_operands(cycle_amp, owner_of, slot_of, slots):
    codes = jnp.concatenate(round_robin(owner_of * slots + slot_of, "ph"))
    near, far = jnp.split(cycle_amp, 2, 0)
    return round_robin(jnp.concatenate([near, far], 2), "ph"), codes


def cycle_partial(amps, codes, ov_slots):
    slots, chol, width = ov_slots.shape
    occ = amps[0].shape[1]
    shares = lax.axis_size(("ph", "vec"))
    copies = shares * lax.axis_size("vir")
    place = lax.axis_index("ph").astype(jnp.int32)[None]
    here = 32
    whole = pl.BlockSpec(memory_space=pltpu.VMEM)
    scalars = pl.BlockSpec(memory_space=pltpu.SMEM)
    return pl.pallas_call(
        functools.partial(cycle_kernel, shares),
        grid=(slots // here,),
        in_specs=[scalars, scalars]
        + [whole] * len(amps)
        + [pl.BlockSpec((here, width, chol), lambda i: (i, 0, 0))],
        out_specs=pl.BlockSpec((copies, occ, chol // shares), lambda i: (0, 0, 0)),
        out_shape=jax.ShapeDtypeStruct((copies, occ, chol // shares), f32),
        scratch_shapes=[
            pltpu.VMEM((codes.shape[0] + 1, occ, width), bf16),
            pltpu.VMEM((occ, chol), f32),
            pltpu.SMEM((slots,), jnp.int32),
        ],
        compiler_params=pltpu.CompilerParams(vmem_limit_bytes=60 << 20),
        cost_estimate=pl.CostEstimate(
            flops=2 * occ * slots * width * chol,
            bytes_accessed=2 * slots * width * chol,
            transcendentals=0,
        ),
    )(place, codes, *amps, jnp.swapaxes(ov_slots, 1, 2))


def swap_matrix(deep):
    n = deep * deep
    r = lax.broadcasted_iota(jnp.int32, (n, n), 0)
    s = lax.broadcasted_iota(jnp.int32, (n, n), 1)
    return (lax.rem(r, deep) * deep + lax.div(r, deep) == s).astype(bf16)


def ladder_kernel(row_ref, amp_ref, factor_ref, out_ref, swap, turned, half):
    virtuals, deep, pairs = amp_ref.shape
    count, chol, _ = row_ref.shape
    square = deep * deep

    @pl.when(pl.program_id(0) == 0)
    def _():
        out_ref[...] = jnp.zeros_like(out_ref)
        swap[...] = swap_matrix(deep)

    group = 8

    @pl.loop(0, virtuals // (deep * group))
    def _(k):
        for q in range(0, group, 2):
            here = [pl.ds(pl.multiple_of((k * group + q + r) * deep, deep), deep) for r in range(2)]
            block = jnp.concatenate([amp_ref[h].reshape(square, pairs) for h in here], axis=1)
            block = jnp.dot(swap[...], block, preferred_element_type=f32).astype(bf16)
            for r, h in enumerate(here):
                part = block[:, r * pairs : (r + 1) * pairs]
                turned[:, h, :] = part.reshape(deep, deep, pairs)

    row = jnp.concatenate([row_ref[k] for k in range(count)], axis=1)
    for d in range(0, deep, 2):
        block = jnp.concatenate([turned[d], turned[d + 1]], axis=1)
        block = jnp.dot(row, block, preferred_element_type=f32).astype(bf16)
        half[d], half[d + 1] = block[:, :pairs], block[:, pairs:]

    join = 4

    @pl.loop(0, chol // (deep * join))
    def _(k):
        parts = []
        for q in range(0, join, 2):
            here = [pl.ds(pl.multiple_of((k * join + q + r) * deep, deep), deep) for r in range(2)]
            block = jnp.concatenate([half[:, h, :].reshape(square, pairs) for h in here], axis=1)
            block = jnp.dot(swap[...], block, preferred_element_type=f32).astype(bf16)
            parts += [block[:, :pairs], block[:, pairs:]]
        flat = jnp.concatenate(parts, axis=0)
        start = pl.multiple_of(k * join * deep, deep)
        block = factor_ref[pl.ds(start, join * deep)]
        out_ref[...] += lax.dot_general(
            flat,
            block.reshape(join * square, block.shape[2]),
            (((0,), (0,)), ((), ())),
            preferred_element_type=f32,
        )


def ladder_partial(row, ladder_amp, vv_factor):
    virtuals, slab, pairs = ladder_amp.shape
    chol = vv_factor.shape[0]
    deep = 16
    return pl.pallas_call(
        ladder_kernel,
        grid=(slab // deep,),
        in_specs=[
            pl.BlockSpec(memory_space=pltpu.VMEM),
            pl.BlockSpec((virtuals, deep, pairs), lambda i: (0, i, 0)),
            pl.BlockSpec((chol, deep, virtuals), lambda i: (0, i, 0)),
        ],
        out_specs=pl.BlockSpec((pairs, virtuals), lambda i: (0, 0)),
        out_shape=jax.ShapeDtypeStruct((pairs, virtuals), f32),
        scratch_shapes=[
            pltpu.VMEM((deep * deep, deep * deep), bf16),
            pltpu.VMEM((deep, virtuals, pairs), bf16),
            pltpu.VMEM((deep, chol, pairs), bf16),
        ],
        compiler_params=pltpu.CompilerParams(vmem_limit_bytes=60 << 20),
        cost_estimate=pl.CostEstimate(
            flops=4 * chol * virtuals * slab * pairs,
            bytes_accessed=2 * virtuals * slab * (pairs + chol),
            transcendentals=0,
        ),
    )(row, ladder_amp, vv_factor)


def scatter_sum(x, axes):
    n = lax.axis_size(axes)
    me = lax.axis_index(axes)
    total = lax.dynamic_index_in_dim(x, me, 0, keepdims=False)
    sent = x.astype(bf16)
    for k in range(1, n):
        piece = lax.dynamic_index_in_dim(sent, (me + k) % n, 0, keepdims=False)
        total = total + shifted(piece, axes, k).astype(f32)
    return total


def local(
    vv_factor, ladder_amp, cycle_amp, ov_slots, owner_of, slot_of, ov_pairs, eps_vir, eps_occ
):
    chol, slab, virtuals = vv_factor.shape
    pairs = ladder_amp.shape[2]
    slots, _, width = ov_slots.shape
    n_vir, n_ph, n_vec = (lax.axis_size(a) for a in ("vir", "ph", "vec"))
    fits = slab == LANES and pairs == 2 * LANES and chol % LANES == 0 and slots % 32 == 0
    if not fits or 256 % width or cycle_amp.shape[0] % 2:
        return plain(
            vv_factor, ladder_amp, cycle_amp, ov_slots, owner_of, slot_of, ov_pairs, eps_vir, eps_occ
        )
    amps, codes = cycle_operands(cycle_amp, owner_of, slot_of, slots)
    row, amps, codes = lax.optimization_barrier((own_row(vv_factor, n_vir), amps, codes))
    row = lax.all_to_all(row, "vir", 0, 0)
    pieces = lax.all_to_all(cycle_partial(amps, codes, ov_slots), ("vir", "ph", "vec"), 0, 0)
    coupling = jnp.sum(pieces, 0).astype(bf16)
    second_count = ov_pairs.shape[1]
    cycle_term = jnp.einsum("ip,pjb->ijb", coupling, ov_pairs, preferred_element_type=f32)
    cycle_term = cycle_term.reshape(pairs, slab)

    ladder = ladder_partial(row, ladder_amp, vv_factor)
    vir = lax.axis_index("vir")
    share = pairs // (n_ph * n_vec)
    own = jnp.arange(n_vir, dtype=jnp.int32)[None, :, None] == vir
    total = ladder.reshape(pairs, n_vir, slab) + jnp.where(own, cycle_term[:, None, :], 0.0)
    total = total.reshape(n_ph, n_vec, share, virtuals)
    total = scatter_sum(jnp.swapaxes(total, 0, 1), "vec").astype(bf16)
    total = total.reshape(n_ph, share, n_vir, slab).transpose(2, 0, 1, 3)
    total = lax.all_to_all(total.reshape(n_vir * n_ph, share, slab), ("vir", "ph"), 0, 0)
    total = jnp.sum(total.astype(f32), 0)

    residual = total.T.astype(bf16)
    place = lax.axis_index(("ph", "vec"))
    pair_index = place * share + jnp.arange(share, dtype=jnp.int32)
    occ_ids = jnp.arange(eps_occ.shape[0], dtype=jnp.int32)[None, :]
    first_occ = jnp.sum(
        jnp.where((pair_index // second_count)[:, None] == occ_ids, eps_occ[None, :], 0.0), 1
    )
    second_occ = jnp.sum(
        jnp.where((pair_index % second_count)[:, None] == occ_ids, eps_occ[None, :], 0.0), 1
    )
    slab_energy = lax.dynamic_slice_in_dim(eps_vir, vir * slab, slab, 0)
    denominator = (eps_vir[0] + slab_energy)[:, None] - first_occ[None, :] - second_occ[None, :]
    update = residual.astype(f32) / denominator
    return residual, update


def solution(mesh):
    placed = (
        P(("ph", "vec"), "vir", None),
        P(None, "vir", None),
        P(("vir", "ph"), None, "vec"),
        P(("vir", "ph"), None, "vec"),
        P(("vir", "ph")),
        P(("vir", "ph")),
        P(("ph", "vec"), None, "vir"),
        P(),
        P(),
    )
    return jax.shard_map(
        local,
        mesh=mesh,
        in_specs=placed,
        out_specs=(P("vir", ("ph", "vec")), P("vir", ("ph", "vec"))),
        check_vma=False,
    )
```

profile of v0, /device:TPU:0, one launch (start us, length us, event | category | flops | bytes accessed | tf_op | source)
XLA Modules:
  0.0 144.7 jit_solution(8611637462456867426)
XLA Ops:
  0.6 0.0 copy-start
  0.6 1.1 fusion.6
  1.8 0.1 pad_maximum_fusion.refs_0_
  1.9 3.0 %collective-permute-start = (bf16[32,32,128]{2,1,0:T(8,128)(2,1)S(1)}, bf16[32,32,128]{2,1,0:T(8,128)(2,1)S(1)}, u32[]{:S(2)}, u32[]{:S(2)}) collective-permute-start(bf16[32,32,128]{2,1,0:T(8,128)(2,1)S(1)} %pad_maximum_fusion.refs_0_), channel_id=1, source_target_pairs={{0,2},{2,0},{1,3},{3,1},{4,6},{6,4},{5,7},{7,5},{8,10},{10,8},{9,1... | collective-permute-start | bytes 786440 | tf_op jit(solution)/shard_map/ppermute | solution.py:93
  5.0 0.7 multiply_add_fusion
  5.6 0.0 collective-permute-start.1
  5.7 6.4 %shard_map.104 = bf16[8,256,128]{2,1,0:T(8,128)(2,1)} custom-call(bf16[256,128,1024]{2,1,0:T(8,128)(2,1)} %factor_ref.1, bf16[256,128,1024]{2,1,0:T(8,128)(2,1)} %factor_ref.1, bf16[256,128,1024]{2,1,0:T(8,128)(2,1)} %factor_ref.1, bf16[256,128,1024]{2,1,0:T(8,128)(2,1)} %factor_ref.1), custom_call_target="tpu_custom_call" | custom-call | flops 8388608 | bytes 8388608 | tf_op jit(solution)/shard_map/pallas_call | solution.py:134
  12.1 0.6 pad_add_fusion.code_ref
  12.7 6.3 %all-to-all-start = ((bf16[8,256,128]{2,1,0:T(8,128)(2,1)}), bf16[8,256,128]{2,1,0:T(8,128)(2,1)S(1)}, u32[]{:S(2)}, u32[]{:S(2)}) async-start(bf16[8,256,128]{2,1,0:T(8,128)(2,1)} %shard_map.104), calls=%async_computation | async-start | bytes 1048576 | tf_op jit(solution)/shard_map/all_to_all | solution.py:336
  19.0 0.1 broadcast_bitcast_fusion
  19.0 11.3 %shard_map.106 = f32[32,32,256]{2,1,0:T(8,128)} custom-call(s32[1]{0:T(128)} %bitcast.2.place_ref, s32[128]{0:T(128)} %pad_add_fusion.code_ref, bf16[32,32,128]{2,1,0:T(8,128)(2,1)} %copy-done.2, bf16[32,32,128]{2,1,0:T(8,128)(2,1)} %copy-done.3, bf16[128,64,1024]{2,1,0:T(8,128)(2,1)} %bitcast.29), custom_call_target="tpu_custom_call" | custom-call | flops 536870912 | bytes 16777216 | tf_op jit(solution)/shard_map/pallas_call | solution.py:205
  30.4 2.6 %all-to-all-done.row_ref = bf16[8,256,128]{2,1,0:T(8,128)(2,1)S(1)} async-done(((bf16[8,256,128]{2,1,0:T(8,128)(2,1)}), bf16[8,256,128]{2,1,0:T(8,128)(2,1)S(1)}, u32[]{:S(2)}, u32[]{:S(2)}) %all-to-all-start) | async-done | bytes 524320 | tf_op jit(solution)/shard_map/all_to_all | solution.py:336
  32.9 3.7 %all-to-all-start.1 = ((f32[32,32,256]{2,1,0:T(8,128)}), f32[32,32,256]{2,1,0:T(8,128)S(1)}, u32[]{:S(2)}, u32[]{:S(2)}) async-start(f32[32,32,256]{2,1,0:T(8,128)} %shard_map.106), calls=%async_computation.1 | async-start | bytes 2097152 | tf_op jit(solution)/shard_map/all_to_all | solution.py:337
  36.6 0.0 copy-start.5
  36.6 85.7 %shard_map.105 = f32[256,1024]{1,0:T(8,128)} custom-call(bf16[8,256,128]{2,1,0:T(8,128)(2,1)} %copy-done.1, bf16[1024,128,256]{2,1,0:T(8,128)(2,1)} %amp_ref.1, bf16[256,128,1024]{2,1,0:T(8,128)(2,1)} %factor_ref.1), custom_call_target="tpu_custom_call" | custom-call | flops 34359738368 | bytes 134217728 | tf_op jit(solution)/shard_map/pallas_call | solution.py:287
  122.4 0.1 reduce_sum.39
  122.4 0.2 fusion.1
  122.6 0.1 copy.24
  122.7 0.1 broadcast_in_dim.61
  122.8 0.2 broadcast_in_dim.62
  123.0 1.4 select_add_fusion
  124.4 0.3 collective-permute-start.2
  124.7 1.3 collective-permute-done.2
  126.0 0.1 fusion
  126.2 0.8 copy.19
  126.9 6.8 %all-to-all-start.2 = ((bf16[16,64,128]{2,1,0:T(8,128)(2,1)}), bf16[16,64,128]{2,1,0:T(8,128)(2,1)S(1)}, u32[]{:S(2)}, u32[]{:S(2)}) async-start(bf16[16,64,128]{2,1,0:T(8,128)(2,1)} %bitcast.9), calls=%async_computation.2 | async-start | bytes 524288 | tf_op jit(solution)/shard_map/all_to_all | solution.py:351
  133.8 1.2 slice.3
  135.0 1.4 dynamic-slice_add_fusion
  136.4 0.2 select_reduce_fusion.1
  136.6 7.4 %all-to-all-done.2 = bf16[16,64,128]{2,1,0:T(8,128)(2,1)S(1)} async-done(((bf16[16,64,128]{2,1,0:T(8,128)(2,1)}), bf16[16,64,128]{2,1,0:T(8,128)(2,1)S(1)}, u32[]{:S(2)}, u32[]{:S(2)}) %all-to-all-start.2) | async-done | bytes 262176 | tf_op jit(solution)/shard_map/all_to_all | solution.py:351
  144.0 0.0 copy-start.4
  144.0 0.7 subtract_divide_fusion
  (18 shorter events, 0.2 us)
Async XLA Ops:
  0.6 121.8 %copy-start = (bf16[256,8,128]{2,1,0:T(8,128)(2,1)S(1)}, bf16[256,8,128]{2,1,0:T(8,128)(2,1)}, u32[]{:S(2)}) copy-start(bf16[256,8,128]{2,1,0:T(8,128)(2,1)} %param.15) | copy-start | bytes 1572868
  1.9 10.2 %copy-start.2 = (bf16[32,32,128]{2,1,0:T(8,128)(2,1)}, bf16[32,32,128]{2,1,0:T(8,128)(2,1)S(1)}, u32[]{:S(2)}) copy-start(bf16[32,32,128]{2,1,0:T(8,128)(2,1)S(1)} %pad_maximum_fusion.refs_0_) | copy-start | bytes 786436
  1.9 10.7 %collective-permute-start = (bf16[32,32,128]{2,1,0:T(8,128)(2,1)S(1)}, bf16[32,32,128]{2,1,0:T(8,128)(2,1)S(1)}, u32[]{:S(2)}, u32[]{:S(2)}) collective-permute-start(bf16[32,32,128]{2,1,0:T(8,128)(2,1)S(1)} %pad_maximum_fusion.refs_0_), channel_id=1, source_target_pairs={{0,2},{2,0},{1,3},{3,1},{4,6},{6,4},{5,7},{7,5},{8,10},{10,8},{9,1... | collective-permute-start | bytes 786440 | tf_op jit(solution)/shard_map/ppermute | solution.py:93
  5.6 6.4 %collective-permute-start.1 = (s32[64]{0:T(128)S(1)}, s32[64]{0:T(128)S(1)}, u32[]{:S(2)}, u32[]{:S(2)}) collective-permute-start(s32[64]{0:T(128)S(1)} %multiply_add_fusion), channel_id=1, source_target_pairs={{0,2},{2,0},{1,3},{3,1},{4,6},{6,4},{5,7},{7,5},{8,10},{10,8},{9,1... | collective-permute-start | bytes 776 | tf_op jit(solution)/shard_map/ppermute | solution.py:93
  12.7 6.4 %copy-start.3 = (bf16[32,32,128]{2,1,0:T(8,128)(2,1)}, bf16[32,32,128]{2,1,0:T(8,128)(2,1)S(1)}, u32[]{:S(2)}) copy-start(bf16[32,32,128]{2,1,0:T(8,128)(2,1)S(1)} %collective-permute-done.refs_1_) | copy-start | bytes 786436
  12.7 20.2 %all-to-all-start = ((bf16[8,256,128]{2,1,0:T(8,128)(2,1)}), bf16[8,256,128]{2,1,0:T(8,128)(2,1)S(1)}, u32[]{:S(2)}, u32[]{:S(2)}) async-start(bf16[8,256,128]{2,1,0:T(8,128)(2,1)} %shard_map.104), calls=%async_computation | async-start | bytes 1048576 | tf_op jit(solution)/shard_map/all_to_all | solution.py:336
  32.9 3.7 %copy-start.1 = (bf16[8,256,128]{2,1,0:T(8,128)(2,1)}, bf16[8,256,128]{2,1,0:T(8,128)(2,1)S(1)}, u32[]{:S(2)}) copy-start(bf16[8,256,128]{2,1,0:T(8,128)(2,1)S(1)} %all-to-all-done.row_ref) | copy-start | bytes 1572868
  32.9 89.4 %all-to-all-start.1 = ((f32[32,32,256]{2,1,0:T(8,128)}), f32[32,32,256]{2,1,0:T(8,128)S(1)}, u32[]{:S(2)}, u32[]{:S(2)}) async-start(f32[32,32,256]{2,1,0:T(8,128)} %shard_map.106), calls=%async_computation.1 | async-start | bytes 2097152 | tf_op jit(solution)/shard_map/all_to_all | solution.py:337
  36.6 99.8 %copy-start.5 = (f32[128]{0:T(128)S(1)}, f32[128]{0:T(128)}, u32[]{:S(2)}) copy-start(f32[128]{0:T(128)} %param.17) | copy-start | bytes 1540
  124.4 1.6 %collective-permute-start.2 = (bf16[2,64,1024]{2,1,0:T(8,128)(2,1)S(1)}, bf16[2,64,1024]{2,1,0:T(8,128)(2,1)S(1)}, u32[]{:S(2)}, u32[]{:S(2)}) collective-permute-start(bf16[2,64,1024]{2,1,0:T(8,128)(2,1)S(1)} %fusion.3), channel_id=1, source_target_pairs={{0,1},{1,0},{2,3},{3,2},{4,5},{5,4},{6,7},{7,6},{8,9},{9,8},{10,11... | collective-permute-start | bytes 786440 | tf_op jit(solution)/shard_map/ppermute | solution.py:93
  126.9 17.0 %all-to-all-start.2 = ((bf16[16,64,128]{2,1,0:T(8,128)(2,1)}), bf16[16,64,128]{2,1,0:T(8,128)(2,1)S(1)}, u32[]{:S(2)}, u32[]{:S(2)}) async-start(bf16[16,64,128]{2,1,0:T(8,128)(2,1)} %bitcast.9), calls=%async_computation.2 | async-start | bytes 524288 | tf_op jit(solution)/shard_map/all_to_all | solution.py:351
  144.0 0.7 copy-start.4
where the time goes:
time: 145 us
  Pallas kernels  103 us (71%)
  starting transfers between devices  20.2 us (14%)
  waiting for transfers between devices  11.2 us (8%)
  other arithmetic  5.28 us (4%)
  local copies, waits for them, and re-layouts  3.61 us (2%)
    pallas_call x1, Pallas kernels, ladder_partial(): pl.pallas_call(ladder_kernel, grid=(slab // deep,), in_specs=[pl.BlockSpe...  85.7 us
    pallas_call x1, Pallas kernels, cycle_partial(): pl.pallas_call(functools.partial(cycle_kernel, shares), grid=(slots // he...  11.3 us
    all_to_all x1, waiting for transfers between devices, local(): lax.all_to_all(total.reshape(n_vir * n_ph, share, slab), ('vir', 'ph'), 0...  7.36 us
    all_to_all x1, starting transfers between devices, local(): lax.all_to_all(total.reshape(n_vir * n_ph, share, slab), ('vir', 'ph'), 0...  6.85 us
    pallas_call x1, Pallas kernels, own_row(): pl.pallas_call(row_kernel, grid=(chol // LANES, steps), in_specs=[side(q)...  6.4 us
    all_to_all x1, starting transfers between devices, local(): row = lax.all_to_all(row, 'vir', 0, 0)  6.28 us
    all_to_all x1, starting transfers between devices, local(): lax.all_to_all(cycle_partial(amps, codes, ov_slots), ('vir', 'ph', 'vec')...  3.68 us
    ppermute x3, starting transfers between devices, shifted(): return lax.ppermute(x, axes, [(i, (i + k) % n) for i in range(n)])  3.39 us
  transfers between devices with their start and end apart: 6, of which 3 were waited for; matrix products, arithmetic and copies ran while one was open for 3% of the time, Pallas kernels for 71%

commit v1 on v0

--- a/solution.py
+++ b/solution.py
@@ -145,8 +145,9 @@
     )(*[vv_factor] * sides)
 
 
-def cycle_kernel(shares, place_ref, code_ref, *refs):
-    (*amp_refs, ov_ref, out_ref, amps, acc, block_of) = refs
+def cycle_kernel(shares, groups, place_ref, code_ref, *refs):
+    (*amp_refs, out_ref, amps, acc, block_of) = refs
+    amp_refs, ov_refs = amp_refs[:groups], amp_refs[groups:]
     step = pl.program_id(0)
     blocks, slots = code_ref.shape[0], block_of.shape[0]
     own, width = 2 * amp_refs[0].shape[0], amps.shape[2]
@@ -174,10 +175,12 @@
             def _():
                 block_of[slot] = n
 
-    here, _, chol = ov_ref.shape
-    left = jnp.concatenate([amps[block_of[step * here + s]] for s in range(here)], axis=1)
-    right = ov_ref[...].reshape(here * width, chol)
-    acc[...] += jnp.dot(left, right, preferred_element_type=f32)
+    here, _, chol = ov_refs[0].shape
+    for side, ref in enumerate(ov_refs):
+        start = (step * len(ov_refs) + side) * here
+        left = jnp.concatenate([amps[block_of[start + s]] for s in range(here)], axis=1)
+        right = ref[...].reshape(here * width, chol)
+        acc[...] += jnp.dot(left, right, preferred_element_type=f32)
 
     @pl.when(step == pl.num_programs(0) - 1)
     def _():
@@ -199,15 +202,19 @@
     shares = lax.axis_size(("ph", "vec"))
     copies = shares * lax.axis_size("vir")
     place = lax.axis_index("ph").astype(jnp.int32)[None]
-    here = 32
+    here, sides = 8, 4
+
+    def side(q):
+        return pl.BlockSpec((here, width, chol), lambda i: (i * sides + q, 0, 0))
+
     whole = pl.BlockSpec(memory_space=pltpu.VMEM)
     scalars = pl.BlockSpec(memory_space=pltpu.SMEM)
     return pl.pallas_call(
-        functools.partial(cycle_kernel, shares),
-        grid=(slots // here,),
+        functools.partial(cycle_kernel, shares, len(amps)),
+        grid=(slots // (here * sides),),
         in_specs=[scalars, scalars]
         + [whole] * len(amps)
-        + [pl.BlockSpec((here, width, chol), lambda i: (i, 0, 0))],
+        + [side(q) for q in range(sides)],
         out_specs=pl.BlockSpec((copies, occ, chol // shares), lambda i: (0, 0, 0)),
         out_shape=jax.ShapeDtypeStruct((copies, occ, chol // shares), f32),
         scratch_shapes=[
@@ -221,7 +228,7 @@
             bytes_accessed=2 * slots * width * chol,
             transcendentals=0,
         ),
-    )(place, codes, *amps, jnp.swapaxes(ov_slots, 1, 2))
+    )(place, codes, *amps, *[jnp.swapaxes(ov_slots, 1, 2)] * sides)
 
 
 def swap_matrix(deep):
@@ -231,8 +238,11 @@
     return (lax.rem(r, deep) * deep + lax.div(r, deep) == s).astype(bf16)
 
 
-def ladder_kernel(row_ref, amp_ref, factor_ref, out_ref, swap, turned, half):
-    virtuals, deep, pairs = amp_ref.shape
+def ladder_kernel(row_ref, *refs):
+    (*in_refs, out_ref, swap, turned, half) = refs
+    sides = len(in_refs) // 2
+    amp_refs, factor_refs = in_refs[:sides], in_refs[sides:]
+    virtuals, deep, pairs = amp_refs[0].shape
     count, chol, _ = row_ref.shape
     square = deep * deep
 
@@ -242,16 +252,18 @@
         swap[...] = swap_matrix(deep)
 
     group = 8
-
-    @pl.loop(0, virtuals // (deep * group))
-    def _(k):
-        for q in range(0, group, 2):
-            here = [pl.ds(pl.multiple_of((k * group + q + r) * deep, deep), deep) for r in range(2)]
-            block = jnp.concatenate([amp_ref[h].reshape(square, pairs) for h in here], axis=1)
-            block = jnp.dot(swap[...], block, preferred_element_type=f32).astype(bf16)
-            for r, h in enumerate(here):
-                part = block[:, r * pairs : (r + 1) * pairs]
-                turned[:, h, :] = part.reshape(deep, deep, pairs)
+    for side, amp_ref in enumerate(amp_refs):
+
+        @pl.loop(0, virtuals // (deep * group))
+        def _(k):
+            for q in range(0, group, 2):
+                start = [pl.multiple_of((k * group + q + r) * deep, deep) for r in range(2)]
+                block = [amp_ref[pl.ds(s, deep)].reshape(square, pairs) for s in start]
+                block = jnp.concatenate(block, axis=1)
+                block = jnp.dot(swap[...], block, preferred_element_type=f32).astype(bf16)
+                for r, s in enumerate(start):
+                    part = block[:, r * pairs : (r + 1) * pairs].reshape(deep, deep, pairs)
+                    turned[:, pl.ds(side * virtuals + s, deep), :] = part
 
     row = jnp.concatenate([row_ref[k] for k in range(count)], axis=1)
     for d in range(0, deep, 2):
@@ -259,22 +271,18 @@
         block = jnp.dot(row, block, preferred_element_type=f32).astype(bf16)
         half[d], half[d + 1] = block[:, :pairs], block[:, pairs:]
 
-    join = 4
-
-    @pl.loop(0, chol // (deep * join))
-    def _(k):
+    for side, factor_ref in enumerate(factor_refs):
         parts = []
+        join = factor_ref.shape[0] // deep
         for q in range(0, join, 2):
-            here = [pl.ds(pl.multiple_of((k * join + q + r) * deep, deep), deep) for r in range(2)]
-            block = jnp.concatenate([half[:, h, :].reshape(square, pairs) for h in here], axis=1)
+            start = [(side * join + q + r) * deep for r in range(2)]
+            block = [half[:, s : s + deep, :].reshape(square, pairs) for s in start]
+            block = jnp.concatenate(block, axis=1)
             block = jnp.dot(swap[...], block, preferred_element_type=f32).astype(bf16)
             parts += [block[:, :pairs], block[:, pairs:]]
-        flat = jnp.concatenate(parts, axis=0)
-        start = pl.multiple_of(k * join * deep, deep)
-        block = factor_ref[pl.ds(start, join * deep)]
         out_ref[...] += lax.dot_general(
-            flat,
-            block.reshape(join * square, block.shape[2]),
+            jnp.concatenate(parts, axis=0),
+            factor_ref[...].reshape(join * square, factor_ref.shape[2]),
             (((0,), (0,)), ((), ())),
             preferred_element_type=f32,
         )
@@ -283,15 +291,17 @@
 def ladder_partial(row, ladder_amp, vv_factor):
     virtuals, slab, pairs = ladder_amp.shape
     chol = vv_factor.shape[0]
-    deep = 16
+    deep, sides = 16, 4
+
+    def side(shape, q):
+        return pl.BlockSpec((shape[0] // sides, deep, shape[2]), lambda i: (q, i, 0))
+
     return pl.pallas_call(
         ladder_kernel,
         grid=(slab // deep,),
-        in_specs=[
-            pl.BlockSpec(memory_space=pltpu.VMEM),
-            pl.BlockSpec((virtuals, deep, pairs), lambda i: (0, i, 0)),
-            pl.BlockSpec((chol, deep, virtuals), lambda i: (0, i, 0)),
-        ],
+        in_specs=[pl.BlockSpec(memory_space=pltpu.VMEM)]
+        + [side(ladder_amp.shape, q) for q in range(sides)]
+        + [side(vv_factor.shape, q) for q in range(sides)],
         out_specs=pl.BlockSpec((pairs, virtuals), lambda i: (0, 0)),
         out_shape=jax.ShapeDtypeStruct((pairs, virtuals), f32),
         scratch_shapes=[
@@ -305,7 +315,7 @@
             bytes_accessed=2 * virtuals * slab * (pairs + chol),
             transcendentals=0,
         ),
-    )(row, ladder_amp, vv_factor)
+    )(row, *[ladder_amp] * sides, *[vv_factor] * sides)
 
 
 def scatter_sum(x, axes):

time: 145 us -> 143 us (0.986)
  Pallas kernels: 103 us -> 99.3 us
    pallas_call x1, Pallas kernels: 85.7 us -> 81.3 us  [ladder_partial(): pl.pallas_call(ladder_kernel, grid=(slab // deep,), in_specs=[pl.BlockSpe...]
  transfers between devices with their start and end apart: 6 -> 6, of which waited for: 3 -> 3; matrix products, arithmetic and copies ran while one was open for 3% -> 3% of each run, Pallas kernels for 71% -> 70%
where the time goes in v1:
time: 143 us; the launch traced here: 142 us
  Pallas kernels  99.3 us (69%)
  starting transfers between devices  20.8 us (15%)
  waiting for transfers between devices  10.5 us (7%)
  other arithmetic  6.58 us (5%)
  local copies, waits for them, and re-layouts  4.17 us (3%)
    pallas_call x1, Pallas kernels, ladder_partial(): pl.pallas_call(ladder_kernel, grid=(slab // deep,), in_specs=[pl.BlockSpe...  81.3 us
    pallas_call x1, Pallas kernels, cycle_partial(): pl.pallas_call(functools.partial(cycle_kernel, shares, len(amps)), grid=(...  11.6 us
    all_to_all x1, waiting for transfers between devices, local(): lax.all_to_all(total.reshape(n_vir * n_ph, share, slab), ('vir', 'ph'), 0...  7.36 us
    all_to_all x1, starting transfers between devices, local(): lax.all_to_all(total.reshape(n_vir * n_ph, share, slab), ('vir', 'ph'), 0...  6.77 us
    pallas_call x1, Pallas kernels, own_row(): pl.pallas_call(row_kernel, grid=(chol // LANES, steps), in_specs=[side(q)...  6.4 us
    all_to_all x1, starting transfers between devices, local(): row = lax.all_to_all(row, 'vir', 0, 0)  6.28 us
    all_to_all x1, starting transfers between devices, local(): lax.all_to_all(cycle_partial(amps, codes, ov_slots), ('vir', 'ph', 'vec')...  4.45 us
    ppermute x3, starting transfers between devices, shifted(): return lax.ppermute(x, axes, [(i, (i + k) % n) for i in range(n)])  3.31 us
  transfers between devices with their start and end apart: 6, of which 3 were waited for; matrix products, arithmetic and copies ran while one was open for 3% of the time, Pallas kernels for 70%

profile of v1, /device:TPU:0, one launch (start us, length us, event | category | flops | bytes accessed | tf_op | source)
XLA Modules:
  0.0 142.4 jit_solution(5649778447972696299)
XLA Ops:
  0.6 0.0 copy-start
  0.6 1.1 fusion.6
  1.8 0.1 pad_maximum_fusion.refs_0_
  1.9 3.0 %collective-permute-start = (bf16[32,32,128]{2,1,0:T(8,128)(2,1)S(1)}, bf16[32,32,128]{2,1,0:T(8,128)(2,1)S(1)}, u32[]{:S(2)}, u32[]{:S(2)}) collective-permute-start(bf16[32,32,128]{2,1,0:T(8,128)(2,1)S(1)} %pad_maximum_fusion.refs_0_), channel_id=1, source_target_pairs={{0,2},{2,0},{1,3},{3,1},{4,6},{6,4},{5,7},{7,5},{8,10},{10,8},{9,1... | collective-permute-start | bytes 786440 | tf_op jit(solution)/shard_map/ppermute | solution.py:93
  5.0 0.7 multiply_add_fusion
  5.6 0.0 collective-permute-start.1
  5.7 6.4 %shard_map.104 = bf16[8,256,128]{2,1,0:T(8,128)(2,1)} custom-call(bf16[256,128,1024]{2,1,0:T(8,128)(2,1)} %refs_7_.1, bf16[256,128,1024]{2,1,0:T(8,128)(2,1)} %refs_7_.1, bf16[256,128,1024]{2,1,0:T(8,128)(2,1)} %refs_7_.1, bf16[256,128,1024]{2,1,0:T(8,128)(2,1)} %refs_7_.1), custom_call_target="tpu_custom_call" | custom-call | flops 8388608 | bytes 8388608 | tf_op jit(solution)/shard_map/pallas_call | solution.py:134
  12.1 0.7 pad_add_fusion.code_ref
  12.7 6.3 %all-to-all-start = ((bf16[8,256,128]{2,1,0:T(8,128)(2,1)}), bf16[8,256,128]{2,1,0:T(8,128)(2,1)S(1)}, u32[]{:S(2)}, u32[]{:S(2)}) async-start(bf16[8,256,128]{2,1,0:T(8,128)(2,1)} %shard_map.104), calls=%async_computation | async-start | bytes 1048576 | tf_op jit(solution)/shard_map/all_to_all | solution.py:346
  19.0 0.6 broadcast_bitcast_fusion
  19.7 11.6 %shard_map.106 = f32[32,32,256]{2,1,0:T(8,128)} custom-call(s32[1]{0:T(128)} %bitcast.2.place_ref, s32[128]{0:T(128)} %pad_add_fusion.code_ref, bf16[32,32,128]{2,1,0:T(8,128)(2,1)} %copy-done.2, bf16[32,32,128]{2,1,0:T(8,128)(2,1)} %copy-done.3, bf16[128,64,1024]{2,1,0:T(8,128)(2,1)} %bitcast.29, bf16[128,64,1024]{2,1,0:T(8,128)(2,1)} %bitcast.30, ...), custom_call_target="tpu_custom_call" | custom-call | flops 536870912 | bytes 16777216 | tf_op jit(solution)/shard_map/pallas_call | solution.py:212
  31.3 1.7 %all-to-all-done.row_ref = bf16[8,256,128]{2,1,0:T(8,128)(2,1)S(1)} async-done(((bf16[8,256,128]{2,1,0:T(8,128)(2,1)}), bf16[8,256,128]{2,1,0:T(8,128)(2,1)S(1)}, u32[]{:S(2)}, u32[]{:S(2)}) %all-to-all-start) | async-done | bytes 524320 | tf_op jit(solution)/shard_map/all_to_all | solution.py:346
  33.0 4.4 %all-to-all-start.1 = ((f32[32,32,256]{2,1,0:T(8,128)}), f32[32,32,256]{2,1,0:T(8,128)}, u32[]{:S(2)}, u32[]{:S(2)}) async-start(f32[32,32,256]{2,1,0:T(8,128)} %shard_map.106), calls=%async_computation.1 | async-start | bytes 2097152 | tf_op jit(solution)/shard_map/all_to_all | solution.py:347
  37.5 0.0 copy-start.5
  37.5 0.0 copy-start.6
  37.5 81.3 %shard_map.105 = f32[256,1024]{1,0:T(8,128)} custom-call(bf16[8,256,128]{2,1,0:T(8,128)(2,1)} %copy-done.1, bf16[1024,128,256]{2,1,0:T(8,128)(2,1)} %refs_3_.3, bf16[1024,128,256]{2,1,0:T(8,128)(2,1)} %refs_3_.3, bf16[1024,128,256]{2,1,0:T(8,128)(2,1)} %refs_3_.3, bf16[1024,128,256]{2,1,0:T(8,128)(2,1)} %refs_3_.3, bf16[256,128,1024]{2,1,0:T(8,128)(2,1)} %refs_7_.1, ...), custom_call_target="tpu_custom_call" | custom-call | flops 34359738368 | bytes 134217728 | tf_op jit(solution)/shard_map/pallas_call | solution.py:299
  118.8 1.3 reduce_sum.39
  120.1 0.2 fusion.1
  120.3 0.1 copy.24
  120.4 0.1 broadcast_in_dim.61
  120.5 0.2 broadcast_in_dim.62
  120.7 1.4 select_add_fusion
  122.1 0.2 collective-permute-start.2
  122.4 1.4 collective-permute-done.2
  123.7 0.1 fusion
  123.9 0.8 copy.19
  124.6 6.8 %all-to-all-start.2 = ((bf16[16,64,128]{2,1,0:T(8,128)(2,1)}), bf16[16,64,128]{2,1,0:T(8,128)(2,1)S(1)}, u32[]{:S(2)}, u32[]{:S(2)}) async-start(bf16[16,64,128]{2,1,0:T(8,128)(2,1)} %bitcast.9), calls=%async_computation.2 | async-start | bytes 524288 | tf_op jit(solution)/shard_map/all_to_all | solution.py:361
  131.4 1.2 slice.3
  132.6 1.4 dynamic-slice_add_fusion
  134.0 0.2 select_reduce_fusion.1
  134.2 7.4 %all-to-all-done.2 = bf16[16,64,128]{2,1,0:T(8,128)(2,1)S(1)} async-done(((bf16[16,64,128]{2,1,0:T(8,128)(2,1)}), bf16[16,64,128]{2,1,0:T(8,128)(2,1)S(1)}, u32[]{:S(2)}, u32[]{:S(2)}) %all-to-all-start.2) | async-done | bytes 262176 | tf_op jit(solution)/shard_map/all_to_all | solution.py:361
  141.6 0.7 subtract_divide_fusion
  (20 shorter events, 0.2 us)
Async XLA Ops:
  0.6 119.5 %copy-start = (bf16[256,8,128]{2,1,0:T(8,128)(2,1)S(1)}, bf16[256,8,128]{2,1,0:T(8,128)(2,1)}, u32[]{:S(2)}) copy-start(bf16[256,8,128]{2,1,0:T(8,128)(2,1)} %param.15) | copy-start | bytes 1572868
  1.9 10.2 %copy-start.2 = (bf16[32,32,128]{2,1,0:T(8,128)(2,1)}, bf16[32,32,128]{2,1,0:T(8,128)(2,1)S(1)}, u32[]{:S(2)}) copy-start(bf16[32,32,128]{2,1,0:T(8,128)(2,1)S(1)} %pad_maximum_fusion.refs_0_) | copy-start | bytes 786436
  1.9 10.8 %collective-permute-start = (bf16[32,32,128]{2,1,0:T(8,128)(2,1)S(1)}, bf16[32,32,128]{2,1,0:T(8,128)(2,1)S(1)}, u32[]{:S(2)}, u32[]{:S(2)}) collective-permute-start(bf16[32,32,128]{2,1,0:T(8,128)(2,1)S(1)} %pad_maximum_fusion.refs_0_), channel_id=1, source_target_pairs={{0,2},{2,0},{1,3},{3,1},{4,6},{6,4},{5,7},{7,5},{8,10},{10,8},{9,1... | collective-permute-start | bytes 786440 | tf_op jit(solution)/shard_map/ppermute | solution.py:93
  5.6 6.4 %collective-permute-start.1 = (s32[64]{0:T(128)S(1)}, s32[64]{0:T(128)S(1)}, u32[]{:S(2)}, u32[]{:S(2)}) collective-permute-start(s32[64]{0:T(128)S(1)} %multiply_add_fusion), channel_id=1, source_target_pairs={{0,2},{2,0},{1,3},{3,1},{4,6},{6,4},{5,7},{7,5},{8,10},{10,8},{9,1... | collective-permute-start | bytes 776 | tf_op jit(solution)/shard_map/ppermute | solution.py:93
  12.7 6.9 %copy-start.3 = (bf16[32,32,128]{2,1,0:T(8,128)(2,1)}, bf16[32,32,128]{2,1,0:T(8,128)(2,1)S(1)}, u32[]{:S(2)}) copy-start(bf16[32,32,128]{2,1,0:T(8,128)(2,1)S(1)} %collective-permute-done.refs_1_) | copy-start | bytes 786436
  12.7 20.2 %all-to-all-start = ((bf16[8,256,128]{2,1,0:T(8,128)(2,1)}), bf16[8,256,128]{2,1,0:T(8,128)(2,1)S(1)}, u32[]{:S(2)}, u32[]{:S(2)}) async-start(bf16[8,256,128]{2,1,0:T(8,128)(2,1)} %shard_map.104), calls=%async_computation | async-start | bytes 1048576 | tf_op jit(solution)/shard_map/all_to_all | solution.py:346
  33.0 4.5 %copy-start.1 = (bf16[8,256,128]{2,1,0:T(8,128)(2,1)}, bf16[8,256,128]{2,1,0:T(8,128)(2,1)S(1)}, u32[]{:S(2)}) copy-start(bf16[8,256,128]{2,1,0:T(8,128)(2,1)S(1)} %all-to-all-done.row_ref) | copy-start | bytes 1572868
  33.0 85.8 %all-to-all-start.1 = ((f32[32,32,256]{2,1,0:T(8,128)}), f32[32,32,256]{2,1,0:T(8,128)}, u32[]{:S(2)}, u32[]{:S(2)}) async-start(f32[32,32,256]{2,1,0:T(8,128)} %shard_map.106), calls=%async_computation.1 | async-start | bytes 2097152 | tf_op jit(solution)/shard_map/all_to_all | solution.py:347
  37.5 83.2 %copy-start.5 = (pred[1024]{0:T(1024)(128)(4,1)S(1)}, pred[1024]{0:T(1024)(128)(4,1)}, u32[]{:S(2)}) copy-start(pred[1024]{0:T(1024)(128)(4,1)} %broadcast_bitcast_fusion) | copy-start | bytes 3076
  37.5 96.6 %copy-start.6 = (f32[128]{0:T(128)S(1)}, f32[128]{0:T(128)}, u32[]{:S(2)}) copy-start(f32[128]{0:T(128)} %param.17) | copy-start | bytes 1540
  122.1 1.6 %collective-permute-start.2 = (bf16[2,64,1024]{2,1,0:T(8,128)(2,1)S(1)}, bf16[2,64,1024]{2,1,0:T(8,128)(2,1)S(1)}, u32[]{:S(2)}, u32[]{:S(2)}) collective-permute-start(bf16[2,64,1024]{2,1,0:T(8,128)(2,1)S(1)} %fusion.3), channel_id=1, source_target_pairs={{0,1},{1,0},{2,3},{3,2},{4,5},{5,4},{6,7},{7,6},{8,9},{9,8},{10,11... | collective-permute-start | bytes 786440 | tf_op jit(solution)/shard_map/ppermute | solution.py:93
  124.6 17.0 %all-to-all-start.2 = ((bf16[16,64,128]{2,1,0:T(8,128)(2,1)}), bf16[16,64,128]{2,1,0:T(8,128)(2,1)S(1)}, u32[]{:S(2)}, u32[]{:S(2)}) async-start(bf16[16,64,128]{2,1,0:T(8,128)(2,1)} %bitcast.9), calls=%async_computation.2 | async-start | bytes 524288 | tf_op jit(solution)/shard_map/all_to_all | solution.py:361
  141.6 0.7 copy-start.4

commit v2 on v1

--- a/solution.py
+++ b/solution.py
@@ -238,32 +238,67 @@
     return (lax.rem(r, deep) * deep + lax.div(r, deep) == s).astype(bf16)
 
 
-def ladder_kernel(row_ref, *refs):
-    (*in_refs, out_ref, swap, turned, half) = refs
-    sides = len(in_refs) // 2
-    amp_refs, factor_refs = in_refs[:sides], in_refs[sides:]
-    virtuals, deep, pairs = amp_refs[0].shape
+def ladder_kernel(sides, row_ref, amp_hbm, factor_hbm, out_ref, *scratch):
+    (amp_buf, factor_buf, amp_sem, factor_sem, swap, turned, half, *areas) = scratch
+    _, virtuals, deep, pairs = amp_buf.shape
     count, chol, _ = row_ref.shape
     square = deep * deep
-
-    @pl.when(pl.program_id(0) == 0)
-    def _():
+    step, steps = pl.program_id(0), pl.num_programs(0)
+    slot = lax.rem(step, 2)
+
+    def arriving(hbm, buf, sem, step, side):
+        size = buf.shape[1] // sides
+        rows, slot = pl.ds(side * size, size), lax.rem(step, 2)
+        block = pl.ds(pl.multiple_of(step * deep, deep), deep)
+        return pltpu.make_async_copy(
+            hbm.at[rows, block], buf.at[slot, rows], sem.at[slot, side]
+        )
+
+    def start(step):
+        for q in range(sides):
+            arriving(amp_hbm, amp_buf, amp_sem, step, q).start()
+        for q in range(sides):
+            arriving(factor_hbm, factor_buf, factor_sem, step, q).start()
+
+    @pl.when(step == 0)
+    def _():
+        start(step)
         out_ref[...] = jnp.zeros_like(out_ref)
         swap[...] = swap_matrix(deep)
 
-    group = 8
-    for side, amp_ref in enumerate(amp_refs):
-
-        @pl.loop(0, virtuals // (deep * group))
-        def _(k):
-            for q in range(0, group, 2):
-                start = [pl.multiple_of((k * group + q + r) * deep, deep) for r in range(2)]
-                block = [amp_ref[pl.ds(s, deep)].reshape(square, pairs) for s in start]
-                block = jnp.concatenate(block, axis=1)
-                block = jnp.dot(swap[...], block, preferred_element_type=f32).astype(bf16)
-                for r, s in enumerate(start):
-                    part = block[:, r * pairs : (r + 1) * pairs].reshape(deep, deep, pairs)
-                    turned[:, pl.ds(side * virtuals + s, deep), :] = part
+    @pl.when(step + 1 < steps)
+    def _():
+        start(step + 1)
+
+    def by_matmul(first):
+        rows = [slice(first + r * deep, first + (r + 1) * deep) for r in range(2)]
+        block = [amp_buf[slot, r].reshape(square, pairs) for r in rows]
+        block = jnp.dot(
+            swap[...], jnp.concatenate(block, axis=1), preferred_element_type=f32
+        ).astype(bf16)
+        for i, r in enumerate(rows):
+            turned[:, r, :] = block[:, i * pairs : (i + 1) * pairs].reshape(deep, deep, pairs)
+
+    def by_stride(first, tall, areas):
+        for h, area in enumerate(areas):
+            lane = slice(h * LANES, (h + 1) * LANES)
+            block = amp_buf[slot, first : first + tall, :, lane].astype(f32)
+            for o in range(deep // 8):
+                area[o] = block[:, o * 8 : (o + 1) * 8].reshape(tall * 8, LANES)
+            for d in range(deep):
+                turned[d, first : first + tall, lane] = area[
+                    d // 8, pl.ds(d % 8, tall, stride=8), :
+                ].astype(bf16)
+
+    tall = 2 * deep
+    for q in range(sides):
+        arriving(amp_hbm, amp_buf, amp_sem, step, q).wait()
+        size = virtuals // sides
+        for k in range(0, size, 2 * tall):
+            first = q * size + k
+            by_matmul(first)
+            pick = k // (2 * tall) % 2 * 2
+            by_stride(first + tall, tall, areas[pick : pick + 2])
 
     row = jnp.concatenate([row_ref[k] for k in range(count)], axis=1)
     for d in range(0, deep, 2):
@@ -271,19 +306,21 @@
         block = jnp.dot(row, block, preferred_element_type=f32).astype(bf16)
         half[d], half[d + 1] = block[:, :pairs], block[:, pairs:]
 
-    for side, factor_ref in enumerate(factor_refs):
-        parts = []
-        join = factor_ref.shape[0] // deep
-        for q in range(0, join, 2):
-            start = [(side * join + q + r) * deep for r in range(2)]
-            block = [half[:, s : s + deep, :].reshape(square, pairs) for s in start]
-            block = jnp.concatenate(block, axis=1)
-            block = jnp.dot(swap[...], block, preferred_element_type=f32).astype(bf16)
-            parts += [block[:, :pairs], block[:, pairs:]]
-        out_ref[...] += lax.dot_general(
-            jnp.concatenate(parts, axis=0),
-            factor_ref[...].reshape(join * square, factor_ref.shape[2]),
-            (((0,), (0,)), ((), ())),
+    for q in range(sides):
+        arriving(factor_hbm, factor_buf, factor_sem, step, q).wait()
+        size = chol // sides
+        block = [
+            half[:, k : k + deep, :].reshape(square, pairs).T
+            for k in range(q * size, (q + 1) * size, deep)
+        ]
+        block = jnp.dot(
+            jnp.concatenate(block, axis=0), swap[...], preferred_element_type=f32
+        ).astype(bf16)
+        block = [block[k * pairs : (k + 1) * pairs] for k in range(size // deep)]
+        factor = factor_buf[slot, q * size : (q + 1) * size]
+        out_ref[...] += jnp.dot(
+            jnp.concatenate(block, axis=1),
+            factor.reshape(size * deep, factor.shape[2]),
             preferred_element_type=f32,
         )
 
@@ -292,30 +329,30 @@
     virtuals, slab, pairs = ladder_amp.shape
     chol = vv_factor.shape[0]
     deep, sides = 16, 4
-
-    def side(shape, q):
-        return pl.BlockSpec((shape[0] // sides, deep, shape[2]), lambda i: (q, i, 0))
-
+    whole = pl.BlockSpec(memory_space=pl.ANY)
     return pl.pallas_call(
-        ladder_kernel,
+        functools.partial(ladder_kernel, sides),
         grid=(slab // deep,),
-        in_specs=[pl.BlockSpec(memory_space=pltpu.VMEM)]
-        + [side(ladder_amp.shape, q) for q in range(sides)]
-        + [side(vv_factor.shape, q) for q in range(sides)],
+        in_specs=[pl.BlockSpec(memory_space=pltpu.VMEM), whole, whole],
         out_specs=pl.BlockSpec((pairs, virtuals), lambda i: (0, 0)),
         out_shape=jax.ShapeDtypeStruct((pairs, virtuals), f32),
         scratch_shapes=[
+            pltpu.VMEM((2, virtuals, deep, pairs), bf16),
+            pltpu.VMEM((2, chol, deep, virtuals), bf16),
+            pltpu.SemaphoreType.DMA((2, sides)),
+            pltpu.SemaphoreType.DMA((2, sides)),
             pltpu.VMEM((deep * deep, deep * deep), bf16),
             pltpu.VMEM((deep, virtuals, pairs), bf16),
             pltpu.VMEM((deep, chol, pairs), bf16),
-        ],
+        ]
+        + [pltpu.VMEM((deep // 8, 2 * deep * 8, LANES), f32)] * 4,
         compiler_params=pltpu.CompilerParams(vmem_limit_bytes=60 << 20),
         cost_estimate=pl.CostEstimate(
             flops=4 * chol * virtuals * slab * pairs,
             bytes_accessed=2 * virtuals * slab * (pairs + chol),
             transcendentals=0,
         ),
-    )(row, *[ladder_amp] * sides, *[vv_factor] * sides)
+    )(row, ladder_amp, vv_factor)
 
 
 def scatter_sum(x, axes):

time: 143 us -> 140 us (0.979)
  transfers between devices with their start and end apart: 6 -> 6, of which waited for: 3 -> 3; matrix products, arithmetic and copies ran while one was open for 3% -> 3% of each run, Pallas kernels for 70% -> 71%
where the time goes in v2:
time: 140 us
  Pallas kernels  98.4 us (70%)
  starting transfers between devices  20.3 us (14%)
  waiting for transfers between devices  10.9 us (8%)
  other arithmetic  5.29 us (4%)
  local copies, waits for them, and re-layouts  3.61 us (3%)
    pallas_call x1, Pallas kernels, ladder_partial(): pl.pallas_call(functools.partial(ladder_kernel, sides), grid=(slab // dee...  80.4 us
    pallas_call x1, Pallas kernels, cycle_partial(): pl.pallas_call(functools.partial(cycle_kernel, shares, len(amps)), grid=(...  11.6 us
    all_to_all x1, waiting for transfers between devices, local(): lax.all_to_all(total.reshape(n_vir * n_ph, share, slab), ('vir', 'ph'), 0...  7.36 us
    all_to_all x1, starting transfers between devices, local(): lax.all_to_all(total.reshape(n_vir * n_ph, share, slab), ('vir', 'ph'), 0...  6.85 us
    pallas_call x1, Pallas kernels, own_row(): pl.pallas_call(row_kernel, grid=(chol // LANES, steps), in_specs=[side(q)...  6.4 us
    all_to_all x1, starting transfers between devices, local(): row = lax.all_to_all(row, 'vir', 0, 0)  6.28 us
    all_to_all x1, starting transfers between devices, local(): lax.all_to_all(cycle_partial(amps, codes, ov_slots), ('vir', 'ph', 'vec')...  3.76 us
    ppermute x3, starting transfers between devices, shifted(): return lax.ppermute(x, axes, [(i, (i + k) % n) for i in range(n)])  3.39 us
  transfers between devices with their start and end apart: 6, of which 3 were waited for; matrix products, arithmetic and copies ran while one was open for 3% of the time, Pallas kernels for 71%

profile of v2, /device:TPU:0, one launch (start us, length us, event | category | flops | bytes accessed | tf_op | source)
XLA Modules:
  0.0 139.5 jit_solution(15898106042205949216)
XLA Ops:
  0.6 0.0 copy-start
  0.6 1.1 fusion.6
  1.8 0.1 pad_maximum_fusion.refs_0_
  1.9 3.0 %collective-permute-start = (bf16[32,32,128]{2,1,0:T(8,128)(2,1)S(1)}, bf16[32,32,128]{2,1,0:T(8,128)(2,1)S(1)}, u32[]{:S(2)}, u32[]{:S(2)}) collective-permute-start(bf16[32,32,128]{2,1,0:T(8,128)(2,1)S(1)} %pad_maximum_fusion.refs_0_), channel_id=1, source_target_pairs={{0,2},{2,0},{1,3},{3,1},{4,6},{6,4},{5,7},{7,5},{8,10},{10,8},{9,1... | collective-permute-start | bytes 786440 | tf_op jit(solution)/shard_map/ppermute | solution.py:93
  5.0 0.7 multiply_add_fusion
  5.6 0.0 collective-permute-start.1
  5.7 6.4 %shard_map.104 = bf16[8,256,128]{2,1,0:T(8,128)(2,1)} custom-call(bf16[256,128,1024]{2,1,0:T(8,128)(2,1)} %factor_hbm.1, bf16[256,128,1024]{2,1,0:T(8,128)(2,1)} %factor_hbm.1, bf16[256,128,1024]{2,1,0:T(8,128)(2,1)} %factor_hbm.1, bf16[256,128,1024]{2,1,0:T(8,128)(2,1)} %factor_hbm.1), custom_call_target="tpu_custom_call" | custom-call | flops 8388608 | bytes 8388608 | tf_op jit(solution)/shard_map/pallas_call | solution.py:134
  12.1 0.6 pad_add_fusion.code_ref
  12.7 6.3 %all-to-all-start = ((bf16[8,256,128]{2,1,0:T(8,128)(2,1)}), bf16[8,256,128]{2,1,0:T(8,128)(2,1)S(1)}, u32[]{:S(2)}, u32[]{:S(2)}) async-start(bf16[8,256,128]{2,1,0:T(8,128)(2,1)} %shard_map.104), calls=%async_computation | async-start | bytes 1048576 | tf_op jit(solution)/shard_map/all_to_all | solution.py:383
  19.0 0.1 broadcast_bitcast_fusion
  19.0 11.6 %shard_map.106 = f32[32,32,256]{2,1,0:T(8,128)} custom-call(s32[1]{0:T(128)} %bitcast.2.place_ref, s32[128]{0:T(128)} %pad_add_fusion.code_ref, bf16[32,32,128]{2,1,0:T(8,128)(2,1)} %copy-done.2, bf16[32,32,128]{2,1,0:T(8,128)(2,1)} %copy-done.3, bf16[128,64,1024]{2,1,0:T(8,128)(2,1)} %bitcast.29, bf16[128,64,1024]{2,1,0:T(8,128)(2,1)} %bitcast.30, ...), custom_call_target="tpu_custom_call" | custom-call | flops 536870912 | bytes 16777216 | tf_op jit(solution)/shard_map/pallas_call | solution.py:212
  30.6 2.3 %all-to-all-done.row_ref = bf16[8,256,128]{2,1,0:T(8,128)(2,1)S(1)} async-done(((bf16[8,256,128]{2,1,0:T(8,128)(2,1)}), bf16[8,256,128]{2,1,0:T(8,128)(2,1)S(1)}, u32[]{:S(2)}, u32[]{:S(2)}) %all-to-all-start) | async-done | bytes 524320 | tf_op jit(solution)/shard_map/all_to_all | solution.py:383
  32.9 3.8 %all-to-all-start.1 = ((f32[32,32,256]{2,1,0:T(8,128)}), f32[32,32,256]{2,1,0:T(8,128)S(1)}, u32[]{:S(2)}, u32[]{:S(2)}) async-start(f32[32,32,256]{2,1,0:T(8,128)} %shard_map.106), calls=%async_computation.1 | async-start | bytes 2097152 | tf_op jit(solution)/shard_map/all_to_all | solution.py:384
  36.7 0.0 copy-start.5
  36.7 80.4 %shard_map.105 = f32[256,1024]{1,0:T(8,128)} custom-call(bf16[8,256,128]{2,1,0:T(8,128)(2,1)} %copy-done.1, bf16[1024,128,256]{2,1,0:T(8,128)(2,1)} %amp_hbm.1, bf16[256,128,1024]{2,1,0:T(8,128)(2,1)} %factor_hbm.1), custom_call_target="tpu_custom_call" | custom-call | flops 34359738368 | bytes 134217728 | tf_op jit(solution)/shard_map/pallas_call | solution.py:333
  117.1 0.1 reduce_sum.39
  117.2 0.2 fusion.1
  117.4 0.1 copy.24
  117.5 0.1 broadcast_in_dim.61
  117.6 0.2 broadcast_in_dim.62
  117.8 1.4 select_add_fusion
  119.2 0.3 collective-permute-start.2
  119.5 1.3 collective-permute-done.2
  120.8 0.1 fusion
  120.9 0.8 copy.19
  121.7 6.8 %all-to-all-start.2 = ((bf16[16,64,128]{2,1,0:T(8,128)(2,1)}), bf16[16,64,128]{2,1,0:T(8,128)(2,1)S(1)}, u32[]{:S(2)}, u32[]{:S(2)}) async-start(bf16[16,64,128]{2,1,0:T(8,128)(2,1)} %bitcast.9), calls=%async_computation.2 | async-start | bytes 524288 | tf_op jit(solution)/shard_map/all_to_all | solution.py:398
  128.6 1.2 slice.3
  129.8 1.4 %dynamic-slice_add_fusion = f32[128]{0:T(128)S(1)} fusion(f32[1024]{0:T(1024)} %param.16, s32[]{:T(128)S(6)} %select_n.53, f32[]{:T(128)} %bitcast.11), kind=kLoop, calls=%fused_computation.25 | loop fusion | flops 128 | bytes 1032 | tf_op jit(solution)/shard_map/add | solution.py:412
  131.2 0.2 select_reduce_fusion.1
  131.4 7.4 %all-to-all-done.2 = bf16[16,64,128]{2,1,0:T(8,128)(2,1)S(1)} async-done(((bf16[16,64,128]{2,1,0:T(8,128)(2,1)}), bf16[16,64,128]{2,1,0:T(8,128)(2,1)S(1)}, u32[]{:S(2)}, u32[]{:S(2)}) %all-to-all-start.2) | async-done | bytes 262176 | tf_op jit(solution)/shard_map/all_to_all | solution.py:398
  138.8 0.0 copy-start.4
  138.8 0.7 subtract_divide_fusion
  (18 shorter events, 0.2 us)
Async XLA Ops:
  0.6 116.6 %copy-start = (bf16[256,8,128]{2,1,0:T(8,128)(2,1)S(1)}, bf16[256,8,128]{2,1,0:T(8,128)(2,1)}, u32[]{:S(2)}) copy-start(bf16[256,8,128]{2,1,0:T(8,128)(2,1)} %param.15) | copy-start | bytes 1572868
  1.9 10.2 %copy-start.2 = (bf16[32,32,128]{2,1,0:T(8,128)(2,1)}, bf16[32,32,128]{2,1,0:T(8,128)(2,1)S(1)}, u32[]{:S(2)}) copy-start(bf16[32,32,128]{2,1,0:T(8,128)(2,1)S(1)} %pad_maximum_fusion.refs_0_) | copy-start | bytes 786436
  1.9 10.7 %collective-permute-start = (bf16[32,32,128]{2,1,0:T(8,128)(2,1)S(1)}, bf16[32,32,128]{2,1,0:T(8,128)(2,1)S(1)}, u32[]{:S(2)}, u32[]{:S(2)}) collective-permute-start(bf16[32,32,128]{2,1,0:T(8,128)(2,1)S(1)} %pad_maximum_fusion.refs_0_), channel_id=1, source_target_pairs={{0,2},{2,0},{1,3},{3,1},{4,6},{6,4},{5,7},{7,5},{8,10},{10,8},{9,1... | collective-permute-start | bytes 786440 | tf_op jit(solution)/shard_map/ppermute | solution.py:93
  5.6 6.4 %collective-permute-start.1 = (s32[64]{0:T(128)S(1)}, s32[64]{0:T(128)S(1)}, u32[]{:S(2)}, u32[]{:S(2)}) collective-permute-start(s32[64]{0:T(128)S(1)} %multiply_add_fusion), channel_id=1, source_target_pairs={{0,2},{2,0},{1,3},{3,1},{4,6},{6,4},{5,7},{7,5},{8,10},{10,8},{9,1... | collective-permute-start | bytes 776 | tf_op jit(solution)/shard_map/ppermute | solution.py:93
  12.7 6.4 %copy-start.3 = (bf16[32,32,128]{2,1,0:T(8,128)(2,1)}, bf16[32,32,128]{2,1,0:T(8,128)(2,1)S(1)}, u32[]{:S(2)}) copy-start(bf16[32,32,128]{2,1,0:T(8,128)(2,1)S(1)} %collective-permute-done.refs_1_) | copy-start | bytes 786436
  12.7 20.2 %all-to-all-start = ((bf16[8,256,128]{2,1,0:T(8,128)(2,1)}), bf16[8,256,128]{2,1,0:T(8,128)(2,1)S(1)}, u32[]{:S(2)}, u32[]{:S(2)}) async-start(bf16[8,256,128]{2,1,0:T(8,128)(2,1)} %shard_map.104), calls=%async_computation | async-start | bytes 1048576 | tf_op jit(solution)/shard_map/all_to_all | solution.py:383
  32.9 3.8 %copy-start.1 = (bf16[8,256,128]{2,1,0:T(8,128)(2,1)}, bf16[8,256,128]{2,1,0:T(8,128)(2,1)S(1)}, u32[]{:S(2)}) copy-start(bf16[8,256,128]{2,1,0:T(8,128)(2,1)S(1)} %all-to-all-done.row_ref) | copy-start | bytes 1572868
  32.9 84.2 %all-to-all-start.1 = ((f32[32,32,256]{2,1,0:T(8,128)}), f32[32,32,256]{2,1,0:T(8,128)S(1)}, u32[]{:S(2)}, u32[]{:S(2)}) async-start(f32[32,32,256]{2,1,0:T(8,128)} %shard_map.106), calls=%async_computation.1 | async-start | bytes 2097152 | tf_op jit(solution)/shard_map/all_to_all | solution.py:384
  36.7 94.5 %copy-start.5 = (f32[128]{0:T(128)S(1)}, f32[128]{0:T(128)}, u32[]{:S(2)}) copy-start(f32[128]{0:T(128)} %param.17) | copy-start | bytes 1540
  119.2 1.6 %collective-permute-start.2 = (bf16[2,64,1024]{2,1,0:T(8,128)(2,1)S(1)}, bf16[2,64,1024]{2,1,0:T(8,128)(2,1)S(1)}, u32[]{:S(2)}, u32[]{:S(2)}) collective-permute-start(bf16[2,64,1024]{2,1,0:T(8,128)(2,1)S(1)} %fusion.3), channel_id=1, source_target_pairs={{0,1},{1,0},{2,3},{3,2},{4,5},{5,4},{6,7},{7,6},{8,9},{9,8},{10,11... | collective-permute-start | bytes 786440 | tf_op jit(solution)/shard_map/ppermute | solution.py:93
  121.7 17.0 %all-to-all-start.2 = ((bf16[16,64,128]{2,1,0:T(8,128)(2,1)}), bf16[16,64,128]{2,1,0:T(8,128)(2,1)S(1)}, u32[]{:S(2)}, u32[]{:S(2)}) async-start(bf16[16,64,128]{2,1,0:T(8,128)(2,1)} %bitcast.9), calls=%async_computation.2 | async-start | bytes 524288 | tf_op jit(solution)/shard_map/all_to_all | solution.py:398
  138.8 0.7 copy-start.4

commit v3 on v2

--- a/solution.py
+++ b/solution.py
@@ -150,15 +150,12 @@
     amp_refs, ov_refs = amp_refs[:groups], amp_refs[groups:]
     step = pl.program_id(0)
     blocks, slots = code_ref.shape[0], block_of.shape[0]
-    own, width = 2 * amp_refs[0].shape[0], amps.shape[2]
+    own = amp_refs[0].shape[0]
 
     @pl.when(step == 0)
     def _():
         for k, ref in enumerate(amp_refs):
-            for h in range(2):
-                amps[pl.ds(k * own + h * (own // 2), own // 2)] = ref[
-                    :, :, h * width : (h + 1) * width
-                ]
+            amps[pl.ds(k * own, own)] = ref[...]
         amps[blocks] = jnp.zeros(amps.shape[1:], bf16)
         acc[...] = jnp.zeros_like(acc)
         first = place_ref[0] * slots
@@ -175,7 +172,7 @@
             def _():
                 block_of[slot] = n
 
-    here, _, chol = ov_refs[0].shape
+    here, width, chol = ov_refs[0].shape
     for side, ref in enumerate(ov_refs):
         start = (step * len(ov_refs) + side) * here
         left = jnp.concatenate([amps[block_of[start + s]] for s in range(here)], axis=1)
@@ -192,8 +189,7 @@
 
 def cycle_operands(cycle_amp, owner_of, slot_of, slots):
     codes = jnp.concatenate(round_robin(owner_of * slots + slot_of, "ph"))
-    near, far = jnp.split(cycle_amp, 2, 0)
-    return round_robin(jnp.concatenate([near, far], 2), "ph"), codes
+    return round_robin(cycle_amp, "ph"), codes
 
 
 def cycle_partial(amps, codes, ov_slots):
@@ -239,7 +235,7 @@
 
 
 def ladder_kernel(sides, row_ref, amp_hbm, factor_hbm, out_ref, *scratch):
-    (amp_buf, factor_buf, amp_sem, factor_sem, swap, turned, half, *areas) = scratch
+    (amp_buf, factor_buf, amp_sem, factor_sem, swap, turned, half) = scratch
     _, virtuals, deep, pairs = amp_buf.shape
     count, chol, _ = row_ref.shape
     square = deep * deep
@@ -279,26 +275,11 @@
         for i, r in enumerate(rows):
             turned[:, r, :] = block[:, i * pairs : (i + 1) * pairs].reshape(deep, deep, pairs)
 
-    def by_stride(first, tall, areas):
-        for h, area in enumerate(areas):
-            lane = slice(h * LANES, (h + 1) * LANES)
-            block = amp_buf[slot, first : first + tall, :, lane].astype(f32)
-            for o in range(deep // 8):
-                area[o] = block[:, o * 8 : (o + 1) * 8].reshape(tall * 8, LANES)
-            for d in range(deep):
-                turned[d, first : first + tall, lane] = area[
-                    d // 8, pl.ds(d % 8, tall, stride=8), :
-                ].astype(bf16)
-
-    tall = 2 * deep
     for q in range(sides):
         arriving(amp_hbm, amp_buf, amp_sem, step, q).wait()
         size = virtuals // sides
-        for k in range(0, size, 2 * tall):
-            first = q * size + k
-            by_matmul(first)
-            pick = k // (2 * tall) % 2 * 2
-            by_stride(first + tall, tall, areas[pick : pick + 2])
+        for k in range(q * size, (q + 1) * size, 2 * deep):
+            by_matmul(k)
 
     row = jnp.concatenate([row_ref[k] for k in range(count)], axis=1)
     for d in range(0, deep, 2):
@@ -344,8 +325,7 @@
             pltpu.VMEM((deep * deep, deep * deep), bf16),
             pltpu.VMEM((deep, virtuals, pairs), bf16),
             pltpu.VMEM((deep, chol, pairs), bf16),
-        ]
-        + [pltpu.VMEM((deep // 8, 2 * deep * 8, LANES), f32)] * 4,
+        ],
         compiler_params=pltpu.CompilerParams(vmem_limit_bytes=60 << 20),
         cost_estimate=pl.CostEstimate(
             flops=4 * chol * virtuals * slab * pairs,
@@ -355,14 +335,27 @@
     )(row, ladder_amp, vv_factor)
 
 
-def scatter_sum(x, axes):
-    n = lax.axis_size(axes)
+def scatter_sum(x, axes, near=None):
+    total_places = lax.axis_size(axes)
     me = lax.axis_index(axes)
-    total = lax.dynamic_index_in_dim(x, me, 0, keepdims=False)
+    n = x.shape[0]
+
+    def moved(place, k):
+        if near is None:
+            return (place + k) % n
+        if near > 0:
+            return place // near * near + (place % near + k) % near
+        return (place + k * -near) % total_places
+
+    def rank(place):
+        return place if near is None else place % near if near > 0 else place // -near
+
+    total = lax.dynamic_index_in_dim(x, rank(me), 0, keepdims=False)
     sent = x.astype(bf16)
     for k in range(1, n):
-        piece = lax.dynamic_index_in_dim(sent, (me + k) % n, 0, keepdims=False)
-        total = total + shifted(piece, axes, k).astype(f32)
+        piece = lax.dynamic_index_in_dim(sent, rank(moved(me, k)), 0, keepdims=False)
+        pairs = [(i, moved(i, k)) for i in range(total_places)]
+        total = total + lax.ppermute(piece, axes, pairs).astype(f32)
     return total
 
 
@@ -374,7 +367,7 @@
     slots, _, width = ov_slots.shape
     n_vir, n_ph, n_vec = (lax.axis_size(a) for a in ("vir", "ph", "vec"))
     fits = slab == LANES and pairs == 2 * LANES and chol % LANES == 0 and slots % 32 == 0
-    if not fits or 256 % width or cycle_amp.shape[0] % 2:
+    if not fits or 256 % width or n_vir * n_ph % 4:
         return plain(
             vv_factor, ladder_amp, cycle_amp, ov_slots, owner_of, slot_of, ov_pairs, eps_vir, eps_occ
         )
@@ -393,10 +386,10 @@
     own = jnp.arange(n_vir, dtype=jnp.int32)[None, :, None] == vir
     total = ladder.reshape(pairs, n_vir, slab) + jnp.where(own, cycle_term[:, None, :], 0.0)
     total = total.reshape(n_ph, n_vec, share, virtuals)
-    total = scatter_sum(jnp.swapaxes(total, 0, 1), "vec").astype(bf16)
+    total = scatter_sum(jnp.swapaxes(total, 0, 1), "vec")
     total = total.reshape(n_ph, share, n_vir, slab).transpose(2, 0, 1, 3)
-    total = lax.all_to_all(total.reshape(n_vir * n_ph, share, slab), ("vir", "ph"), 0, 0)
-    total = jnp.sum(total.astype(f32), 0)
+    total = total.reshape(n_vir * n_ph // 4, 4, share, slab).transpose(1, 0, 2, 3)
+    total = scatter_sum(scatter_sum(total, ("vir", "ph"), 4), ("vir", "ph"), -4)
 
     residual = total.T.astype(bf16)
     place = lax.axis_index(("ph", "vec"))

time: 140 us -> 136 us (0.971)
  Pallas kernels: 98.4 us -> 92.8 us
  starting transfers between devices: 20.3 us -> 23.8 us
  local copies, waits for them, and re-layouts: 3.61 us -> 1.93 us
    ppermute x0 -> x7, starting transfers between devices: none -> 10.4 us  [scatter_sum(): total = total + lax.ppermute(piece, axes, pairs).astype(f32)]
    all_to_all x1 -> x0, waiting for transfers between devices: 7.36 us -> none  [local(): lax.all_to_all(total.reshape(n_vir * n_ph, share, slab), ('vir', 'ph'), 0...]
    all_to_all x1 -> x0, starting transfers between devices: 6.85 us -> none  [local(): lax.all_to_all(total.reshape(n_vir * n_ph, share, slab), ('vir', 'ph'), 0...]
    pallas_call x1, Pallas kernels: 80.4 us -> 74.7 us  [ladder_partial(): pl.pallas_call(functools.partial(ladder_kernel, sides), grid=(slab // dee...]
    ppermute x3 -> x2, waiting for transfers between devices: 1.28 us -> 5.04 us  [shifted(): return lax.ppermute(x, axes, [(i, (i + k) % n) for i in range(n)])]
    ppermute x0 -> x7, waiting for transfers between devices: none -> 3.63 us  [scatter_sum(): total = total + lax.ppermute(piece, axes, pairs).astype(f32)]
    ppermute x3 -> x2, starting transfers between devices: 3.39 us -> 3.1 us  [shifted(): return lax.ppermute(x, axes, [(i, (i + k) % n) for i in range(n)])]
  transfers between devices with their start and end apart: 6 -> 11, of which waited for: 3 -> 7; matrix products, arithmetic and copies ran while one was open for 3% -> 3% of each run, Pallas kernels for 71% -> 69%
where the time goes in v3:
time: 136 us; the launch traced here: 135 us
  Pallas kernels  92.8 us (68%)
  starting transfers between devices  23.8 us (18%)
  waiting for transfers between devices  10.5 us (8%)
  other arithmetic  5.17 us (4%)
  local copies, waits for them, and re-layouts  1.93 us (1%)
    pallas_call x1, Pallas kernels, ladder_partial(): pl.pallas_call(functools.partial(ladder_kernel, sides), grid=(slab // dee...  74.7 us
    pallas_call x1, Pallas kernels, cycle_partial(): pl.pallas_call(functools.partial(cycle_kernel, shares, len(amps)), grid=(...  11.6 us
    ppermute x7, starting transfers between devices, scatter_sum(): total = total + lax.ppermute(piece, axes, pairs).astype(f32)  10.4 us
    pallas_call x1, Pallas kernels, own_row(): pl.pallas_call(row_kernel, grid=(chol // LANES, steps), in_specs=[side(q)...  6.42 us
    all_to_all x1, starting transfers between devices, local(): row = lax.all_to_all(row, 'vir', 0, 0)  6.02 us
    ppermute x2, waiting for transfers between devices, shifted(): return lax.ppermute(x, axes, [(i, (i + k) % n) for i in range(n)])  5.04 us
    all_to_all x1, starting transfers between devices, local(): lax.all_to_all(cycle_partial(amps, codes, ov_slots), ('vir', 'ph', 'vec')...  4.21 us
    ppermute x7, waiting for transfers between devices, scatter_sum(): total = total + lax.ppermute(piece, axes, pairs).astype(f32)  3.63 us
  transfers between devices with their start and end apart: 11, of which 7 were waited for; matrix products, arithmetic and copies ran while one was open for 3% of the time, Pallas kernels for 69%

profile of v3, /device:TPU:0, one launch (start us, length us, event | category | flops | bytes accessed | tf_op | source)
XLA Modules:
  0.0 135.1 jit_solution(13909361190048631311)
XLA Ops:
  0.6 3.0 %collective-permute-start = (bf16[64,32,64]{2,1,0:T(8,128)(2,1)}, bf16[64,32,64]{2,1,0:T(8,128)(2,1)S(1)}, u32[]{:S(2)}, u32[]{:S(2)}) collective-permute-start(bf16[64,32,64]{2,1,0:T(8,128)(2,1)} %refs_0_.2), channel_id=1, source_target_pairs={{0,2},{2,0},{1,3},{3,1},{4,6},{6,4},{5,7},{7,5},{8,10},{10,8},{9,1... | collective-permute-start | bytes 786440 | tf_op jit(solution)/shard_map/ppermute | solution.py:93
  3.7 0.7 multiply_add_fusion
  4.4 6.4 %shard_map.104 = bf16[8,256,128]{2,1,0:T(8,128)(2,1)} custom-call(bf16[256,128,1024]{2,1,0:T(8,128)(2,1)} %factor_hbm.1, bf16[256,128,1024]{2,1,0:T(8,128)(2,1)} %factor_hbm.1, bf16[256,128,1024]{2,1,0:T(8,128)(2,1)} %factor_hbm.1, bf16[256,128,1024]{2,1,0:T(8,128)(2,1)} %factor_hbm.1), custom_call_target="tpu_custom_call" | custom-call | flops 8388608 | bytes 8388608 | tf_op jit(solution)/shard_map/pallas_call | solution.py:134
  10.8 5.0 %collective-permute-done.1 = s32[64]{0:T(128)S(1)} collective-permute-done((s32[64]{0:T(128)S(1)}, s32[64]{0:T(128)S(1)}, u32[]{:S(2)}, u32[]{:S(2)}) %collective-permute-start.1) | collective-permute-done | bytes 288 | tf_op jit(solution)/shard_map/ppermute | solution.py:93
  15.9 0.6 pad_add_fusion.code_ref
  16.5 6.0 %all-to-all-start = ((bf16[8,256,128]{2,1,0:T(8,128)(2,1)}), bf16[8,256,128]{2,1,0:T(8,128)(2,1)S(1)}, u32[]{:S(2)}, u32[]{:S(2)}) async-start(bf16[8,256,128]{2,1,0:T(8,128)(2,1)} %shard_map.104), calls=%async_computation | async-start | bytes 1048576 | tf_op jit(solution)/shard_map/all_to_all | solution.py:376
  22.6 11.6 %shard_map.106 = f32[32,32,256]{2,1,0:T(8,128)} custom-call(s32[1]{0:T(128)} %bitcast.2.place_ref, s32[128]{0:T(128)} %pad_add_fusion.code_ref, bf16[64,32,64]{2,1,0:T(8,128)(2,1)} %refs_0_.2, bf16[64,32,64]{2,1,0:T(8,128)(2,1)} %copy-done.2, bf16[128,64,1024]{2,1,0:T(8,128)(2,1)} %bitcast.60, bf16[128,64,1024]{2,1,0:T(8,128)(2,1)} %bitcast.61, ...), custom_call_target="tpu_custom_call" | custom-call | flops 536870912 | bytes 16777216 | tf_op jit(solution)/shard_map/pallas_call | solution.py:208
  34.2 1.8 %all-to-all-done.row_ref = bf16[8,256,128]{2,1,0:T(8,128)(2,1)S(1)} async-done(((bf16[8,256,128]{2,1,0:T(8,128)(2,1)}), bf16[8,256,128]{2,1,0:T(8,128)(2,1)S(1)}, u32[]{:S(2)}, u32[]{:S(2)}) %all-to-all-start) | async-done | bytes 524320 | tf_op jit(solution)/shard_map/all_to_all | solution.py:376
  36.0 4.2 %all-to-all-start.1 = ((f32[32,32,256]{2,1,0:T(8,128)}), f32[32,32,256]{2,1,0:T(8,128)S(1)}, u32[]{:S(2)}, u32[]{:S(2)}) async-start(f32[32,32,256]{2,1,0:T(8,128)} %shard_map.106), calls=%async_computation.1 | async-start | bytes 2097152 | tf_op jit(solution)/shard_map/all_to_all | solution.py:377
  40.3 74.7 %shard_map.105 = f32[256,1024]{1,0:T(8,128)} custom-call(bf16[8,256,128]{2,1,0:T(8,128)(2,1)} %copy-done.1, bf16[1024,128,256]{2,1,0:T(8,128)(2,1)} %amp_hbm.1, bf16[256,128,1024]{2,1,0:T(8,128)(2,1)} %factor_hbm.1), custom_call_target="tpu_custom_call" | custom-call | flops 34359738368 | bytes 134217728 | tf_op jit(solution)/shard_map/pallas_call | solution.py:314
  115.1 0.2 fusion
  115.3 0.1 copy.24
  115.5 0.2 broadcast_in_dim.62
  115.6 1.4 %select_add_fusion = f32[2,2,64,1024]{3,2,1,0:T(8,128)S(1)} fusion(f32[2,2,64,1024]{3,2,1,0:T(8,128)} %bitcast.64, f32[2,2,64,1024]{3,2,1,0:T(8,128)S(1)} %broadcast_in_dim.62, pred[1024]{0:T(1024)(128)(4,1)S(1)} %broadcast_bitcast_fusion), kind=kLoop, calls=%fused_computation | loop fusion | flops 524288 | bytes 3146752 | tf_op jit(solution)/shard_map/add | solution.py:387
  117.1 0.3 collective-permute-start.2
  117.4 1.2 slice.3
  118.6 0.1 collective-permute-done.2
  118.8 0.1 copy.20
  118.9 0.1 copy.19
  119.1 1.8 %collective-permute-start.3 = (bf16[4,64,128]{2,1,0:T(8,128)(2,1)S(1)}, bf16[4,64,128]{2,1,0:T(8,128)(2,1)S(1)}, u32[]{:S(2)}, u32[]{:S(2)}) collective-permute-start(bf16[4,64,128]{2,1,0:T(8,128)(2,1)S(1)} %get-tuple-element.16), channel_id=1, source_target_pairs={{0,2},{2,4},{4,6},{6,0},{8,10},{10,12},{12,14},{14,8},{16,18},{18,... | collective-permute-start | bytes 196616 | tf_op jit(solution)/shard_map/ppermute | solution.py:358
  120.9 1.5 %collective-permute-start.4 = (bf16[4,64,128]{2,1,0:T(8,128)(2,1)S(1)}, bf16[4,64,128]{2,1,0:T(8,128)(2,1)S(1)}, u32[]{:S(2)}, u32[]{:S(2)}) collective-permute-start(bf16[4,64,128]{2,1,0:T(8,128)(2,1)S(1)} %get-tuple-element.18), channel_id=1, source_target_pairs={{0,4},{2,6},{4,0},{6,2},{8,12},{10,14},{12,8},{14,10},{16,20},{18,... | collective-permute-start | bytes 196616 | tf_op jit(solution)/shard_map/ppermute | solution.py:358
  122.4 1.5 %collective-permute-start.5 = (bf16[4,64,128]{2,1,0:T(8,128)(2,1)S(1)}, bf16[4,64,128]{2,1,0:T(8,128)(2,1)S(1)}, u32[]{:S(2)}, u32[]{:S(2)}) collective-permute-start(bf16[4,64,128]{2,1,0:T(8,128)(2,1)S(1)} %get-tuple-element.17), channel_id=1, source_target_pairs={{0,6},{2,0},{4,2},{6,4},{8,14},{10,8},{12,10},{14,12},{16,22},{18,... | collective-permute-start | bytes 196616 | tf_op jit(solution)/shard_map/ppermute | solution.py:358
  123.8 0.2 select_reduce_fusion.1
  124.0 0.3 collective-permute-done.3
  124.3 1.5 %collective-permute-done.4 = bf16[4,64,128]{2,1,0:T(8,128)(2,1)S(1)} collective-permute-done((bf16[4,64,128]{2,1,0:T(8,128)(2,1)S(1)}, bf16[4,64,128]{2,1,0:T(8,128)(2,1)S(1)}, u32[]{:S(2)}, u32[]{:S(2)}) %collective-permute-start.4) | collective-permute-done | bytes 65568 | tf_op jit(solution)/shard_map/ppermute | solution.py:358
  125.8 0.8 collective-permute-done.5
  126.7 1.5 %collective-permute-start.6 = (bf16[64,128]{1,0:T(8,128)(2,1)S(1)}, bf16[64,128]{1,0:T(8,128)(2,1)S(1)}, u32[]{:S(2)}, u32[]{:S(2)}) collective-permute-start(bf16[64,128]{1,0:T(8,128)(2,1)S(1)} %get-tuple-element.19), channel_id=1, source_target_pairs={{0,8},{2,10},{4,12},{6,14},{8,16},{10,18},{12,20},{14,22},{16,24},... | collective-permute-start | bytes 49160 | tf_op jit(solution)/shard_map/ppermute | solution.py:358
  128.2 2.5 %collective-permute-start.7 = (bf16[64,128]{1,0:T(8,128)(2,1)S(1)}, bf16[64,128]{1,0:T(8,128)(2,1)S(1)}, u32[]{:S(2)}, u32[]{:S(2)}) collective-permute-start(bf16[64,128]{1,0:T(8,128)(2,1)S(1)} %get-tuple-element.21), channel_id=1, source_target_pairs={{0,16},{2,18},{4,20},{6,22},{8,24},{10,26},{12,28},{14,30},{16,0},... | collective-permute-start | bytes 49160 | tf_op jit(solution)/shard_map/ppermute | solution.py:358
  130.7 1.4 %collective-permute-start.8 = (bf16[64,128]{1,0:T(8,128)(2,1)S(1)}, bf16[64,128]{1,0:T(8,128)(2,1)S(1)}, u32[]{:S(2)}, u32[]{:S(2)}) collective-permute-start(bf16[64,128]{1,0:T(8,128)(2,1)S(1)} %get-tuple-element.20), channel_id=1, source_target_pairs={{0,24},{2,26},{4,28},{6,30},{8,0},{10,2},{12,4},{14,6},{16,8},{18,... | collective-permute-start | bytes 49160 | tf_op jit(solution)/shard_map/ppermute | solution.py:358
  132.1 1.4 %dynamic-slice_add_fusion = f32[128]{0:T(128)S(1)} fusion(f32[1024]{0:T(1024)} %param.16, s32[]{:T(128)S(6)} %select_n.165, f32[]{:T(128)} %bitcast.19), kind=kLoop, calls=%fused_computation.37 | loop fusion | flops 128 | bytes 1032 | tf_op jit(solution)/shard_map/add | solution.py:405
  133.5 0.9 collective-permute-done.8
  134.4 0.7 subtract_divide_fusion
  (25 shorter events, 0.6 us)
Async XLA Ops:
  0.6 114.5 %copy-start = (bf16[256,8,128]{2,1,0:T(8,128)(2,1)S(1)}, bf16[256,8,128]{2,1,0:T(8,128)(2,1)}, u32[]{:S(2)}) copy-start(bf16[256,8,128]{2,1,0:T(8,128)(2,1)} %param.15) | copy-start | bytes 1572868
  0.6 15.8 %collective-permute-start = (bf16[64,32,64]{2,1,0:T(8,128)(2,1)}, bf16[64,32,64]{2,1,0:T(8,128)(2,1)S(1)}, u32[]{:S(2)}, u32[]{:S(2)}) collective-permute-start(bf16[64,32,64]{2,1,0:T(8,128)(2,1)} %refs_0_.2), channel_id=1, source_target_pairs={{0,2},{2,0},{1,3},{3,1},{4,6},{6,4},{5,7},{7,5},{8,10},{10,8},{9,1... | collective-permute-start | bytes 786440 | tf_op jit(solution)/shard_map/ppermute | solution.py:93
  4.4 11.5 %collective-permute-start.1 = (s32[64]{0:T(128)S(1)}, s32[64]{0:T(128)S(1)}, u32[]{:S(2)}, u32[]{:S(2)}) collective-permute-start(s32[64]{0:T(128)S(1)} %multiply_add_fusion), channel_id=1, source_target_pairs={{0,2},{2,0},{1,3},{3,1},{4,6},{6,4},{5,7},{7,5},{8,10},{10,8},{9,1... | collective-permute-start | bytes 776 | tf_op jit(solution)/shard_map/ppermute | solution.py:93
  16.5 6.1 %copy-start.2 = (bf16[64,32,64]{2,1,0:T(8,128)(2,1)}, bf16[64,32,64]{2,1,0:T(8,128)(2,1)S(1)}, u32[]{:S(2)}) copy-start(bf16[64,32,64]{2,1,0:T(8,128)(2,1)S(1)} %collective-permute-done.refs_1_) | copy-start | bytes 786436
  16.5 19.6 %all-to-all-start = ((bf16[8,256,128]{2,1,0:T(8,128)(2,1)}), bf16[8,256,128]{2,1,0:T(8,128)(2,1)S(1)}, u32[]{:S(2)}, u32[]{:S(2)}) async-start(bf16[8,256,128]{2,1,0:T(8,128)(2,1)} %shard_map.104), calls=%async_computation | async-start | bytes 1048576 | tf_op jit(solution)/shard_map/all_to_all | solution.py:376
  36.0 4.2 %copy-start.1 = (bf16[8,256,128]{2,1,0:T(8,128)(2,1)}, bf16[8,256,128]{2,1,0:T(8,128)(2,1)S(1)}, u32[]{:S(2)}) copy-start(bf16[8,256,128]{2,1,0:T(8,128)(2,1)S(1)} %all-to-all-done.row_ref) | copy-start | bytes 1572868
  36.0 79.0 %all-to-all-start.1 = ((f32[32,32,256]{2,1,0:T(8,128)}), f32[32,32,256]{2,1,0:T(8,128)S(1)}, u32[]{:S(2)}, u32[]{:S(2)}) async-start(f32[32,32,256]{2,1,0:T(8,128)} %shard_map.106), calls=%async_computation.1 | async-start | bytes 2097152 | tf_op jit(solution)/shard_map/all_to_all | solution.py:377
  40.3 83.6 %copy-start.3 = (f32[128]{0:T(128)S(1)}, f32[128]{0:T(128)}, u32[]{:S(2)}) copy-start(f32[128]{0:T(128)} %param.17) | copy-start | bytes 1540
  117.1 1.6 %collective-permute-start.2 = (bf16[2,64,1024]{2,1,0:T(8,128)(2,1)S(1)}, bf16[2,64,1024]{2,1,0:T(8,128)(2,1)S(1)}, u32[]{:S(2)}, u32[]{:S(2)}) collective-permute-start(bf16[2,64,1024]{2,1,0:T(8,128)(2,1)S(1)} %fusion.2), channel_id=1, source_target_pairs={{0,1},{1,0},{2,3},{3,2},{4,5},{5,4},{6,7},{7,6},{8,9},{9,8},{10,11... | collective-permute-start | bytes 786440 | tf_op jit(solution)/shard_map/ppermute | solution.py:358
  119.1 5.2 %collective-permute-start.3 = (bf16[4,64,128]{2,1,0:T(8,128)(2,1)S(1)}, bf16[4,64,128]{2,1,0:T(8,128)(2,1)S(1)}, u32[]{:S(2)}, u32[]{:S(2)}) collective-permute-start(bf16[4,64,128]{2,1,0:T(8,128)(2,1)S(1)} %get-tuple-element.16), channel_id=1, source_target_pairs={{0,2},{2,4},{4,6},{6,0},{8,10},{10,12},{12,14},{14,8},{16,18},{18,... | collective-permute-start | bytes 196616 | tf_op jit(solution)/shard_map/ppermute | solution.py:358
  120.9 4.9 %collective-permute-start.4 = (bf16[4,64,128]{2,1,0:T(8,128)(2,1)S(1)}, bf16[4,64,128]{2,1,0:T(8,128)(2,1)S(1)}, u32[]{:S(2)}, u32[]{:S(2)}) collective-permute-start(bf16[4,64,128]{2,1,0:T(8,128)(2,1)S(1)} %get-tuple-element.18), channel_id=1, source_target_pairs={{0,4},{2,6},{4,0},{6,2},{8,12},{10,14},{12,8},{14,10},{16,20},{18,... | collective-permute-start | bytes 196616 | tf_op jit(solution)/shard_map/ppermute | solution.py:358
  122.4 4.3 %collective-permute-start.5 = (bf16[4,64,128]{2,1,0:T(8,128)(2,1)S(1)}, bf16[4,64,128]{2,1,0:T(8,128)(2,1)S(1)}, u32[]{:S(2)}, u32[]{:S(2)}) collective-permute-start(bf16[4,64,128]{2,1,0:T(8,128)(2,1)S(1)} %get-tuple-element.17), channel_id=1, source_target_pairs={{0,6},{2,0},{4,2},{6,4},{8,14},{10,8},{12,10},{14,12},{16,22},{18,... | collective-permute-start | bytes 196616 | tf_op jit(solution)/shard_map/ppermute | solution.py:358
  126.7 6.8 %collective-permute-start.6 = (bf16[64,128]{1,0:T(8,128)(2,1)S(1)}, bf16[64,128]{1,0:T(8,128)(2,1)S(1)}, u32[]{:S(2)}, u32[]{:S(2)}) collective-permute-start(bf16[64,128]{1,0:T(8,128)(2,1)S(1)} %get-tuple-element.19), channel_id=1, source_target_pairs={{0,8},{2,10},{4,12},{6,14},{8,16},{10,18},{12,20},{14,22},{16,24},... | collective-permute-start | bytes 49160 | tf_op jit(solution)/shard_map/ppermute | solution.py:358
  128.2 5.3 %collective-permute-start.7 = (bf16[64,128]{1,0:T(8,128)(2,1)S(1)}, bf16[64,128]{1,0:T(8,128)(2,1)S(1)}, u32[]{:S(2)}, u32[]{:S(2)}) collective-permute-start(bf16[64,128]{1,0:T(8,128)(2,1)S(1)} %get-tuple-element.21), channel_id=1, source_target_pairs={{0,16},{2,18},{4,20},{6,22},{8,24},{10,26},{12,28},{14,30},{16,0},... | collective-permute-start | bytes 49160 | tf_op jit(solution)/shard_map/ppermute | solution.py:358
  130.7 3.7 %collective-permute-start.8 = (bf16[64,128]{1,0:T(8,128)(2,1)S(1)}, bf16[64,128]{1,0:T(8,128)(2,1)S(1)}, u32[]{:S(2)}, u32[]{:S(2)}) collective-permute-start(bf16[64,128]{1,0:T(8,128)(2,1)S(1)} %get-tuple-element.20), channel_id=1, source_target_pairs={{0,24},{2,26},{4,28},{6,30},{8,0},{10,2},{12,4},{14,6},{16,8},{18,... | collective-permute-start | bytes 49160 | tf_op jit(solution)/shard_map/ppermute | solution.py:358

commit v4 on v3

--- a/solution.py
+++ b/solution.py
@@ -150,21 +150,24 @@
     amp_refs, ov_refs = amp_refs[:groups], amp_refs[groups:]
     step = pl.program_id(0)
     blocks, slots = code_ref.shape[0], block_of.shape[0]
-    own = amp_refs[0].shape[0]
+    own, width = 2 * amp_refs[0].shape[0], amps.shape[2]
 
     @pl.when(step == 0)
     def _():
         for k, ref in enumerate(amp_refs):
-            amps[pl.ds(k * own, own)] = ref[...]
+            for h in range(2):
+                amps[pl.ds(k * own + h * (own // 2), own // 2)] = ref[
+                    :, :, h * width : (h + 1) * width
+                ]
         amps[blocks] = jnp.zeros(amps.shape[1:], bf16)
         acc[...] = jnp.zeros_like(acc)
         first = place_ref[0] * slots
 
-        @pl.loop(0, slots)
+        @pl.loop(0, slots, unroll=16)
         def _(s):
             block_of[s] = blocks
 
-        @pl.loop(0, blocks)
+        @pl.loop(0, blocks, unroll=8)
         def _(n):
             slot = code_ref[n] - first
 
@@ -172,12 +175,11 @@
             def _():
                 block_of[slot] = n
 
-    here, width, chol = ov_refs[0].shape
-    for side, ref in enumerate(ov_refs):
-        start = (step * len(ov_refs) + side) * here
-        left = jnp.concatenate([amps[block_of[start + s]] for s in range(here)], axis=1)
-        right = ref[...].reshape(here * width, chol)
-        acc[...] += jnp.dot(left, right, preferred_element_type=f32)
+    here, _, chol = ov_refs[0].shape
+    start, count = step * len(ov_refs) * here, len(ov_refs) * here
+    left = jnp.concatenate([amps[block_of[start + s]] for s in range(count)], axis=1)
+    right = jnp.concatenate([ref[...].reshape(here * width, chol) for ref in ov_refs], axis=0)
+    acc[...] += jnp.dot(left, right, preferred_element_type=f32)
 
     @pl.when(step == pl.num_programs(0) - 1)
     def _():
@@ -189,7 +191,8 @@
 
 def cycle_operands(cycle_amp, owner_of, slot_of, slots):
     codes = jnp.concatenate(round_robin(owner_of * slots + slot_of, "ph"))
-    return round_robin(cycle_amp, "ph"), codes
+    near, far = jnp.split(cycle_amp, 2, 0)
+    return round_robin(jnp.concatenate([near, far], 2), "ph"), codes
 
 
 def cycle_partial(amps, codes, ov_slots):
@@ -275,11 +278,34 @@
         for i, r in enumerate(rows):
             turned[:, r, :] = block[:, i * pairs : (i + 1) * pairs].reshape(deep, deep, pairs)
 
+    sublane = lax.broadcasted_iota(jnp.int32, (deep // 8, 8, LANES), 1)
+
+    def by_shuffle(first):
+        for h in range(pairs // LANES):
+            lane = slice(h * LANES, (h + 1) * LANES)
+            block = amp_buf[slot, first : first + deep, :, lane].astype(f32)
+            block = block.reshape(deep // 8, 8, deep, LANES)
+            for o in range(0, deep, 8):
+                v = [block[:, a, o : o + 8] for a in range(8)]
+                for k in (4, 2, 1):
+                    keep = (sublane & k) == 0
+                    for a in range(8):
+                        if not a & k:
+                            x, y = v[a], v[a + k]
+                            v[a] = jnp.where(keep, x, pltpu.roll(y, k, 1))
+                            v[a + k] = jnp.where(keep, pltpu.roll(x, 8 - k, 1), y)
+                for d in range(8):
+                    turned[o + d, first : first + deep, lane] = (
+                        v[d].reshape(deep, LANES).astype(bf16)
+                    )
+
     for q in range(sides):
         arriving(amp_hbm, amp_buf, amp_sem, step, q).wait()
         size = virtuals // sides
-        for k in range(q * size, (q + 1) * size, 2 * deep):
+        for k in range(q * size, (q + 1) * size, 4 * deep):
             by_matmul(k)
+            by_shuffle(k + 2 * deep)
+            by_shuffle(k + 3 * deep)
 
     row = jnp.concatenate([row_ref[k] for k in range(count)], axis=1)
     for d in range(0, deep, 2):
@@ -367,7 +393,7 @@
     slots, _, width = ov_slots.shape
     n_vir, n_ph, n_vec = (lax.axis_size(a) for a in ("vir", "ph", "vec"))
     fits = slab == LANES and pairs == 2 * LANES and chol % LANES == 0 and slots % 32 == 0
-    if not fits or 256 % width or n_vir * n_ph % 4:
+    if not fits or 256 % width or cycle_amp.shape[0] % 2 or n_vir * n_ph % 4:
         return plain(
             vv_factor, ladder_amp, cycle_amp, ov_slots, owner_of, slot_of, ov_pairs, eps_vir, eps_occ
         )

time: 136 us -> 134 us (0.985)
  waiting for transfers between devices: 10.5 us -> 7.68 us
    ppermute x2, waiting for transfers between devices: 5.04 us -> 0.01 us  [shifted(): return lax.ppermute(x, axes, [(i, (i + k) % n) for i in range(n)])]
    all_to_all x1, waiting for transfers between devices: 1.85 us -> 4.04 us  [local(): row = lax.all_to_all(row, 'vir', 0, 0)]
    pallas_call x1, Pallas kernels: 11.6 us -> 9.84 us  [cycle_partial(): pl.pallas_call(functools.partial(cycle_kernel, shares, len(amps)), grid=(...]
    pallas_call x1, Pallas kernels: 74.7 us -> 76.2 us  [ladder_partial(): pl.pallas_call(functools.partial(ladder_kernel, sides), grid=(slab // dee...]
  transfers between devices with their start and end apart: 11 -> 11, of which waited for: 7 -> 6; matrix products, arithmetic and copies ran while one was open for 3% -> 3% of each run, Pallas kernels for 69% -> 70%
where the time goes in v4:
time: 134 us; the launch traced here: 133 us
  Pallas kernels  92.5 us (69%)
  starting transfers between devices  23.5 us (18%)
  waiting for transfers between devices  7.68 us (6%)
  other arithmetic  5.32 us (4%)
  local copies, waits for them, and re-layouts  3.05 us (2%)
    pallas_call x1, Pallas kernels, ladder_partial(): pl.pallas_call(functools.partial(ladder_kernel, sides), grid=(slab // dee...  76.2 us
    ppermute x7, starting transfers between devices, scatter_sum(): total = total + lax.ppermute(piece, axes, pairs).astype(f32)  10.4 us
    pallas_call x1, Pallas kernels, cycle_partial(): pl.pallas_call(functools.partial(cycle_kernel, shares, len(amps)), grid=(...  9.84 us
    pallas_call x1, Pallas kernels, own_row(): pl.pallas_call(row_kernel, grid=(chol // LANES, steps), in_specs=[side(q)...  6.42 us
    all_to_all x1, starting transfers between devices, local(): row = lax.all_to_all(row, 'vir', 0, 0)  6.28 us
    all_to_all x1, waiting for transfers between devices, local(): row = lax.all_to_all(row, 'vir', 0, 0)  4.04 us
    all_to_all x1, starting transfers between devices, local(): lax.all_to_all(cycle_partial(amps, codes, ov_slots), ('vir', 'ph', 'vec')...  3.68 us
    ppermute x7, waiting for transfers between devices, scatter_sum(): total = total + lax.ppermute(piece, axes, pairs).astype(f32)  3.63 us
  transfers between devices with their start and end apart: 11, of which 6 were waited for; matrix products, arithmetic and copies ran while one was open for 3% of the time, Pallas kernels for 70%

profile of v4, /device:TPU:0, one launch (start us, length us, event | category | flops | bytes accessed | tf_op | source)
XLA Modules:
  0.0 133.0 jit_solution(10520835894687022523)
XLA Ops:
  0.6 1.1 fusion.14
  1.8 0.1 pad_maximum_fusion.refs_0_
  1.9 3.0 %collective-permute-start = (bf16[32,32,128]{2,1,0:T(8,128)(2,1)S(1)}, bf16[32,32,128]{2,1,0:T(8,128)(2,1)S(1)}, u32[]{:S(2)}, u32[]{:S(2)}) collective-permute-start(bf16[32,32,128]{2,1,0:T(8,128)(2,1)S(1)} %pad_maximum_fusion.refs_0_), channel_id=1, source_target_pairs={{0,2},{2,0},{1,3},{3,1},{4,6},{6,4},{5,7},{7,5},{8,10},{10,8},{9,1... | collective-permute-start | bytes 786440 | tf_op jit(solution)/shard_map/ppermute | solution.py:93
  5.0 0.7 multiply_add_fusion
  5.7 6.4 %shard_map.104 = bf16[8,256,128]{2,1,0:T(8,128)(2,1)} custom-call(bf16[256,128,1024]{2,1,0:T(8,128)(2,1)} %factor_hbm.1, bf16[256,128,1024]{2,1,0:T(8,128)(2,1)} %factor_hbm.1, bf16[256,128,1024]{2,1,0:T(8,128)(2,1)} %factor_hbm.1, bf16[256,128,1024]{2,1,0:T(8,128)(2,1)} %factor_hbm.1), custom_call_target="tpu_custom_call" | custom-call | flops 8388608 | bytes 8388608 | tf_op jit(solution)/shard_map/pallas_call | solution.py:134
  12.1 0.6 pad_add_fusion.code_ref
  12.7 6.3 %all-to-all-start = ((bf16[8,256,128]{2,1,0:T(8,128)(2,1)}), bf16[8,256,128]{2,1,0:T(8,128)(2,1)S(1)}, u32[]{:S(2)}, u32[]{:S(2)}) async-start(bf16[8,256,128]{2,1,0:T(8,128)(2,1)} %shard_map.104), calls=%async_computation | async-start | bytes 1048576 | tf_op jit(solution)/shard_map/all_to_all | solution.py:402
  19.1 9.8 %shard_map.106 = f32[32,32,256]{2,1,0:T(8,128)} custom-call(s32[1]{0:T(128)} %bitcast.2.place_ref, s32[128]{0:T(128)} %pad_add_fusion.code_ref, bf16[32,32,128]{2,1,0:T(8,128)(2,1)} %copy-done.2, bf16[32,32,128]{2,1,0:T(8,128)(2,1)} %copy-done.3, bf16[128,64,1024]{2,1,0:T(8,128)(2,1)} %bitcast.60, bf16[128,64,1024]{2,1,0:T(8,128)(2,1)} %bitcast.61, ...), custom_call_target="tpu_custom_call" | custom-call | flops 536870912 | bytes 16777216 | tf_op jit(solution)/shard_map/pallas_call | solution.py:211
  28.9 4.0 %all-to-all-done.row_ref = bf16[8,256,128]{2,1,0:T(8,128)(2,1)S(1)} async-done(((bf16[8,256,128]{2,1,0:T(8,128)(2,1)}), bf16[8,256,128]{2,1,0:T(8,128)(2,1)S(1)}, u32[]{:S(2)}, u32[]{:S(2)}) %all-to-all-start) | async-done | bytes 524320 | tf_op jit(solution)/shard_map/all_to_all | solution.py:402
  32.9 3.7 %all-to-all-start.1 = ((f32[32,32,256]{2,1,0:T(8,128)}), f32[32,32,256]{2,1,0:T(8,128)S(1)}, u32[]{:S(2)}, u32[]{:S(2)}) async-start(f32[32,32,256]{2,1,0:T(8,128)} %shard_map.106), calls=%async_computation.1 | async-start | bytes 2097152 | tf_op jit(solution)/shard_map/all_to_all | solution.py:403
  36.7 76.2 %shard_map.105 = f32[256,1024]{1,0:T(8,128)} custom-call(bf16[8,256,128]{2,1,0:T(8,128)(2,1)} %copy-done.1, bf16[1024,128,256]{2,1,0:T(8,128)(2,1)} %amp_hbm.1, bf16[256,128,1024]{2,1,0:T(8,128)(2,1)} %factor_hbm.1), custom_call_target="tpu_custom_call" | custom-call | flops 34359738368 | bytes 134217728 | tf_op jit(solution)/shard_map/pallas_call | solution.py:340
  113.0 0.2 fusion
  113.2 0.1 copy.24
  113.3 0.2 broadcast_in_dim.62
  113.5 1.4 %select_add_fusion = f32[2,2,64,1024]{3,2,1,0:T(8,128)S(1)} fusion(f32[2,2,64,1024]{3,2,1,0:T(8,128)} %bitcast.64, f32[2,2,64,1024]{3,2,1,0:T(8,128)S(1)} %broadcast_in_dim.62, pred[1024]{0:T(1024)(128)(4,1)S(1)} %broadcast_bitcast_fusion), kind=kLoop, calls=%fused_computation | loop fusion | flops 524288 | bytes 3146752 | tf_op jit(solution)/shard_map/add | solution.py:413
  114.9 0.3 collective-permute-start.2
  115.2 1.2 slice.3
  116.6 0.1 copy.20
  116.8 0.1 copy.19
  116.9 1.8 %collective-permute-start.3 = (bf16[4,64,128]{2,1,0:T(8,128)(2,1)S(1)}, bf16[4,64,128]{2,1,0:T(8,128)(2,1)S(1)}, u32[]{:S(2)}, u32[]{:S(2)}) collective-permute-start(bf16[4,64,128]{2,1,0:T(8,128)(2,1)S(1)} %get-tuple-element.18), channel_id=1, source_target_pairs={{0,2},{2,4},{4,6},{6,0},{8,10},{10,12},{12,14},{14,8},{16,18},{18,... | collective-permute-start | bytes 196616 | tf_op jit(solution)/shard_map/ppermute | solution.py:384
  118.8 1.5 %collective-permute-start.4 = (bf16[4,64,128]{2,1,0:T(8,128)(2,1)S(1)}, bf16[4,64,128]{2,1,0:T(8,128)(2,1)S(1)}, u32[]{:S(2)}, u32[]{:S(2)}) collective-permute-start(bf16[4,64,128]{2,1,0:T(8,128)(2,1)S(1)} %get-tuple-element.20), channel_id=1, source_target_pairs={{0,4},{2,6},{4,0},{6,2},{8,12},{10,14},{12,8},{14,10},{16,20},{18,... | collective-permute-start | bytes 196616 | tf_op jit(solution)/shard_map/ppermute | solution.py:384
  120.2 1.5 %collective-permute-start.5 = (bf16[4,64,128]{2,1,0:T(8,128)(2,1)S(1)}, bf16[4,64,128]{2,1,0:T(8,128)(2,1)S(1)}, u32[]{:S(2)}, u32[]{:S(2)}) collective-permute-start(bf16[4,64,128]{2,1,0:T(8,128)(2,1)S(1)} %get-tuple-element.19), channel_id=1, source_target_pairs={{0,6},{2,0},{4,2},{6,4},{8,14},{10,8},{12,10},{14,12},{16,22},{18,... | collective-permute-start | bytes 196616 | tf_op jit(solution)/shard_map/ppermute | solution.py:384
  121.7 0.2 select_reduce_fusion.1
  121.9 0.3 collective-permute-done.3
  122.2 1.5 %collective-permute-done.4 = bf16[4,64,128]{2,1,0:T(8,128)(2,1)S(1)} collective-permute-done((bf16[4,64,128]{2,1,0:T(8,128)(2,1)S(1)}, bf16[4,64,128]{2,1,0:T(8,128)(2,1)S(1)}, u32[]{:S(2)}, u32[]{:S(2)}) %collective-permute-start.4) | collective-permute-done | bytes 65568 | tf_op jit(solution)/shard_map/ppermute | solution.py:384
  123.7 0.8 collective-permute-done.5
  124.6 1.5 %collective-permute-start.6 = (bf16[64,128]{1,0:T(8,128)(2,1)S(1)}, bf16[64,128]{1,0:T(8,128)(2,1)S(1)}, u32[]{:S(2)}, u32[]{:S(2)}) collective-permute-start(bf16[64,128]{1,0:T(8,128)(2,1)S(1)} %get-tuple-element.21), channel_id=1, source_target_pairs={{0,8},{2,10},{4,12},{6,14},{8,16},{10,18},{12,20},{14,22},{16,24},... | collective-permute-start | bytes 49160 | tf_op jit(solution)/shard_map/ppermute | solution.py:384
  126.1 2.5 %collective-permute-start.7 = (bf16[64,128]{1,0:T(8,128)(2,1)S(1)}, bf16[64,128]{1,0:T(8,128)(2,1)S(1)}, u32[]{:S(2)}, u32[]{:S(2)}) collective-permute-start(bf16[64,128]{1,0:T(8,128)(2,1)S(1)} %get-tuple-element.23), channel_id=1, source_target_pairs={{0,16},{2,18},{4,20},{6,22},{8,24},{10,26},{12,28},{14,30},{16,0},... | collective-permute-start | bytes 49160 | tf_op jit(solution)/shard_map/ppermute | solution.py:384
  128.5 1.4 %collective-permute-start.8 = (bf16[64,128]{1,0:T(8,128)(2,1)S(1)}, bf16[64,128]{1,0:T(8,128)(2,1)S(1)}, u32[]{:S(2)}, u32[]{:S(2)}) collective-permute-start(bf16[64,128]{1,0:T(8,128)(2,1)S(1)} %get-tuple-element.22), channel_id=1, source_target_pairs={{0,24},{2,26},{4,28},{6,30},{8,0},{10,2},{12,4},{14,6},{16,8},{18,... | collective-permute-start | bytes 49160 | tf_op jit(solution)/shard_map/ppermute | solution.py:384
  129.9 1.4 %dynamic-slice_add_fusion = f32[128]{0:T(128)S(1)} fusion(f32[1024]{0:T(1024)} %param.16, s32[]{:T(128)S(6)} %select_n.165, f32[]{:T(128)} %bitcast.19), kind=kLoop, calls=%fused_computation.38 | loop fusion | flops 128 | bytes 1032 | tf_op jit(solution)/shard_map/add | solution.py:431
  131.4 0.9 collective-permute-done.8
  132.3 0.7 subtract_divide_fusion
  (29 shorter events, 0.6 us)
Async XLA Ops:
  0.6 112.3 %copy-start = (bf16[256,8,128]{2,1,0:T(8,128)(2,1)S(1)}, bf16[256,8,128]{2,1,0:T(8,128)(2,1)}, u32[]{:S(2)}) copy-start(bf16[256,8,128]{2,1,0:T(8,128)(2,1)} %param.15) | copy-start | bytes 1572868
  1.9 10.2 %copy-start.2 = (bf16[32,32,128]{2,1,0:T(8,128)(2,1)}, bf16[32,32,128]{2,1,0:T(8,128)(2,1)S(1)}, u32[]{:S(2)}) copy-start(bf16[32,32,128]{2,1,0:T(8,128)(2,1)S(1)} %pad_maximum_fusion.refs_0_) | copy-start | bytes 786436
  1.9 10.8 %collective-permute-start = (bf16[32,32,128]{2,1,0:T(8,128)(2,1)S(1)}, bf16[32,32,128]{2,1,0:T(8,128)(2,1)S(1)}, u32[]{:S(2)}, u32[]{:S(2)}) collective-permute-start(bf16[32,32,128]{2,1,0:T(8,128)(2,1)S(1)} %pad_maximum_fusion.refs_0_), channel_id=1, source_target_pairs={{0,2},{2,0},{1,3},{3,1},{4,6},{6,4},{5,7},{7,5},{8,10},{10,8},{9,1... | collective-permute-start | bytes 786440 | tf_op jit(solution)/shard_map/ppermute | solution.py:93
  5.6 6.5 %collective-permute-start.1 = (s32[64]{0:T(128)S(1)}, s32[64]{0:T(128)S(1)}, u32[]{:S(2)}, u32[]{:S(2)}) collective-permute-start(s32[64]{0:T(128)S(1)} %multiply_add_fusion), channel_id=1, source_target_pairs={{0,2},{2,0},{1,3},{3,1},{4,6},{6,4},{5,7},{7,5},{8,10},{10,8},{9,1... | collective-permute-start | bytes 776 | tf_op jit(solution)/shard_map/ppermute | solution.py:93
  12.7 6.4 %copy-start.3 = (bf16[32,32,128]{2,1,0:T(8,128)(2,1)}, bf16[32,32,128]{2,1,0:T(8,128)(2,1)S(1)}, u32[]{:S(2)}) copy-start(bf16[32,32,128]{2,1,0:T(8,128)(2,1)S(1)} %collective-permute-done.refs_1_) | copy-start | bytes 786436
  12.7 20.2 %all-to-all-start = ((bf16[8,256,128]{2,1,0:T(8,128)(2,1)}), bf16[8,256,128]{2,1,0:T(8,128)(2,1)S(1)}, u32[]{:S(2)}, u32[]{:S(2)}) async-start(bf16[8,256,128]{2,1,0:T(8,128)(2,1)} %shard_map.104), calls=%async_computation | async-start | bytes 1048576 | tf_op jit(solution)/shard_map/all_to_all | solution.py:402
  32.9 3.7 %copy-start.1 = (bf16[8,256,128]{2,1,0:T(8,128)(2,1)}, bf16[8,256,128]{2,1,0:T(8,128)(2,1)S(1)}, u32[]{:S(2)}) copy-start(bf16[8,256,128]{2,1,0:T(8,128)(2,1)S(1)} %all-to-all-done.row_ref) | copy-start | bytes 1572868
  32.9 79.9 %all-to-all-start.1 = ((f32[32,32,256]{2,1,0:T(8,128)}), f32[32,32,256]{2,1,0:T(8,128)S(1)}, u32[]{:S(2)}, u32[]{:S(2)}) async-start(f32[32,32,256]{2,1,0:T(8,128)} %shard_map.106), calls=%async_computation.1 | async-start | bytes 2097152 | tf_op jit(solution)/shard_map/all_to_all | solution.py:403
  36.6 85.0 %copy-start.4 = (f32[128]{0:T(128)S(1)}, f32[128]{0:T(128)}, u32[]{:S(2)}) copy-start(f32[128]{0:T(128)} %param.17) | copy-start | bytes 1540
  114.9 1.6 %collective-permute-start.2 = (bf16[2,64,1024]{2,1,0:T(8,128)(2,1)S(1)}, bf16[2,64,1024]{2,1,0:T(8,128)(2,1)S(1)}, u32[]{:S(2)}, u32[]{:S(2)}) collective-permute-start(bf16[2,64,1024]{2,1,0:T(8,128)(2,1)S(1)} %fusion.2), channel_id=1, source_target_pairs={{0,1},{1,0},{2,3},{3,2},{4,5},{5,4},{6,7},{7,6},{8,9},{9,8},{10,11... | collective-permute-start | bytes 786440 | tf_op jit(solution)/shard_map/ppermute | solution.py:384
  116.9 5.2 %collective-permute-start.3 = (bf16[4,64,128]{2,1,0:T(8,128)(2,1)S(1)}, bf16[4,64,128]{2,1,0:T(8,128)(2,1)S(1)}, u32[]{:S(2)}, u32[]{:S(2)}) collective-permute-start(bf16[4,64,128]{2,1,0:T(8,128)(2,1)S(1)} %get-tuple-element.18), channel_id=1, source_target_pairs={{0,2},{2,4},{4,6},{6,0},{8,10},{10,12},{12,14},{14,8},{16,18},{18,... | collective-permute-start | bytes 196616 | tf_op jit(solution)/shard_map/ppermute | solution.py:384
  118.8 4.9 %collective-permute-start.4 = (bf16[4,64,128]{2,1,0:T(8,128)(2,1)S(1)}, bf16[4,64,128]{2,1,0:T(8,128)(2,1)S(1)}, u32[]{:S(2)}, u32[]{:S(2)}) collective-permute-start(bf16[4,64,128]{2,1,0:T(8,128)(2,1)S(1)} %get-tuple-element.20), channel_id=1, source_target_pairs={{0,4},{2,6},{4,0},{6,2},{8,12},{10,14},{12,8},{14,10},{16,20},{18,... | collective-permute-start | bytes 196616 | tf_op jit(solution)/shard_map/ppermute | solution.py:384
  120.2 4.3 %collective-permute-start.5 = (bf16[4,64,128]{2,1,0:T(8,128)(2,1)S(1)}, bf16[4,64,128]{2,1,0:T(8,128)(2,1)S(1)}, u32[]{:S(2)}, u32[]{:S(2)}) collective-permute-start(bf16[4,64,128]{2,1,0:T(8,128)(2,1)S(1)} %get-tuple-element.19), channel_id=1, source_target_pairs={{0,6},{2,0},{4,2},{6,4},{8,14},{10,8},{12,10},{14,12},{16,22},{18,... | collective-permute-start | bytes 196616 | tf_op jit(solution)/shard_map/ppermute | solution.py:384
  124.6 6.8 %collective-permute-start.6 = (bf16[64,128]{1,0:T(8,128)(2,1)S(1)}, bf16[64,128]{1,0:T(8,128)(2,1)S(1)}, u32[]{:S(2)}, u32[]{:S(2)}) collective-permute-start(bf16[64,128]{1,0:T(8,128)(2,1)S(1)} %get-tuple-element.21), channel_id=1, source_target_pairs={{0,8},{2,10},{4,12},{6,14},{8,16},{10,18},{12,20},{14,22},{16,24},... | collective-permute-start | bytes 49160 | tf_op jit(solution)/shard_map/ppermute | solution.py:384
  126.1 5.3 %collective-permute-start.7 = (bf16[64,128]{1,0:T(8,128)(2,1)S(1)}, bf16[64,128]{1,0:T(8,128)(2,1)S(1)}, u32[]{:S(2)}, u32[]{:S(2)}) collective-permute-start(bf16[64,128]{1,0:T(8,128)(2,1)S(1)} %get-tuple-element.23), channel_id=1, source_target_pairs={{0,16},{2,18},{4,20},{6,22},{8,24},{10,26},{12,28},{14,30},{16,0},... | collective-permute-start | bytes 49160 | tf_op jit(solution)/shard_map/ppermute | solution.py:384
  128.5 3.7 %collective-permute-start.8 = (bf16[64,128]{1,0:T(8,128)(2,1)S(1)}, bf16[64,128]{1,0:T(8,128)(2,1)S(1)}, u32[]{:S(2)}, u32[]{:S(2)}) collective-permute-start(bf16[64,128]{1,0:T(8,128)(2,1)S(1)} %get-tuple-element.22), channel_id=1, source_target_pairs={{0,24},{2,26},{4,28},{6,30},{8,0},{10,2},{12,4},{14,6},{16,8},{18,... | collective-permute-start | bytes 49160 | tf_op jit(solution)/shard_map/ppermute | solution.py:384

commit v5 on v4

--- a/solution.py
+++ b/solution.py
@@ -238,7 +238,7 @@
 
 
 def ladder_kernel(sides, row_ref, amp_hbm, factor_hbm, out_ref, *scratch):
-    (amp_buf, factor_buf, amp_sem, factor_sem, swap, turned, half) = scratch
+    (amp_buf, factor_buf, amp_sem, factor_sem, swap, turned, half, flat) = scratch
     _, virtuals, deep, pairs = amp_buf.shape
     count, chol, _ = row_ref.shape
     square = deep * deep
@@ -269,67 +269,76 @@
     def _():
         start(step + 1)
 
-    def by_matmul(first):
+    def later(jobs):
+        store = None
+        for job in jobs:
+            after = job()
+            if store is not None:
+                store()
+            store = after
+        store()
+
+    def reorder(first):
         rows = [slice(first + r * deep, first + (r + 1) * deep) for r in range(2)]
         block = [amp_buf[slot, r].reshape(square, pairs) for r in rows]
         block = jnp.dot(
             swap[...], jnp.concatenate(block, axis=1), preferred_element_type=f32
         ).astype(bf16)
-        for i, r in enumerate(rows):
-            turned[:, r, :] = block[:, i * pairs : (i + 1) * pairs].reshape(deep, deep, pairs)
-
-    sublane = lax.broadcasted_iota(jnp.int32, (deep // 8, 8, LANES), 1)
-
-    def by_shuffle(first):
-        for h in range(pairs // LANES):
-            lane = slice(h * LANES, (h + 1) * LANES)
-            block = amp_buf[slot, first : first + deep, :, lane].astype(f32)
-            block = block.reshape(deep // 8, 8, deep, LANES)
-            for o in range(0, deep, 8):
-                v = [block[:, a, o : o + 8] for a in range(8)]
-                for k in (4, 2, 1):
-                    keep = (sublane & k) == 0
-                    for a in range(8):
-                        if not a & k:
-                            x, y = v[a], v[a + k]
-                            v[a] = jnp.where(keep, x, pltpu.roll(y, k, 1))
-                            v[a + k] = jnp.where(keep, pltpu.roll(x, 8 - k, 1), y)
-                for d in range(8):
-                    turned[o + d, first : first + deep, lane] = (
-                        v[d].reshape(deep, LANES).astype(bf16)
-                    )
+
+        def store():
+            for i, r in enumerate(rows):
+                turned[:, r, :] = block[:, i * pairs : (i + 1) * pairs].reshape(deep, deep, pairs)
+
+        return store
 
     for q in range(sides):
         arriving(amp_hbm, amp_buf, amp_sem, step, q).wait()
         size = virtuals // sides
-        for k in range(q * size, (q + 1) * size, 4 * deep):
-            by_matmul(k)
-            by_shuffle(k + 2 * deep)
-            by_shuffle(k + 3 * deep)
+        later(
+            functools.partial(reorder, k) for k in range(q * size, (q + 1) * size, 2 * deep)
+        )
 
     row = jnp.concatenate([row_ref[k] for k in range(count)], axis=1)
-    for d in range(0, deep, 2):
+
+    def halves(d):
         block = jnp.concatenate([turned[d], turned[d + 1]], axis=1)
         block = jnp.dot(row, block, preferred_element_type=f32).astype(bf16)
-        half[d], half[d + 1] = block[:, :pairs], block[:, pairs:]
-
-    for q in range(sides):
-        arriving(factor_hbm, factor_buf, factor_sem, step, q).wait()
-        size = chol // sides
-        block = [
-            half[:, k : k + deep, :].reshape(square, pairs).T
-            for k in range(q * size, (q + 1) * size, deep)
-        ]
+
+        def store():
+            half[d], half[d + 1] = block[:, :pairs], block[:, pairs:]
+
+        return store
+
+    later(functools.partial(halves, d) for d in range(0, deep, 2))
+
+    def flatten(first):
+        parts = range(first, first + 4 * deep, deep)
+        block = [half[:, k : k + deep, :].reshape(square, pairs).T for k in parts]
         block = jnp.dot(
             jnp.concatenate(block, axis=0), swap[...], preferred_element_type=f32
         ).astype(bf16)
-        block = [block[k * pairs : (k + 1) * pairs] for k in range(size // deep)]
-        factor = factor_buf[slot, q * size : (q + 1) * size]
-        out_ref[...] += jnp.dot(
-            jnp.concatenate(block, axis=1),
-            factor.reshape(size * deep, factor.shape[2]),
-            preferred_element_type=f32,
-        )
+
+        def store():
+            for i, k in enumerate(parts):
+                flat[:, k * deep : (k + deep) * deep] = block[i * pairs : (i + 1) * pairs]
+
+        return store
+
+    later(functools.partial(flatten, k) for k in range(0, chol, 4 * deep))
+    for q in range(sides):
+        arriving(factor_hbm, factor_buf, factor_sem, step, q).wait()
+    columns = 512
+
+    def ladder(first):
+        block = factor_buf[slot, :, :, first : first + columns].reshape(chol * deep, columns)
+        block = jnp.dot(flat[...], block, preferred_element_type=f32)
+
+        def store():
+            out_ref[:, first : first + columns] += block
+
+        return store
+
+    later(functools.partial(ladder, n) for n in range(0, out_ref.shape[1], columns))
 
 
 def ladder_partial(row, ladder_amp, vv_factor):
@@ -351,6 +360,7 @@
             pltpu.VMEM((deep * deep, deep * deep), bf16),
             pltpu.VMEM((deep, virtuals, pairs), bf16),
             pltpu.VMEM((deep, chol, pairs), bf16),
+            pltpu.VMEM((pairs, chol * deep), bf16),
         ],
         compiler_params=pltpu.CompilerParams(vmem_limit_bytes=60 << 20),
         cost_estimate=pl.CostEstimate(
@@ -392,7 +402,7 @@
     pairs = ladder_amp.shape[2]
     slots, _, width = ov_slots.shape
     n_vir, n_ph, n_vec = (lax.axis_size(a) for a in ("vir", "ph", "vec"))
-    fits = slab == LANES and pairs == 2 * LANES and chol % LANES == 0 and slots % 32 == 0
+    fits = slab == LANES and virtuals % 512 == 0 and pairs == 2 * LANES and chol % LANES == 0 and slots % 32 == 0
     if not fits or 256 % width or cycle_amp.shape[0] % 2 or n_vir * n_ph % 4:
         return plain(
             vv_factor, ladder_amp, cycle_amp, ov_slots, owner_of, slot_of, ov_pairs, eps_vir, eps_occ

time: 134 us -> 127 us (0.948)
  Pallas kernels: 92.5 us -> 86.3 us
    pallas_call x1, Pallas kernels: 76.2 us -> 70 us  [ladder_partial(): pl.pallas_call(functools.partial(ladder_kernel, sides), grid=(slab // dee...]
  transfers between devices with their start and end apart: 11 -> 11, of which waited for: 6 -> 6; matrix products, arithmetic and copies ran while one was open for 3% -> 3% of each run, Pallas kernels for 70% -> 68%
where the time goes in v5:
time: 127 us
  Pallas kernels  86.3 us (68%)
  starting transfers between devices  23.5 us (19%)
  waiting for transfers between devices  7.69 us (6%)
  other arithmetic  5.32 us (4%)
  local copies, waits for them, and re-layouts  3.05 us (2%)
    pallas_call x1, Pallas kernels, ladder_partial(): pl.pallas_call(functools.partial(ladder_kernel, sides), grid=(slab // dee...  70 us
    ppermute x7, starting transfers between devices, scatter_sum(): total = total + lax.ppermute(piece, axes, pairs).astype(f32)  10.4 us
    pallas_call x1, Pallas kernels, cycle_partial(): pl.pallas_call(functools.partial(cycle_kernel, shares, len(amps)), grid=(...  9.84 us
    pallas_call x1, Pallas kernels, own_row(): pl.pallas_call(row_kernel, grid=(chol // LANES, steps), in_specs=[side(q)...  6.42 us
    all_to_all x1, starting transfers between devices, local(): row = lax.all_to_all(row, 'vir', 0, 0)  6.28 us
    all_to_all x1, waiting for transfers between devices, local(): row = lax.all_to_all(row, 'vir', 0, 0)  4.05 us
    all_to_all x1, starting transfers between devices, local(): lax.all_to_all(cycle_partial(amps, codes, ov_slots), ('vir', 'ph', 'vec')...  3.68 us
    ppermute x7, waiting for transfers between devices, scatter_sum(): total = total + lax.ppermute(piece, axes, pairs).astype(f32)  3.63 us
  transfers between devices with their start and end apart: 11, of which 6 were waited for; matrix products, arithmetic and copies ran while one was open for 3% of the time, Pallas kernels for 68%

profile of v5, /device:TPU:0, one launch (start us, length us, event | category | flops | bytes accessed | tf_op | source)
XLA Modules:
  0.0 126.8 jit_solution(17365801337383608964)
XLA Ops:
  0.6 1.1 fusion.14
  1.8 0.1 pad_maximum_fusion.refs_0_
  1.9 3.0 %collective-permute-start = (bf16[32,32,128]{2,1,0:T(8,128)(2,1)S(1)}, bf16[32,32,128]{2,1,0:T(8,128)(2,1)S(1)}, u32[]{:S(2)}, u32[]{:S(2)}) collective-permute-start(bf16[32,32,128]{2,1,0:T(8,128)(2,1)S(1)} %pad_maximum_fusion.refs_0_), channel_id=1, source_target_pairs={{0,2},{2,0},{1,3},{3,1},{4,6},{6,4},{5,7},{7,5},{8,10},{10,8},{9,1... | collective-permute-start | bytes 786440 | tf_op jit(solution)/shard_map/ppermute | solution.py:93
  5.0 0.7 multiply_add_fusion
  5.7 6.4 %shard_map.104 = bf16[8,256,128]{2,1,0:T(8,128)(2,1)} custom-call(bf16[256,128,1024]{2,1,0:T(8,128)(2,1)} %factor_hbm.1, bf16[256,128,1024]{2,1,0:T(8,128)(2,1)} %factor_hbm.1, bf16[256,128,1024]{2,1,0:T(8,128)(2,1)} %factor_hbm.1, bf16[256,128,1024]{2,1,0:T(8,128)(2,1)} %factor_hbm.1), custom_call_target="tpu_custom_call" | custom-call | flops 8388608 | bytes 8388608 | tf_op jit(solution)/shard_map/pallas_call | solution.py:134
  12.1 0.6 pad_add_fusion.code_ref
  12.7 6.3 %all-to-all-start = ((bf16[8,256,128]{2,1,0:T(8,128)(2,1)}), bf16[8,256,128]{2,1,0:T(8,128)(2,1)S(1)}, u32[]{:S(2)}, u32[]{:S(2)}) async-start(bf16[8,256,128]{2,1,0:T(8,128)(2,1)} %shard_map.104), calls=%async_computation | async-start | bytes 1048576 | tf_op jit(solution)/shard_map/all_to_all | solution.py:412
  19.1 9.8 %shard_map.106 = f32[32,32,256]{2,1,0:T(8,128)} custom-call(s32[1]{0:T(128)} %bitcast.2.place_ref, s32[128]{0:T(128)} %pad_add_fusion.code_ref, bf16[32,32,128]{2,1,0:T(8,128)(2,1)} %copy-done.2, bf16[32,32,128]{2,1,0:T(8,128)(2,1)} %copy-done.3, bf16[128,64,1024]{2,1,0:T(8,128)(2,1)} %bitcast.60, bf16[128,64,1024]{2,1,0:T(8,128)(2,1)} %bitcast.61, ...), custom_call_target="tpu_custom_call" | custom-call | flops 536870912 | bytes 16777216 | tf_op jit(solution)/shard_map/pallas_call | solution.py:211
  28.9 4.0 %all-to-all-done.row_ref = bf16[8,256,128]{2,1,0:T(8,128)(2,1)S(1)} async-done(((bf16[8,256,128]{2,1,0:T(8,128)(2,1)}), bf16[8,256,128]{2,1,0:T(8,128)(2,1)S(1)}, u32[]{:S(2)}, u32[]{:S(2)}) %all-to-all-start) | async-done | bytes 524320 | tf_op jit(solution)/shard_map/all_to_all | solution.py:412
  32.9 3.7 %all-to-all-start.1 = ((f32[32,32,256]{2,1,0:T(8,128)}), f32[32,32,256]{2,1,0:T(8,128)S(1)}, u32[]{:S(2)}, u32[]{:S(2)}) async-start(f32[32,32,256]{2,1,0:T(8,128)} %shard_map.106), calls=%async_computation.1 | async-start | bytes 2097152 | tf_op jit(solution)/shard_map/all_to_all | solution.py:413
  36.7 70.0 %shard_map.105 = f32[256,1024]{1,0:T(8,128)} custom-call(bf16[8,256,128]{2,1,0:T(8,128)(2,1)} %copy-done.1, bf16[1024,128,256]{2,1,0:T(8,128)(2,1)} %amp_hbm.1, bf16[256,128,1024]{2,1,0:T(8,128)(2,1)} %factor_hbm.1), custom_call_target="tpu_custom_call" | custom-call | flops 34359738368 | bytes 134217728 | tf_op jit(solution)/shard_map/pallas_call | solution.py:349
  106.8 0.2 fusion
  107.0 0.1 copy.24
  107.2 0.2 broadcast_in_dim.62
  107.3 1.4 %select_add_fusion = f32[2,2,64,1024]{3,2,1,0:T(8,128)S(1)} fusion(f32[2,2,64,1024]{3,2,1,0:T(8,128)} %bitcast.64, f32[2,2,64,1024]{3,2,1,0:T(8,128)S(1)} %broadcast_in_dim.62, pred[1024]{0:T(1024)(128)(4,1)S(1)} %broadcast_bitcast_fusion), kind=kLoop, calls=%fused_computation | loop fusion | flops 524288 | bytes 3146752 | tf_op jit(solution)/shard_map/add | solution.py:423
  108.8 0.3 collective-permute-start.2
  109.1 1.2 slice.3
  110.4 0.1 copy.20
  110.6 0.1 copy.19
  110.8 1.8 %collective-permute-start.3 = (bf16[4,64,128]{2,1,0:T(8,128)(2,1)S(1)}, bf16[4,64,128]{2,1,0:T(8,128)(2,1)S(1)}, u32[]{:S(2)}, u32[]{:S(2)}) collective-permute-start(bf16[4,64,128]{2,1,0:T(8,128)(2,1)S(1)} %get-tuple-element.18), channel_id=1, source_target_pairs={{0,2},{2,4},{4,6},{6,0},{8,10},{10,12},{12,14},{14,8},{16,18},{18,... | collective-permute-start | bytes 196616 | tf_op jit(solution)/shard_map/ppermute | solution.py:394
  112.6 1.5 %collective-permute-start.4 = (bf16[4,64,128]{2,1,0:T(8,128)(2,1)S(1)}, bf16[4,64,128]{2,1,0:T(8,128)(2,1)S(1)}, u32[]{:S(2)}, u32[]{:S(2)}) collective-permute-start(bf16[4,64,128]{2,1,0:T(8,128)(2,1)S(1)} %get-tuple-element.20), channel_id=1, source_target_pairs={{0,4},{2,6},{4,0},{6,2},{8,12},{10,14},{12,8},{14,10},{16,20},{18,... | collective-permute-start | bytes 196616 | tf_op jit(solution)/shard_map/ppermute | solution.py:394
  114.1 1.5 %collective-permute-start.5 = (bf16[4,64,128]{2,1,0:T(8,128)(2,1)S(1)}, bf16[4,64,128]{2,1,0:T(8,128)(2,1)S(1)}, u32[]{:S(2)}, u32[]{:S(2)}) collective-permute-start(bf16[4,64,128]{2,1,0:T(8,128)(2,1)S(1)} %get-tuple-element.19), channel_id=1, source_target_pairs={{0,6},{2,0},{4,2},{6,4},{8,14},{10,8},{12,10},{14,12},{16,22},{18,... | collective-permute-start | bytes 196616 | tf_op jit(solution)/shard_map/ppermute | solution.py:394
  115.5 0.2 select_reduce_fusion.1
  115.7 0.3 collective-permute-done.3
  116.0 1.5 %collective-permute-done.4 = bf16[4,64,128]{2,1,0:T(8,128)(2,1)S(1)} collective-permute-done((bf16[4,64,128]{2,1,0:T(8,128)(2,1)S(1)}, bf16[4,64,128]{2,1,0:T(8,128)(2,1)S(1)}, u32[]{:S(2)}, u32[]{:S(2)}) %collective-permute-start.4) | collective-permute-done | bytes 65568 | tf_op jit(solution)/shard_map/ppermute | solution.py:394
  117.5 0.8 collective-permute-done.5
  118.4 1.5 %collective-permute-start.6 = (bf16[64,128]{1,0:T(8,128)(2,1)S(1)}, bf16[64,128]{1,0:T(8,128)(2,1)S(1)}, u32[]{:S(2)}, u32[]{:S(2)}) collective-permute-start(bf16[64,128]{1,0:T(8,128)(2,1)S(1)} %get-tuple-element.21), channel_id=1, source_target_pairs={{0,8},{2,10},{4,12},{6,14},{8,16},{10,18},{12,20},{14,22},{16,24},... | collective-permute-start | bytes 49160 | tf_op jit(solution)/shard_map/ppermute | solution.py:394
  119.9 2.5 %collective-permute-start.7 = (bf16[64,128]{1,0:T(8,128)(2,1)S(1)}, bf16[64,128]{1,0:T(8,128)(2,1)S(1)}, u32[]{:S(2)}, u32[]{:S(2)}) collective-permute-start(bf16[64,128]{1,0:T(8,128)(2,1)S(1)} %get-tuple-element.23), channel_id=1, source_target_pairs={{0,16},{2,18},{4,20},{6,22},{8,24},{10,26},{12,28},{14,30},{16,0},... | collective-permute-start | bytes 49160 | tf_op jit(solution)/shard_map/ppermute | solution.py:394
  122.4 1.4 %collective-permute-start.8 = (bf16[64,128]{1,0:T(8,128)(2,1)S(1)}, bf16[64,128]{1,0:T(8,128)(2,1)S(1)}, u32[]{:S(2)}, u32[]{:S(2)}) collective-permute-start(bf16[64,128]{1,0:T(8,128)(2,1)S(1)} %get-tuple-element.22), channel_id=1, source_target_pairs={{0,24},{2,26},{4,28},{6,30},{8,0},{10,2},{12,4},{14,6},{16,8},{18,... | collective-permute-start | bytes 49160 | tf_op jit(solution)/shard_map/ppermute | solution.py:394
  123.8 1.4 %dynamic-slice_add_fusion = f32[128]{0:T(128)S(1)} fusion(f32[1024]{0:T(1024)} %param.16, s32[]{:T(128)S(6)} %select_n.165, f32[]{:T(128)} %bitcast.19), kind=kLoop, calls=%fused_computation.38 | loop fusion | flops 128 | bytes 1032 | tf_op jit(solution)/shard_map/add | solution.py:441
  125.2 0.9 collective-permute-done.8
  126.1 0.7 subtract_divide_fusion
  (29 shorter events, 0.6 us)
Async XLA Ops:
  0.6 106.2 %copy-start = (bf16[256,8,128]{2,1,0:T(8,128)(2,1)S(1)}, bf16[256,8,128]{2,1,0:T(8,128)(2,1)}, u32[]{:S(2)}) copy-start(bf16[256,8,128]{2,1,0:T(8,128)(2,1)} %param.15) | copy-start | bytes 1572868
  1.9 10.2 %copy-start.2 = (bf16[32,32,128]{2,1,0:T(8,128)(2,1)}, bf16[32,32,128]{2,1,0:T(8,128)(2,1)S(1)}, u32[]{:S(2)}) copy-start(bf16[32,32,128]{2,1,0:T(8,128)(2,1)S(1)} %pad_maximum_fusion.refs_0_) | copy-start | bytes 786436
  1.9 10.8 %collective-permute-start = (bf16[32,32,128]{2,1,0:T(8,128)(2,1)S(1)}, bf16[32,32,128]{2,1,0:T(8,128)(2,1)S(1)}, u32[]{:S(2)}, u32[]{:S(2)}) collective-permute-start(bf16[32,32,128]{2,1,0:T(8,128)(2,1)S(1)} %pad_maximum_fusion.refs_0_), channel_id=1, source_target_pairs={{0,2},{2,0},{1,3},{3,1},{4,6},{6,4},{5,7},{7,5},{8,10},{10,8},{9,1... | collective-permute-start | bytes 786440 | tf_op jit(solution)/shard_map/ppermute | solution.py:93
  5.6 6.5 %collective-permute-start.1 = (s32[64]{0:T(128)S(1)}, s32[64]{0:T(128)S(1)}, u32[]{:S(2)}, u32[]{:S(2)}) collective-permute-start(s32[64]{0:T(128)S(1)} %multiply_add_fusion), channel_id=1, source_target_pairs={{0,2},{2,0},{1,3},{3,1},{4,6},{6,4},{5,7},{7,5},{8,10},{10,8},{9,1... | collective-permute-start | bytes 776 | tf_op jit(solution)/shard_map/ppermute | solution.py:93
  12.7 6.4 %copy-start.3 = (bf16[32,32,128]{2,1,0:T(8,128)(2,1)}, bf16[32,32,128]{2,1,0:T(8,128)(2,1)S(1)}, u32[]{:S(2)}) copy-start(bf16[32,32,128]{2,1,0:T(8,128)(2,1)S(1)} %collective-permute-done.refs_1_) | copy-start | bytes 786436
  12.7 20.2 %all-to-all-start = ((bf16[8,256,128]{2,1,0:T(8,128)(2,1)}), bf16[8,256,128]{2,1,0:T(8,128)(2,1)S(1)}, u32[]{:S(2)}, u32[]{:S(2)}) async-start(bf16[8,256,128]{2,1,0:T(8,128)(2,1)} %shard_map.104), calls=%async_computation | async-start | bytes 1048576 | tf_op jit(solution)/shard_map/all_to_all | solution.py:412
  32.9 3.7 %copy-start.1 = (bf16[8,256,128]{2,1,0:T(8,128)(2,1)}, bf16[8,256,128]{2,1,0:T(8,128)(2,1)S(1)}, u32[]{:S(2)}) copy-start(bf16[8,256,128]{2,1,0:T(8,128)(2,1)S(1)} %all-to-all-done.row_ref) | copy-start | bytes 1572868
  32.9 73.8 %all-to-all-start.1 = ((f32[32,32,256]{2,1,0:T(8,128)}), f32[32,32,256]{2,1,0:T(8,128)S(1)}, u32[]{:S(2)}, u32[]{:S(2)}) async-start(f32[32,32,256]{2,1,0:T(8,128)} %shard_map.106), calls=%async_computation.1 | async-start | bytes 2097152 | tf_op jit(solution)/shard_map/all_to_all | solution.py:413
  36.6 78.9 %copy-start.4 = (f32[128]{0:T(128)S(1)}, f32[128]{0:T(128)}, u32[]{:S(2)}) copy-start(f32[128]{0:T(128)} %param.17) | copy-start | bytes 1540
  108.8 1.6 %collective-permute-start.2 = (bf16[2,64,1024]{2,1,0:T(8,128)(2,1)S(1)}, bf16[2,64,1024]{2,1,0:T(8,128)(2,1)S(1)}, u32[]{:S(2)}, u32[]{:S(2)}) collective-permute-start(bf16[2,64,1024]{2,1,0:T(8,128)(2,1)S(1)} %fusion.2), channel_id=1, source_target_pairs={{0,1},{1,0},{2,3},{3,2},{4,5},{5,4},{6,7},{7,6},{8,9},{9,8},{10,11... | collective-permute-start | bytes 786440 | tf_op jit(solution)/shard_map/ppermute | solution.py:394
  110.8 5.2 %collective-permute-start.3 = (bf16[4,64,128]{2,1,0:T(8,128)(2,1)S(1)}, bf16[4,64,128]{2,1,0:T(8,128)(2,1)S(1)}, u32[]{:S(2)}, u32[]{:S(2)}) collective-permute-start(bf16[4,64,128]{2,1,0:T(8,128)(2,1)S(1)} %get-tuple-element.18), channel_id=1, source_target_pairs={{0,2},{2,4},{4,6},{6,0},{8,10},{10,12},{12,14},{14,8},{16,18},{18,... | collective-permute-start | bytes 196616 | tf_op jit(solution)/shard_map/ppermute | solution.py:394
  112.6 4.9 %collective-permute-start.4 = (bf16[4,64,128]{2,1,0:T(8,128)(2,1)S(1)}, bf16[4,64,128]{2,1,0:T(8,128)(2,1)S(1)}, u32[]{:S(2)}, u32[]{:S(2)}) collective-permute-start(bf16[4,64,128]{2,1,0:T(8,128)(2,1)S(1)} %get-tuple-element.20), channel_id=1, source_target_pairs={{0,4},{2,6},{4,0},{6,2},{8,12},{10,14},{12,8},{14,10},{16,20},{18,... | collective-permute-start | bytes 196616 | tf_op jit(solution)/shard_map/ppermute | solution.py:394
  114.1 4.3 %collective-permute-start.5 = (bf16[4,64,128]{2,1,0:T(8,128)(2,1)S(1)}, bf16[4,64,128]{2,1,0:T(8,128)(2,1)S(1)}, u32[]{:S(2)}, u32[]{:S(2)}) collective-permute-start(bf16[4,64,128]{2,1,0:T(8,128)(2,1)S(1)} %get-tuple-element.19), channel_id=1, source_target_pairs={{0,6},{2,0},{4,2},{6,4},{8,14},{10,8},{12,10},{14,12},{16,22},{18,... | collective-permute-start | bytes 196616 | tf_op jit(solution)/shard_map/ppermute | solution.py:394
  118.4 6.8 %collective-permute-start.6 = (bf16[64,128]{1,0:T(8,128)(2,1)S(1)}, bf16[64,128]{1,0:T(8,128)(2,1)S(1)}, u32[]{:S(2)}, u32[]{:S(2)}) collective-permute-start(bf16[64,128]{1,0:T(8,128)(2,1)S(1)} %get-tuple-element.21), channel_id=1, source_target_pairs={{0,8},{2,10},{4,12},{6,14},{8,16},{10,18},{12,20},{14,22},{16,24},... | collective-permute-start | bytes 49160 | tf_op jit(solution)/shard_map/ppermute | solution.py:394
  119.9 5.3 %collective-permute-start.7 = (bf16[64,128]{1,0:T(8,128)(2,1)S(1)}, bf16[64,128]{1,0:T(8,128)(2,1)S(1)}, u32[]{:S(2)}, u32[]{:S(2)}) collective-permute-start(bf16[64,128]{1,0:T(8,128)(2,1)S(1)} %get-tuple-element.23), channel_id=1, source_target_pairs={{0,16},{2,18},{4,20},{6,22},{8,24},{10,26},{12,28},{14,30},{16,0},... | collective-permute-start | bytes 49160 | tf_op jit(solution)/shard_map/ppermute | solution.py:394
  122.4 3.7 %collective-permute-start.8 = (bf16[64,128]{1,0:T(8,128)(2,1)S(1)}, bf16[64,128]{1,0:T(8,128)(2,1)S(1)}, u32[]{:S(2)}, u32[]{:S(2)}) collective-permute-start(bf16[64,128]{1,0:T(8,128)(2,1)S(1)} %get-tuple-element.22), channel_id=1, source_target_pairs={{0,24},{2,26},{4,28},{6,30},{8,0},{10,2},{12,4},{14,6},{16,8},{18,... | collective-permute-start | bytes 49160 | tf_op jit(solution)/shard_map/ppermute | solution.py:394

commit v6 on v5

--- a/solution.py
+++ b/solution.py
@@ -242,8 +242,8 @@
     _, virtuals, deep, pairs = amp_buf.shape
     count, chol, _ = row_ref.shape
     square = deep * deep
-    step, steps = pl.program_id(0), pl.num_programs(0)
-    slot = lax.rem(step, 2)
+    step, blocks = pl.program_id(0), pl.num_programs(0) - 1
+    slot, before = lax.rem(step, 2), lax.rem(step + 1, 2)
 
     def arriving(hbm, buf, sem, step, side):
         size = buf.shape[1] // sides
@@ -253,21 +253,22 @@
             hbm.at[rows, block], buf.at[slot, rows], sem.at[slot, side]
         )
 
-    def start(step):
+    @pl.when(step == 0)
+    def _():
         for q in range(sides):
             arriving(amp_hbm, amp_buf, amp_sem, step, q).start()
+        out_ref[...] = jnp.zeros_like(out_ref)
+        swap[...] = swap_matrix(deep)
+
+    @pl.when(step + 1 < blocks)
+    def _():
+        for q in range(sides):
+            arriving(amp_hbm, amp_buf, amp_sem, step + 1, q).start()
+
+    @pl.when(step < blocks)
+    def _():
         for q in range(sides):
             arriving(factor_hbm, factor_buf, factor_sem, step, q).start()
-
-    @pl.when(step == 0)
-    def _():
-        start(step)
-        out_ref[...] = jnp.zeros_like(out_ref)
-        swap[...] = swap_matrix(deep)
-
-    @pl.when(step + 1 < steps)
-    def _():
-        start(step + 1)
 
     def later(jobs):
         store = None
@@ -278,7 +279,7 @@
             store = after
         store()
 
-    def reorder(first):
+    def by_matmul(first):
         rows = [slice(first + r * deep, first + (r + 1) * deep) for r in range(2)]
         block = [amp_buf[slot, r].reshape(square, pairs) for r in rows]
         block = jnp.dot(
@@ -291,12 +292,64 @@
 
         return store
 
-    for q in range(sides):
-        arriving(amp_hbm, amp_buf, amp_sem, step, q).wait()
-        size = virtuals // sides
-        later(
-            functools.partial(reorder, k) for k in range(q * size, (q + 1) * size, 2 * deep)
+    sublane = lax.broadcasted_iota(jnp.int32, (deep // 8, 8, LANES), 1)
+
+    def by_shuffle(first, h):
+        rows, lane = slice(first, first + deep), slice(h * LANES, (h + 1) * LANES)
+        block = amp_buf[slot, rows, :, lane].astype(f32).reshape(deep // 8, 8, deep, LANES)
+        result = []
+        for o in range(0, deep, 8):
+            v = [block[:, a, o : o + 8] for a in range(8)]
+            for k in (4, 2, 1):
+                keep = (sublane & k) == 0
+                for a in range(8):
+                    if not a & k:
+                        x, y = v[a], v[a + k]
+                        v[a] = jnp.where(keep, x, pltpu.roll(y, k, 1))
+                        v[a + k] = jnp.where(keep, pltpu.roll(x, 8 - k, 1), y)
+            result += [x.reshape(deep, LANES).astype(bf16) for x in v]
+
+        def store():
+            for d in range(deep):
+                turned[d, rows, lane] = result[d]
+
+        return store
+
+    def ladder(side, first):
+        size, column = chol // sides, slice(first, first + 256)
+        block = factor_buf[before, side * size : (side + 1) * size, :, column]
+        block = jnp.dot(
+            flat[:, side * size * deep : (side + 1) * size * deep],
+            block.reshape(size * deep, 256),
+            preferred_element_type=f32,
         )
+
+        def store():
+            out_ref[:, column] += block
+
+        return store
+
+    def reorder_jobs(side):
+        size, unit = virtuals // sides, 2 * deep
+        firsts = range(side * size, (side + 1) * size, unit)
+        shuffles = [
+            functools.partial(by_shuffle, k + r, h)
+            for i, k in enumerate(firsts)
+            if i % 4
+            for r in range(0, unit, deep)
+            for h in range(pairs // LANES)
+        ]
+        matmuls = [functools.partial(by_matmul, k) for k in firsts[::4]]
+        share = len(shuffles) // 4
+        for i in range(4):
+            yield matmuls[i // 2 : i // 2 + 1] * (1 - i % 2) + shuffles[i * share : (i + 1) * share]
+
+    def ladder_jobs(side):
+        width = out_ref.shape[1] // 4
+        for i in range(4):
+            yield [
+                functools.partial(ladder, side, n) for n in range(i * width, (i + 1) * width, 256)
+            ]
 
     row = jnp.concatenate([row_ref[k] for k in range(count)], axis=1)
 
@@ -308,8 +361,6 @@
             half[d], half[d + 1] = block[:, :pairs], block[:, pairs:]
 
         return store
-
-    later(functools.partial(halves, d) for d in range(0, deep, 2))
 
     def flatten(first):
         parts = range(first, first + 4 * deep, deep)
@@ -324,21 +375,32 @@
 
         return store
 
-    later(functools.partial(flatten, k) for k in range(0, chol, 4 * deep))
-    for q in range(sides):
-        arriving(factor_hbm, factor_buf, factor_sem, step, q).wait()
-    columns = 512
-
-    def ladder(first):
-        block = factor_buf[slot, :, :, first : first + columns].reshape(chol * deep, columns)
-        block = jnp.dot(flat[...], block, preferred_element_type=f32)
-
-        def store():
-            out_ref[:, first : first + columns] += block
-
-        return store
-
-    later(functools.partial(ladder, n) for n in range(0, out_ref.shape[1], columns))
+    def stages(early, late):
+        if late:
+            for q in range(sides):
+                arriving(factor_hbm, factor_buf, factor_sem, step - 1, q).wait()
+        for q in range(sides):
+            if early:
+                arriving(amp_hbm, amp_buf, amp_sem, step, q).wait()
+            jobs = []
+            for one, other in zip(ladder_jobs(q), reorder_jobs(q)):
+                jobs += one * late + other * early
+            later(job for job in jobs)
+        if early:
+            later(functools.partial(halves, d) for d in range(0, deep, 2))
+            later(functools.partial(flatten, k) for k in range(0, chol, 4 * deep))
+
+    @pl.when(step == 0)
+    def _():
+        stages(True, False)
+
+    @pl.when((step > 0) & (step < blocks))
+    def _():
+        stages(True, True)
+
+    @pl.when(step == blocks)
+    def _():
+        stages(False, True)
 
 
 def ladder_partial(row, ladder_amp, vv_factor):
@@ -348,7 +410,7 @@
     whole = pl.BlockSpec(memory_space=pl.ANY)
     return pl.pallas_call(
         functools.partial(ladder_kernel, sides),
-        grid=(slab // deep,),
+        grid=(slab // deep + 1,),
         in_specs=[pl.BlockSpec(memory_space=pltpu.VMEM), whole, whole],
         out_specs=pl.BlockSpec((pairs, virtuals), lambda i: (0, 0)),
         out_shape=jax.ShapeDtypeStruct((pairs, virtuals), f32),
@@ -402,7 +464,7 @@
     pairs = ladder_amp.shape[2]
     slots, _, width = ov_slots.shape
     n_vir, n_ph, n_vec = (lax.axis_size(a) for a in ("vir", "ph", "vec"))
-    fits = slab == LANES and virtuals % 512 == 0 and pairs == 2 * LANES and chol % LANES == 0 and slots % 32 == 0
+    fits = slab == LANES and virtuals % 1024 == 0 and pairs == 2 * LANES and chol % LANES == 0 and slots % 32 == 0
     if not fits or 256 % width or cycle_amp.shape[0] % 2 or n_vir * n_ph % 4:
         return plain(
             vv_factor, ladder_amp, cycle_amp, ov_slots, owner_of, slot_of, ov_pairs, eps_vir, eps_occ

time: 127 us -> 139 us (1.094)
  Pallas kernels: 86.3 us -> 98 us
    pallas_call x1, Pallas kernels: 70 us -> 81.8 us  [ladder_partial(): pl.pallas_call(functools.partial(ladder_kernel, sides), grid=(slab // dee...]
  transfers between devices with their start and end apart: 11 -> 11, of which waited for: 6 -> 6; matrix products, arithmetic and copies ran while one was open for 3% -> 3% of each run, Pallas kernels for 68% -> 71%
where the time goes in v6:
time: 139 us
  Pallas kernels  98 us (71%)
  starting transfers between devices  23.5 us (17%)
  waiting for transfers between devices  7.67 us (6%)
  other arithmetic  5.32 us (4%)
  local copies, waits for them, and re-layouts  3.05 us (2%)
    pallas_call x1, Pallas kernels, ladder_partial(): pl.pallas_call(functools.partial(ladder_kernel, sides), grid=(slab // dee...  81.8 us
    ppermute x7, starting transfers between devices, scatter_sum(): total = total + lax.ppermute(piece, axes, pairs).astype(f32)  10.4 us
    pallas_call x1, Pallas kernels, cycle_partial(): pl.pallas_call(functools.partial(cycle_kernel, shares, len(amps)), grid=(...  9.84 us
    pallas_call x1, Pallas kernels, own_row(): pl.pallas_call(row_kernel, grid=(chol // LANES, steps), in_specs=[side(q)...  6.42 us
    all_to_all x1, starting transfers between devices, local(): row = lax.all_to_all(row, 'vir', 0, 0)  6.28 us
    all_to_all x1, waiting for transfers between devices, local(): row = lax.all_to_all(row, 'vir', 0, 0)  4.05 us
    all_to_all x1, starting transfers between devices, local(): lax.all_to_all(cycle_partial(amps, codes, ov_slots), ('vir', 'ph', 'vec')...  3.68 us
    ppermute x7, waiting for transfers between devices, scatter_sum(): total = total + lax.ppermute(piece, axes, pairs).astype(f32)  3.62 us
  transfers between devices with their start and end apart: 11, of which 6 were waited for; matrix products, arithmetic and copies ran while one was open for 3% of the time, Pallas kernels for 71%

profile of v6, /device:TPU:0, one launch (start us, length us, event | category | flops | bytes accessed | tf_op | source)
XLA Modules:
  0.0 138.5 jit_solution(11723890470468658939)
XLA Ops:
  0.6 1.1 fusion.14
  1.8 0.1 pad_maximum_fusion.refs_0_
  1.9 3.0 %collective-permute-start = (bf16[32,32,128]{2,1,0:T(8,128)(2,1)S(1)}, bf16[32,32,128]{2,1,0:T(8,128)(2,1)S(1)}, u32[]{:S(2)}, u32[]{:S(2)}) collective-permute-start(bf16[32,32,128]{2,1,0:T(8,128)(2,1)S(1)} %pad_maximum_fusion.refs_0_), channel_id=1, source_target_pairs={{0,2},{2,0},{1,3},{3,1},{4,6},{6,4},{5,7},{7,5},{8,10},{10,8},{9,1... | collective-permute-start | bytes 786440 | tf_op jit(solution)/shard_map/ppermute | solution.py:93
  5.0 0.7 multiply_add_fusion
  5.7 6.4 %shard_map.104 = bf16[8,256,128]{2,1,0:T(8,128)(2,1)} custom-call(bf16[256,128,1024]{2,1,0:T(8,128)(2,1)} %factor_hbm.1, bf16[256,128,1024]{2,1,0:T(8,128)(2,1)} %factor_hbm.1, bf16[256,128,1024]{2,1,0:T(8,128)(2,1)} %factor_hbm.1, bf16[256,128,1024]{2,1,0:T(8,128)(2,1)} %factor_hbm.1), custom_call_target="tpu_custom_call" | custom-call | flops 8388608 | bytes 8388608 | tf_op jit(solution)/shard_map/pallas_call | solution.py:134
  12.1 0.6 pad_add_fusion.code_ref
  12.7 6.3 %all-to-all-start = ((bf16[8,256,128]{2,1,0:T(8,128)(2,1)}), bf16[8,256,128]{2,1,0:T(8,128)(2,1)S(1)}, u32[]{:S(2)}, u32[]{:S(2)}) async-start(bf16[8,256,128]{2,1,0:T(8,128)(2,1)} %shard_map.104), calls=%async_computation | async-start | bytes 1048576 | tf_op jit(solution)/shard_map/all_to_all | solution.py:474
  19.1 9.8 %shard_map.106 = f32[32,32,256]{2,1,0:T(8,128)} custom-call(s32[1]{0:T(128)} %bitcast.2.place_ref, s32[128]{0:T(128)} %pad_add_fusion.code_ref, bf16[32,32,128]{2,1,0:T(8,128)(2,1)} %copy-done.2, bf16[32,32,128]{2,1,0:T(8,128)(2,1)} %copy-done.3, bf16[128,64,1024]{2,1,0:T(8,128)(2,1)} %bitcast.60, bf16[128,64,1024]{2,1,0:T(8,128)(2,1)} %bitcast.61, ...), custom_call_target="tpu_custom_call" | custom-call | flops 536870912 | bytes 16777216 | tf_op jit(solution)/shard_map/pallas_call | solution.py:211
  28.9 4.0 %all-to-all-done.row_ref = bf16[8,256,128]{2,1,0:T(8,128)(2,1)S(1)} async-done(((bf16[8,256,128]{2,1,0:T(8,128)(2,1)}), bf16[8,256,128]{2,1,0:T(8,128)(2,1)S(1)}, u32[]{:S(2)}, u32[]{:S(2)}) %all-to-all-start) | async-done | bytes 524320 | tf_op jit(solution)/shard_map/all_to_all | solution.py:474
  32.9 3.7 %all-to-all-start.1 = ((f32[32,32,256]{2,1,0:T(8,128)}), f32[32,32,256]{2,1,0:T(8,128)S(1)}, u32[]{:S(2)}, u32[]{:S(2)}) async-start(f32[32,32,256]{2,1,0:T(8,128)} %shard_map.106), calls=%async_computation.1 | async-start | bytes 2097152 | tf_op jit(solution)/shard_map/all_to_all | solution.py:475
  36.7 81.8 %shard_map.105 = f32[256,1024]{1,0:T(8,128)} custom-call(bf16[8,256,128]{2,1,0:T(8,128)(2,1)} %copy-done.1, bf16[1024,128,256]{2,1,0:T(8,128)(2,1)} %amp_hbm.1, bf16[256,128,1024]{2,1,0:T(8,128)(2,1)} %factor_hbm.1), custom_call_target="tpu_custom_call" | custom-call | flops 34359738368 | bytes 134217728 | tf_op jit(solution)/shard_map/pallas_call | solution.py:411
  118.5 0.2 fusion
  118.7 0.1 copy.24
  118.9 0.2 broadcast_in_dim.62
  119.1 1.4 %select_add_fusion = f32[2,2,64,1024]{3,2,1,0:T(8,128)S(1)} fusion(f32[2,2,64,1024]{3,2,1,0:T(8,128)} %bitcast.64, f32[2,2,64,1024]{3,2,1,0:T(8,128)S(1)} %broadcast_in_dim.62, pred[1024]{0:T(1024)(128)(4,1)S(1)} %broadcast_bitcast_fusion), kind=kLoop, calls=%fused_computation | loop fusion | flops 524288 | bytes 3146752 | tf_op jit(solution)/shard_map/add | solution.py:485
  120.5 0.3 collective-permute-start.2
  120.8 1.2 slice.3
  122.2 0.1 copy.20
  122.3 0.1 copy.19
  122.5 1.8 %collective-permute-start.3 = (bf16[4,64,128]{2,1,0:T(8,128)(2,1)S(1)}, bf16[4,64,128]{2,1,0:T(8,128)(2,1)S(1)}, u32[]{:S(2)}, u32[]{:S(2)}) collective-permute-start(bf16[4,64,128]{2,1,0:T(8,128)(2,1)S(1)} %get-tuple-element.18), channel_id=1, source_target_pairs={{0,2},{2,4},{4,6},{6,0},{8,10},{10,12},{12,14},{14,8},{16,18},{18,... | collective-permute-start | bytes 196616 | tf_op jit(solution)/shard_map/ppermute | solution.py:456
  124.3 1.5 %collective-permute-start.4 = (bf16[4,64,128]{2,1,0:T(8,128)(2,1)S(1)}, bf16[4,64,128]{2,1,0:T(8,128)(2,1)S(1)}, u32[]{:S(2)}, u32[]{:S(2)}) collective-permute-start(bf16[4,64,128]{2,1,0:T(8,128)(2,1)S(1)} %get-tuple-element.20), channel_id=1, source_target_pairs={{0,4},{2,6},{4,0},{6,2},{8,12},{10,14},{12,8},{14,10},{16,20},{18,... | collective-permute-start | bytes 196616 | tf_op jit(solution)/shard_map/ppermute | solution.py:456
  125.8 1.5 %collective-permute-start.5 = (bf16[4,64,128]{2,1,0:T(8,128)(2,1)S(1)}, bf16[4,64,128]{2,1,0:T(8,128)(2,1)S(1)}, u32[]{:S(2)}, u32[]{:S(2)}) collective-permute-start(bf16[4,64,128]{2,1,0:T(8,128)(2,1)S(1)} %get-tuple-element.19), channel_id=1, source_target_pairs={{0,6},{2,0},{4,2},{6,4},{8,14},{10,8},{12,10},{14,12},{16,22},{18,... | collective-permute-start | bytes 196616 | tf_op jit(solution)/shard_map/ppermute | solution.py:456
  127.3 0.2 select_reduce_fusion.1
  127.4 0.3 collective-permute-done.3
  127.7 1.5 %collective-permute-done.4 = bf16[4,64,128]{2,1,0:T(8,128)(2,1)S(1)} collective-permute-done((bf16[4,64,128]{2,1,0:T(8,128)(2,1)S(1)}, bf16[4,64,128]{2,1,0:T(8,128)(2,1)S(1)}, u32[]{:S(2)}, u32[]{:S(2)}) %collective-permute-start.4) | collective-permute-done | bytes 65568 | tf_op jit(solution)/shard_map/ppermute | solution.py:456
  129.2 0.8 collective-permute-done.5
  130.1 1.5 %collective-permute-start.6 = (bf16[64,128]{1,0:T(8,128)(2,1)S(1)}, bf16[64,128]{1,0:T(8,128)(2,1)S(1)}, u32[]{:S(2)}, u32[]{:S(2)}) collective-permute-start(bf16[64,128]{1,0:T(8,128)(2,1)S(1)} %get-tuple-element.21), channel_id=1, source_target_pairs={{0,8},{2,10},{4,12},{6,14},{8,16},{10,18},{12,20},{14,22},{16,24},... | collective-permute-start | bytes 49160 | tf_op jit(solution)/shard_map/ppermute | solution.py:456
  131.6 2.5 %collective-permute-start.7 = (bf16[64,128]{1,0:T(8,128)(2,1)S(1)}, bf16[64,128]{1,0:T(8,128)(2,1)S(1)}, u32[]{:S(2)}, u32[]{:S(2)}) collective-permute-start(bf16[64,128]{1,0:T(8,128)(2,1)S(1)} %get-tuple-element.23), channel_id=1, source_target_pairs={{0,16},{2,18},{4,20},{6,22},{8,24},{10,26},{12,28},{14,30},{16,0},... | collective-permute-start | bytes 49160 | tf_op jit(solution)/shard_map/ppermute | solution.py:456
  134.1 1.4 %collective-permute-start.8 = (bf16[64,128]{1,0:T(8,128)(2,1)S(1)}, bf16[64,128]{1,0:T(8,128)(2,1)S(1)}, u32[]{:S(2)}, u32[]{:S(2)}) collective-permute-start(bf16[64,128]{1,0:T(8,128)(2,1)S(1)} %get-tuple-element.22), channel_id=1, source_target_pairs={{0,24},{2,26},{4,28},{6,30},{8,0},{10,2},{12,4},{14,6},{16,8},{18,... | collective-permute-start | bytes 49160 | tf_op jit(solution)/shard_map/ppermute | solution.py:456
  135.5 1.4 %dynamic-slice_add_fusion = f32[128]{0:T(128)S(1)} fusion(f32[1024]{0:T(1024)} %param.16, s32[]{:T(128)S(6)} %select_n.165, f32[]{:T(128)} %bitcast.19), kind=kLoop, calls=%fused_computation.38 | loop fusion | flops 128 | bytes 1032 | tf_op jit(solution)/shard_map/add | solution.py:503
  136.9 0.9 collective-permute-done.8
  137.8 0.7 subtract_divide_fusion
  (29 shorter events, 0.6 us)
Async XLA Ops:
  0.6 117.9 %copy-start = (bf16[256,8,128]{2,1,0:T(8,128)(2,1)S(1)}, bf16[256,8,128]{2,1,0:T(8,128)(2,1)}, u32[]{:S(2)}) copy-start(bf16[256,8,128]{2,1,0:T(8,128)(2,1)} %param.15) | copy-start | bytes 1572868
  1.9 10.2 %copy-start.2 = (bf16[32,32,128]{2,1,0:T(8,128)(2,1)}, bf16[32,32,128]{2,1,0:T(8,128)(2,1)S(1)}, u32[]{:S(2)}) copy-start(bf16[32,32,128]{2,1,0:T(8,128)(2,1)S(1)} %pad_maximum_fusion.refs_0_) | copy-start | bytes 786436
  1.9 10.8 %collective-permute-start = (bf16[32,32,128]{2,1,0:T(8,128)(2,1)S(1)}, bf16[32,32,128]{2,1,0:T(8,128)(2,1)S(1)}, u32[]{:S(2)}, u32[]{:S(2)}) collective-permute-start(bf16[32,32,128]{2,1,0:T(8,128)(2,1)S(1)} %pad_maximum_fusion.refs_0_), channel_id=1, source_target_pairs={{0,2},{2,0},{1,3},{3,1},{4,6},{6,4},{5,7},{7,5},{8,10},{10,8},{9,1... | collective-permute-start | bytes 786440 | tf_op jit(solution)/shard_map/ppermute | solution.py:93
  5.6 6.5 %collective-permute-start.1 = (s32[64]{0:T(128)S(1)}, s32[64]{0:T(128)S(1)}, u32[]{:S(2)}, u32[]{:S(2)}) collective-permute-start(s32[64]{0:T(128)S(1)} %multiply_add_fusion), channel_id=1, source_target_pairs={{0,2},{2,0},{1,3},{3,1},{4,6},{6,4},{5,7},{7,5},{8,10},{10,8},{9,1... | collective-permute-start | bytes 776 | tf_op jit(solution)/shard_map/ppermute | solution.py:93
  12.7 6.4 %copy-start.3 = (bf16[32,32,128]{2,1,0:T(8,128)(2,1)}, bf16[32,32,128]{2,1,0:T(8,128)(2,1)S(1)}, u32[]{:S(2)}) copy-start(bf16[32,32,128]{2,1,0:T(8,128)(2,1)S(1)} %collective-permute-done.refs_1_) | copy-start | bytes 786436
  12.7 20.2 %all-to-all-start = ((bf16[8,256,128]{2,1,0:T(8,128)(2,1)}), bf16[8,256,128]{2,1,0:T(8,128)(2,1)S(1)}, u32[]{:S(2)}, u32[]{:S(2)}) async-start(bf16[8,256,128]{2,1,0:T(8,128)(2,1)} %shard_map.104), calls=%async_computation | async-start | bytes 1048576 | tf_op jit(solution)/shard_map/all_to_all | solution.py:474
  32.9 3.7 %copy-start.1 = (bf16[8,256,128]{2,1,0:T(8,128)(2,1)}, bf16[8,256,128]{2,1,0:T(8,128)(2,1)S(1)}, u32[]{:S(2)}) copy-start(bf16[8,256,128]{2,1,0:T(8,128)(2,1)S(1)} %all-to-all-done.row_ref) | copy-start | bytes 1572868
  32.9 85.5 %all-to-all-start.1 = ((f32[32,32,256]{2,1,0:T(8,128)}), f32[32,32,256]{2,1,0:T(8,128)S(1)}, u32[]{:S(2)}, u32[]{:S(2)}) async-start(f32[32,32,256]{2,1,0:T(8,128)} %shard_map.106), calls=%async_computation.1 | async-start | bytes 2097152 | tf_op jit(solution)/shard_map/all_to_all | solution.py:475
  36.6 90.6 %copy-start.4 = (f32[128]{0:T(128)S(1)}, f32[128]{0:T(128)}, u32[]{:S(2)}) copy-start(f32[128]{0:T(128)} %param.17) | copy-start | bytes 1540
  120.5 1.6 %collective-permute-start.2 = (bf16[2,64,1024]{2,1,0:T(8,128)(2,1)S(1)}, bf16[2,64,1024]{2,1,0:T(8,128)(2,1)S(1)}, u32[]{:S(2)}, u32[]{:S(2)}) collective-permute-start(bf16[2,64,1024]{2,1,0:T(8,128)(2,1)S(1)} %fusion.2), channel_id=1, source_target_pairs={{0,1},{1,0},{2,3},{3,2},{4,5},{5,4},{6,7},{7,6},{8,9},{9,8},{10,11... | collective-permute-start | bytes 786440 | tf_op jit(solution)/shard_map/ppermute | solution.py:456
  122.5 5.2 %collective-permute-start.3 = (bf16[4,64,128]{2,1,0:T(8,128)(2,1)S(1)}, bf16[4,64,128]{2,1,0:T(8,128)(2,1)S(1)}, u32[]{:S(2)}, u32[]{:S(2)}) collective-permute-start(bf16[4,64,128]{2,1,0:T(8,128)(2,1)S(1)} %get-tuple-element.18), channel_id=1, source_target_pairs={{0,2},{2,4},{4,6},{6,0},{8,10},{10,12},{12,14},{14,8},{16,18},{18,... | collective-permute-start | bytes 196616 | tf_op jit(solution)/shard_map/ppermute | solution.py:456
  124.3 4.9 %collective-permute-start.4 = (bf16[4,64,128]{2,1,0:T(8,128)(2,1)S(1)}, bf16[4,64,128]{2,1,0:T(8,128)(2,1)S(1)}, u32[]{:S(2)}, u32[]{:S(2)}) collective-permute-start(bf16[4,64,128]{2,1,0:T(8,128)(2,1)S(1)} %get-tuple-element.20), channel_id=1, source_target_pairs={{0,4},{2,6},{4,0},{6,2},{8,12},{10,14},{12,8},{14,10},{16,20},{18,... | collective-permute-start | bytes 196616 | tf_op jit(solution)/shard_map/ppermute | solution.py:456
  125.8 4.3 %collective-permute-start.5 = (bf16[4,64,128]{2,1,0:T(8,128)(2,1)S(1)}, bf16[4,64,128]{2,1,0:T(8,128)(2,1)S(1)}, u32[]{:S(2)}, u32[]{:S(2)}) collective-permute-start(bf16[4,64,128]{2,1,0:T(8,128)(2,1)S(1)} %get-tuple-element.19), channel_id=1, source_target_pairs={{0,6},{2,0},{4,2},{6,4},{8,14},{10,8},{12,10},{14,12},{16,22},{18,... | collective-permute-start | bytes 196616 | tf_op jit(solution)/shard_map/ppermute | solution.py:456
  130.1 6.8 %collective-permute-start.6 = (bf16[64,128]{1,0:T(8,128)(2,1)S(1)}, bf16[64,128]{1,0:T(8,128)(2,1)S(1)}, u32[]{:S(2)}, u32[]{:S(2)}) collective-permute-start(bf16[64,128]{1,0:T(8,128)(2,1)S(1)} %get-tuple-element.21), channel_id=1, source_target_pairs={{0,8},{2,10},{4,12},{6,14},{8,16},{10,18},{12,20},{14,22},{16,24},... | collective-permute-start | bytes 49160 | tf_op jit(solution)/shard_map/ppermute | solution.py:456
  131.6 5.3 %collective-permute-start.7 = (bf16[64,128]{1,0:T(8,128)(2,1)S(1)}, bf16[64,128]{1,0:T(8,128)(2,1)S(1)}, u32[]{:S(2)}, u32[]{:S(2)}) collective-permute-start(bf16[64,128]{1,0:T(8,128)(2,1)S(1)} %get-tuple-element.23), channel_id=1, source_target_pairs={{0,16},{2,18},{4,20},{6,22},{8,24},{10,26},{12,28},{14,30},{16,0},... | collective-permute-start | bytes 49160 | tf_op jit(solution)/shard_map/ppermute | solution.py:456
  134.1 3.7 %collective-permute-start.8 = (bf16[64,128]{1,0:T(8,128)(2,1)S(1)}, bf16[64,128]{1,0:T(8,128)(2,1)S(1)}, u32[]{:S(2)}, u32[]{:S(2)}) collective-permute-start(bf16[64,128]{1,0:T(8,128)(2,1)S(1)} %get-tuple-element.22), channel_id=1, source_target_pairs={{0,24},{2,26},{4,28},{6,30},{8,0},{10,2},{12,4},{14,6},{16,8},{18,... | collective-permute-start | bytes 49160 | tf_op jit(solution)/shard_map/ppermute | solution.py:456

commit v7 on v5

--- a/solution.py
+++ b/solution.py
@@ -279,7 +279,7 @@
         store()
 
     def reorder(first):
-        rows = [slice(first + r * deep, first + (r + 1) * deep) for r in range(2)]
+        rows = [slice(first + r * deep, first + (r + 1) * deep) for r in range(4)]
         block = [amp_buf[slot, r].reshape(square, pairs) for r in rows]
         block = jnp.dot(
             swap[...], jnp.concatenate(block, axis=1), preferred_element_type=f32
@@ -295,24 +295,25 @@
         arriving(amp_hbm, amp_buf, amp_sem, step, q).wait()
         size = virtuals // sides
         later(
-            functools.partial(reorder, k) for k in range(q * size, (q + 1) * size, 2 * deep)
+            functools.partial(reorder, k) for k in range(q * size, (q + 1) * size, 4 * deep)
         )
 
     row = jnp.concatenate([row_ref[k] for k in range(count)], axis=1)
 
     def halves(d):
-        block = jnp.concatenate([turned[d], turned[d + 1]], axis=1)
+        block = jnp.concatenate([turned[d + r] for r in range(4)], axis=1)
         block = jnp.dot(row, block, preferred_element_type=f32).astype(bf16)
 
         def store():
-            half[d], half[d + 1] = block[:, :pairs], block[:, pairs:]
+            for r in range(4):
+                half[d + r] = block[:, r * pairs : (r + 1) * pairs]
 
         return store
 
-    later(functools.partial(halves, d) for d in range(0, deep, 2))
+    later(functools.partial(halves, d) for d in range(0, deep, 4))
 
     def flatten(first):
-        parts = range(first, first + 4 * deep, deep)
+        parts = range(first, first + chol, deep)
         block = [half[:, k : k + deep, :].reshape(square, pairs).T for k in parts]
         block = jnp.dot(
             jnp.concatenate(block, axis=0), swap[...], preferred_element_type=f32
@@ -324,10 +325,10 @@
 
         return store
 
-    later(functools.partial(flatten, k) for k in range(0, chol, 4 * deep))
+    flatten(0)()
     for q in range(sides):
         arriving(factor_hbm, factor_buf, factor_sem, step, q).wait()
-    columns = 512
+    columns = out_ref.shape[1]
 
     def ladder(first):
         block = factor_buf[slot, :, :, first : first + columns].reshape(chol * deep, columns)
@@ -419,11 +420,14 @@
     ladder = ladder_partial(row, ladder_amp, vv_factor)
     vir = lax.axis_index("vir")
     share = pairs // (n_ph * n_vec)
-    own = jnp.arange(n_vir, dtype=jnp.int32)[None, :, None] == vir
-    total = ladder.reshape(pairs, n_vir, slab) + jnp.where(own, cycle_term[:, None, :], 0.0)
-    total = total.reshape(n_ph, n_vec, share, virtuals)
+    own = jnp.arange(n_vir, dtype=jnp.int32)[:, None] == vir
+    total = ladder.reshape(n_ph, n_vec, share, virtuals)
     total = scatter_sum(jnp.swapaxes(total, 0, 1), "vec")
-    total = total.reshape(n_ph, share, n_vir, slab).transpose(2, 0, 1, 3)
+    cycle_term = cycle_term.reshape(n_ph, n_vec, share, slab)
+    cycle_term = scatter_sum(jnp.swapaxes(cycle_term, 0, 1), "vec")
+    total = total.reshape(n_ph, share, n_vir, slab)
+    total = total + jnp.where(own, cycle_term[:, :, None, :], 0.0)
+    total = total.transpose(2, 0, 1, 3)
     total = total.reshape(n_vir * n_ph // 4, 4, share, slab).transpose(1, 0, 2, 3)
     total = scatter_sum(scatter_sum(total, ("vir", "ph"), 4), ("vir", "ph"), -4)
 

time: 127 us -> 130 us (1.024)
  waiting for transfers between devices: 7.69 us -> 10.9 us
  starting transfers between devices: 23.5 us -> 22 us
    ppermute x7 -> x8, waiting for transfers between devices: 3.63 us -> 8.06 us  [scatter_sum(): total = total + lax.ppermute(piece, axes, pairs).astype(f32)]
    ppermute x7 -> x8, starting transfers between devices: 10.4 us -> 8.95 us  [scatter_sum(): total = total + lax.ppermute(piece, axes, pairs).astype(f32)]
    add x1 -> x0, other arithmetic: 1.39 us -> none  [local(): ladder.reshape(pairs, n_vir, slab)]
  transfers between devices with their start and end apart: 11 -> 12, of which waited for: 6 -> 7; matrix products, arithmetic and copies ran while one was open for 3% -> 5% of each run, Pallas kernels for 68% -> 67%
where the time goes in v7:
time: 130 us; the launch traced here: 129 us
  Pallas kernels  86.4 us (66%)
  starting transfers between devices  22 us (17%)
  waiting for transfers between devices  10.9 us (8%)
  other arithmetic  5.18 us (4%)
  local copies, waits for them, and re-layouts  3.77 us (3%)
    pallas_call x1, Pallas kernels, ladder_partial(): pl.pallas_call(functools.partial(ladder_kernel, sides), grid=(slab // dee...  70.2 us
    pallas_call x1, Pallas kernels, cycle_partial(): pl.pallas_call(functools.partial(cycle_kernel, shares, len(amps)), grid=(...  9.87 us
    ppermute x8, starting transfers between devices, scatter_sum(): total = total + lax.ppermute(piece, axes, pairs).astype(f32)  8.95 us
    ppermute x8, waiting for transfers between devices, scatter_sum(): total = total + lax.ppermute(piece, axes, pairs).astype(f32)  8.06 us
    pallas_call x1, Pallas kernels, own_row(): pl.pallas_call(row_kernel, grid=(chol // LANES, steps), in_specs=[side(q)...  6.39 us
    all_to_all x1, starting transfers between devices, local(): row = lax.all_to_all(row, 'vir', 0, 0)  6.28 us
    all_to_all x1, starting transfers between devices, local(): lax.all_to_all(cycle_partial(amps, codes, ov_slots), ('vir', 'ph', 'vec')...  3.68 us
    ppermute x2, starting transfers between devices, shifted(): return lax.ppermute(x, axes, [(i, (i + k) % n) for i in range(n)])  3.07 us
  transfers between devices with their start and end apart: 12, of which 7 were waited for; matrix products, arithmetic and copies ran while one was open for 5% of the time, Pallas kernels for 67%

profile of v7, /device:TPU:0, one launch (start us, length us, event | category | flops | bytes accessed | tf_op | source)
XLA Modules:
  0.0 129.3 jit_solution(9284875468026726893)
XLA Ops:
  0.6 1.1 fusion.16
  1.8 0.1 pad_maximum_fusion.refs_0_
  1.9 3.0 %collective-permute-start = (bf16[32,32,128]{2,1,0:T(8,128)(2,1)S(1)}, bf16[32,32,128]{2,1,0:T(8,128)(2,1)S(1)}, u32[]{:S(2)}, u32[]{:S(2)}) collective-permute-start(bf16[32,32,128]{2,1,0:T(8,128)(2,1)S(1)} %pad_maximum_fusion.refs_0_), channel_id=1, source_target_pairs={{0,2},{2,0},{1,3},{3,1},{4,6},{6,4},{5,7},{7,5},{8,10},{10,8},{9,1... | collective-permute-start | bytes 786440 | tf_op jit(solution)/shard_map/ppermute | solution.py:93
  5.0 0.7 multiply_add_fusion
  5.7 6.4 %shard_map.104 = bf16[8,256,128]{2,1,0:T(8,128)(2,1)} custom-call(bf16[256,128,1024]{2,1,0:T(8,128)(2,1)} %factor_hbm.1, bf16[256,128,1024]{2,1,0:T(8,128)(2,1)} %factor_hbm.1, bf16[256,128,1024]{2,1,0:T(8,128)(2,1)} %factor_hbm.1, bf16[256,128,1024]{2,1,0:T(8,128)(2,1)} %factor_hbm.1), custom_call_target="tpu_custom_call" | custom-call | flops 8388608 | bytes 8388608 | tf_op jit(solution)/shard_map/pallas_call | solution.py:134
  12.1 0.7 pad_add_fusion.code_ref
  12.7 6.3 %all-to-all-start = ((bf16[8,256,128]{2,1,0:T(8,128)(2,1)}), bf16[8,256,128]{2,1,0:T(8,128)(2,1)S(1)}, u32[]{:S(2)}, u32[]{:S(2)}) async-start(bf16[8,256,128]{2,1,0:T(8,128)(2,1)} %shard_map.104), calls=%async_computation | async-start | bytes 1048576 | tf_op jit(solution)/shard_map/all_to_all | solution.py:413
  19.0 1.2 slice.3
  20.2 9.9 %shard_map.106 = f32[32,32,256]{2,1,0:T(8,128)} custom-call(s32[1]{0:T(128)} %bitcast.3.place_ref, s32[128]{0:T(128)} %pad_add_fusion.code_ref, bf16[32,32,128]{2,1,0:T(8,128)(2,1)} %copy-done.2, bf16[32,32,128]{2,1,0:T(8,128)(2,1)} %copy-done.3, bf16[128,64,1024]{2,1,0:T(8,128)(2,1)} %bitcast.62, bf16[128,64,1024]{2,1,0:T(8,128)(2,1)} %bitcast.63, ...), custom_call_target="tpu_custom_call" | custom-call | flops 536870912 | bytes 16777216 | tf_op jit(solution)/shard_map/pallas_call | solution.py:211
  30.1 2.9 %all-to-all-done.row_ref = bf16[8,256,128]{2,1,0:T(8,128)(2,1)S(1)} async-done(((bf16[8,256,128]{2,1,0:T(8,128)(2,1)}), bf16[8,256,128]{2,1,0:T(8,128)(2,1)S(1)}, u32[]{:S(2)}, u32[]{:S(2)}) %all-to-all-start) | async-done | bytes 524320 | tf_op jit(solution)/shard_map/all_to_all | solution.py:413
  33.0 3.7 %all-to-all-start.1 = ((f32[32,32,256]{2,1,0:T(8,128)}), f32[32,32,256]{2,1,0:T(8,128)S(1)}, u32[]{:S(2)}, u32[]{:S(2)}) async-start(f32[32,32,256]{2,1,0:T(8,128)} %shard_map.106), calls=%async_computation.1 | async-start | bytes 2097152 | tf_op jit(solution)/shard_map/all_to_all | solution.py:414
  36.7 70.2 %shard_map.105 = f32[256,1024]{1,0:T(8,128)} custom-call(bf16[8,256,128]{2,1,0:T(8,128)(2,1)} %copy-done.1, bf16[1024,128,256]{2,1,0:T(8,128)(2,1)} %amp_hbm.1, bf16[256,128,1024]{2,1,0:T(8,128)(2,1)} %factor_hbm.1), custom_call_target="tpu_custom_call" | custom-call | flops 34359738368 | bytes 134217728 | tf_op jit(solution)/shard_map/pallas_call | solution.py:350
  106.9 1.1 fusion.3
  108.0 0.3 collective-permute-start.2
  108.4 0.2 fusion.1
  108.7 0.3 collective-permute-start.3
  109.0 0.6 collective-permute-done.2
  109.6 1.1 bitcast_add_fusion.1
  110.8 0.1 fusion
  111.1 2.7 %collective-permute-start.6 = (bf16[4,64,128]{2,1,0:T(8,128)(2,1)S(1)}, bf16[4,64,128]{2,1,0:T(8,128)(2,1)S(1)}, u32[]{:S(2)}, u32[]{:S(2)}) collective-permute-start(bf16[4,64,128]{2,1,0:T(8,128)(2,1)S(1)} %get-tuple-element.19), channel_id=1, source_target_pairs={{0,6},{2,0},{4,2},{6,4},{8,14},{10,8},{12,10},{14,12},{16,22},{18,... | collective-permute-start | bytes 196616 | tf_op jit(solution)/shard_map/ppermute | solution.py:395
  113.8 0.6 collective-permute-start.5
  114.4 0.6 collective-permute-start.4
  115.0 0.2 select_reduce_fusion.1
  115.1 1.1 collective-permute-done.6
  116.2 1.9 %collective-permute-done.5 = bf16[4,64,128]{2,1,0:T(8,128)(2,1)S(1)} collective-permute-done((bf16[4,64,128]{2,1,0:T(8,128)(2,1)S(1)}, bf16[4,64,128]{2,1,0:T(8,128)(2,1)S(1)}, u32[]{:S(2)}, u32[]{:S(2)}) %collective-permute-start.5) | collective-permute-done | bytes 65568 | tf_op jit(solution)/shard_map/ppermute | solution.py:395
  118.1 1.5 %collective-permute-done.4 = bf16[4,64,128]{2,1,0:T(8,128)(2,1)S(1)} collective-permute-done((bf16[4,64,128]{2,1,0:T(8,128)(2,1)S(1)}, bf16[4,64,128]{2,1,0:T(8,128)(2,1)S(1)}, u32[]{:S(2)}, u32[]{:S(2)}) %collective-permute-start.4) | collective-permute-done | bytes 65568 | tf_op jit(solution)/shard_map/ppermute | solution.py:395
  119.6 3.4 %collective-permute-start.9 = (bf16[64,128]{1,0:T(8,128)(2,1)S(1)}, bf16[64,128]{1,0:T(8,128)(2,1)S(1)}, u32[]{:S(2)}, u32[]{:S(2)}) collective-permute-start(bf16[64,128]{1,0:T(8,128)(2,1)S(1)} %get-tuple-element.22), channel_id=1, source_target_pairs={{0,24},{2,26},{4,28},{6,30},{8,0},{10,2},{12,4},{14,6},{16,8},{18,... | collective-permute-start | bytes 49160 | tf_op jit(solution)/shard_map/ppermute | solution.py:395
  123.0 1.1 collective-permute-start.7
  124.1 1.4 %dynamic-slice_add_fusion = f32[128]{0:T(128)S(1)} fusion(f32[1024]{0:T(1024)} %param.16, s32[]{:T(128)S(6)} %select_n.170, f32[]{:T(128)} %bitcast.20), kind=kLoop, calls=%fused_computation.39 | loop fusion | flops 128 | bytes 1032 | tf_op jit(solution)/shard_map/add | solution.py:445
  125.5 2.2 %collective-permute-done.8 = bf16[64,128]{1,0:T(8,128)(2,1)S(1)} collective-permute-done((bf16[64,128]{1,0:T(8,128)(2,1)S(1)}, bf16[64,128]{1,0:T(8,128)(2,1)S(1)}, u32[]{:S(2)}, u32[]{:S(2)}) %collective-permute-start.8) | collective-permute-done | bytes 16416 | tf_op jit(solution)/shard_map/ppermute | solution.py:395
  127.7 0.9 collective-permute-done.7
  128.6 0.7 subtract_divide_fusion
  (29 shorter events, 0.6 us)
Async XLA Ops:
  0.6 107.7 %copy-start = (bf16[256,8,128]{2,1,0:T(8,128)(2,1)S(1)}, bf16[256,8,128]{2,1,0:T(8,128)(2,1)}, u32[]{:S(2)}) copy-start(bf16[256,8,128]{2,1,0:T(8,128)(2,1)} %param.15) | copy-start | bytes 1572868
  1.9 10.1 %copy-start.2 = (bf16[32,32,128]{2,1,0:T(8,128)(2,1)}, bf16[32,32,128]{2,1,0:T(8,128)(2,1)S(1)}, u32[]{:S(2)}) copy-start(bf16[32,32,128]{2,1,0:T(8,128)(2,1)S(1)} %pad_maximum_fusion.refs_0_) | copy-start | bytes 786436
  1.9 10.8 %collective-permute-start = (bf16[32,32,128]{2,1,0:T(8,128)(2,1)S(1)}, bf16[32,32,128]{2,1,0:T(8,128)(2,1)S(1)}, u32[]{:S(2)}, u32[]{:S(2)}) collective-permute-start(bf16[32,32,128]{2,1,0:T(8,128)(2,1)S(1)} %pad_maximum_fusion.refs_0_), channel_id=1, source_target_pairs={{0,2},{2,0},{1,3},{3,1},{4,6},{6,4},{5,7},{7,5},{8,10},{10,8},{9,1... | collective-permute-start | bytes 786440 | tf_op jit(solution)/shard_map/ppermute | solution.py:93
  5.6 6.4 %collective-permute-start.1 = (s32[64]{0:T(128)S(1)}, s32[64]{0:T(128)S(1)}, u32[]{:S(2)}, u32[]{:S(2)}) collective-permute-start(s32[64]{0:T(128)S(1)} %multiply_add_fusion), channel_id=1, source_target_pairs={{0,2},{2,0},{1,3},{3,1},{4,6},{6,4},{5,7},{7,5},{8,10},{10,8},{9,1... | collective-permute-start | bytes 776 | tf_op jit(solution)/shard_map/ppermute | solution.py:93
  12.7 7.5 %copy-start.3 = (bf16[32,32,128]{2,1,0:T(8,128)(2,1)}, bf16[32,32,128]{2,1,0:T(8,128)(2,1)S(1)}, u32[]{:S(2)}) copy-start(bf16[32,32,128]{2,1,0:T(8,128)(2,1)S(1)} %collective-permute-done.refs_1_) | copy-start | bytes 786436
  12.7 20.2 %all-to-all-start = ((bf16[8,256,128]{2,1,0:T(8,128)(2,1)}), bf16[8,256,128]{2,1,0:T(8,128)(2,1)S(1)}, u32[]{:S(2)}, u32[]{:S(2)}) async-start(bf16[8,256,128]{2,1,0:T(8,128)(2,1)} %shard_map.104), calls=%async_computation | async-start | bytes 1048576 | tf_op jit(solution)/shard_map/all_to_all | solution.py:413
  33.0 3.7 %copy-start.1 = (bf16[8,256,128]{2,1,0:T(8,128)(2,1)}, bf16[8,256,128]{2,1,0:T(8,128)(2,1)S(1)}, u32[]{:S(2)}) copy-start(bf16[8,256,128]{2,1,0:T(8,128)(2,1)S(1)} %all-to-all-done.row_ref) | copy-start | bytes 1572868
  33.0 75.3 %all-to-all-start.1 = ((f32[32,32,256]{2,1,0:T(8,128)}), f32[32,32,256]{2,1,0:T(8,128)S(1)}, u32[]{:S(2)}, u32[]{:S(2)}) async-start(f32[32,32,256]{2,1,0:T(8,128)} %shard_map.106), calls=%async_computation.1 | async-start | bytes 2097152 | tf_op jit(solution)/shard_map/all_to_all | solution.py:414
  36.7 78.3 %copy-start.4 = (f32[128]{0:T(128)S(1)}, f32[128]{0:T(128)}, u32[]{:S(2)}) copy-start(f32[128]{0:T(128)} %param.17) | copy-start | bytes 1540
  108.0 1.6 %collective-permute-start.2 = (bf16[2,64,1024]{2,1,0:T(8,128)(2,1)S(1)}, bf16[2,64,1024]{2,1,0:T(8,128)(2,1)S(1)}, u32[]{:S(2)}, u32[]{:S(2)}) collective-permute-start(bf16[2,64,1024]{2,1,0:T(8,128)(2,1)S(1)} %fusion.3), channel_id=1, source_target_pairs={{0,1},{1,0},{2,3},{3,2},{4,5},{5,4},{6,7},{7,6},{8,9},{9,8},{10,11... | collective-permute-start | bytes 786440 | tf_op jit(solution)/shard_map/ppermute | solution.py:395
  108.7 2.1 %collective-permute-start.3 = (bf16[2,64,128]{2,1,0:T(8,128)(2,1)S(1)}, bf16[2,64,128]{2,1,0:T(8,128)(2,1)S(1)}, u32[]{:S(2)}, u32[]{:S(2)}) collective-permute-start(bf16[2,64,128]{2,1,0:T(8,128)(2,1)S(1)} %fusion.6), channel_id=1, source_target_pairs={{0,1},{1,0},{2,3},{3,2},{4,5},{5,4},{6,7},{7,6},{8,9},{9,8},{10,11... | collective-permute-start | bytes 98312 | tf_op jit(solution)/shard_map/ppermute | solution.py:395
  111.1 5.1 %collective-permute-start.6 = (bf16[4,64,128]{2,1,0:T(8,128)(2,1)S(1)}, bf16[4,64,128]{2,1,0:T(8,128)(2,1)S(1)}, u32[]{:S(2)}, u32[]{:S(2)}) collective-permute-start(bf16[4,64,128]{2,1,0:T(8,128)(2,1)S(1)} %get-tuple-element.19), channel_id=1, source_target_pairs={{0,6},{2,0},{4,2},{6,4},{8,14},{10,8},{12,10},{14,12},{16,22},{18,... | collective-permute-start | bytes 196616 | tf_op jit(solution)/shard_map/ppermute | solution.py:395
  113.8 4.3 %collective-permute-start.5 = (bf16[4,64,128]{2,1,0:T(8,128)(2,1)S(1)}, bf16[4,64,128]{2,1,0:T(8,128)(2,1)S(1)}, u32[]{:S(2)}, u32[]{:S(2)}) collective-permute-start(bf16[4,64,128]{2,1,0:T(8,128)(2,1)S(1)} %get-tuple-element.20), channel_id=1, source_target_pairs={{0,4},{2,6},{4,0},{6,2},{8,12},{10,14},{12,8},{14,10},{16,20},{18,... | collective-permute-start | bytes 196616 | tf_op jit(solution)/shard_map/ppermute | solution.py:395
  114.4 5.2 %collective-permute-start.4 = (bf16[4,64,128]{2,1,0:T(8,128)(2,1)S(1)}, bf16[4,64,128]{2,1,0:T(8,128)(2,1)S(1)}, u32[]{:S(2)}, u32[]{:S(2)}) collective-permute-start(bf16[4,64,128]{2,1,0:T(8,128)(2,1)S(1)} %get-tuple-element.18), channel_id=1, source_target_pairs={{0,2},{2,4},{4,6},{6,0},{8,10},{10,12},{12,14},{14,8},{16,18},{18,... | collective-permute-start | bytes 196616 | tf_op jit(solution)/shard_map/ppermute | solution.py:395
  119.6 5.9 %collective-permute-start.9 = (bf16[64,128]{1,0:T(8,128)(2,1)S(1)}, bf16[64,128]{1,0:T(8,128)(2,1)S(1)}, u32[]{:S(2)}, u32[]{:S(2)}) collective-permute-start(bf16[64,128]{1,0:T(8,128)(2,1)S(1)} %get-tuple-element.22), channel_id=1, source_target_pairs={{0,24},{2,26},{4,28},{6,30},{8,0},{10,2},{12,4},{14,6},{16,8},{18,... | collective-permute-start | bytes 49160 | tf_op jit(solution)/shard_map/ppermute | solution.py:395
  123.0 4.6 %collective-permute-start.8 = (bf16[64,128]{1,0:T(8,128)(2,1)S(1)}, bf16[64,128]{1,0:T(8,128)(2,1)S(1)}, u32[]{:S(2)}, u32[]{:S(2)}) collective-permute-start(bf16[64,128]{1,0:T(8,128)(2,1)S(1)} %get-tuple-element.23), channel_id=1, source_target_pairs={{0,16},{2,18},{4,20},{6,22},{8,24},{10,26},{12,28},{14,30},{16,0},... | collective-permute-start | bytes 49160 | tf_op jit(solution)/shard_map/ppermute | solution.py:395
  123.0 5.5 %collective-permute-start.7 = (bf16[64,128]{1,0:T(8,128)(2,1)S(1)}, bf16[64,128]{1,0:T(8,128)(2,1)S(1)}, u32[]{:S(2)}, u32[]{:S(2)}) collective-permute-start(bf16[64,128]{1,0:T(8,128)(2,1)S(1)} %get-tuple-element.21), channel_id=1, source_target_pairs={{0,8},{2,10},{4,12},{6,14},{8,16},{10,18},{12,20},{14,22},{16,24},... | collective-permute-start | bytes 49160 | tf_op jit(solution)/shard_map/ppermute | solution.py:395

commit v8 on v5

--- a/solution.py
+++ b/solution.py
@@ -145,11 +145,12 @@
     )(*[vv_factor] * sides)
 
 
-def cycle_kernel(shares, groups, place_ref, code_ref, *refs):
-    (*amp_refs, out_ref, amps, acc, block_of) = refs
-    amp_refs, ov_refs = amp_refs[:groups], amp_refs[groups:]
+def cycle_kernel(shares, groups, place_ref, *refs):
+    (*in_refs, out_ref, amps, acc, block_of) = refs
+    code_refs, amp_refs = in_refs[:groups], in_refs[groups : 2 * groups]
+    ov_refs = in_refs[2 * groups :]
     step = pl.program_id(0)
-    blocks, slots = code_ref.shape[0], block_of.shape[0]
+    blocks, slots = groups * code_refs[0].shape[0], block_of.shape[0]
     own, width = 2 * amp_refs[0].shape[0], amps.shape[2]
 
     @pl.when(step == 0)
@@ -167,13 +168,15 @@
         def _(s):
             block_of[s] = blocks
 
-        @pl.loop(0, blocks, unroll=8)
-        def _(n):
-            slot = code_ref[n] - first
-
-            @pl.when((slot >= 0) & (slot < slots))
-            def _():
-                block_of[slot] = n
+        for k, ref in enumerate(code_refs):
+
+            @pl.loop(0, ref.shape[0], unroll=8)
+            def _(n):
+                slot = ref[n] - first
+
+                @pl.when((slot >= 0) & (slot < slots))
+                def _():
+                    block_of[slot] = k * ref.shape[0] + n
 
     here, _, chol = ov_refs[0].shape
     start, count = step * len(ov_refs) * here, len(ov_refs) * here
@@ -190,7 +193,7 @@
 
 
 def cycle_operands(cycle_amp, owner_of, slot_of, slots):
-    codes = jnp.concatenate(round_robin(owner_of * slots + slot_of, "ph"))
+    codes = round_robin(owner_of * slots + slot_of, "ph")
     near, far = jnp.split(cycle_amp, 2, 0)
     return round_robin(jnp.concatenate([near, far], 2), "ph"), codes
 
@@ -211,13 +214,13 @@
     return pl.pallas_call(
         functools.partial(cycle_kernel, shares, len(amps)),
         grid=(slots // (here * sides),),
-        in_specs=[scalars, scalars]
+        in_specs=[scalars] * (1 + len(codes))
         + [whole] * len(amps)
         + [side(q) for q in range(sides)],
         out_specs=pl.BlockSpec((copies, occ, chol // shares), lambda i: (0, 0, 0)),
         out_shape=jax.ShapeDtypeStruct((copies, occ, chol // shares), f32),
         scratch_shapes=[
-            pltpu.VMEM((codes.shape[0] + 1, occ, width), bf16),
+            pltpu.VMEM((len(codes) * codes[0].shape[0] + 1, occ, width), bf16),
             pltpu.VMEM((occ, chol), f32),
             pltpu.SMEM((slots,), jnp.int32),
         ],
@@ -227,7 +230,7 @@
             bytes_accessed=2 * slots * width * chol,
             transcendentals=0,
         ),
-    )(place, codes, *amps, *[jnp.swapaxes(ov_slots, 1, 2)] * sides)
+    )(place, *codes, *amps, *[jnp.swapaxes(ov_slots, 1, 2)] * sides)
 
 
 def swap_matrix(deep):
@@ -253,21 +256,20 @@
             hbm.at[rows, block], buf.at[slot, rows], sem.at[slot, side]
         )
 
-    def start(step):
+    def start(hbm, buf, sem, step):
         for q in range(sides):
-            arriving(amp_hbm, amp_buf, amp_sem, step, q).start()
-        for q in range(sides):
-            arriving(factor_hbm, factor_buf, factor_sem, step, q).start()
+            arriving(hbm, buf, sem, step, q).start()
 
     @pl.when(step == 0)
     def _():
-        start(step)
+        start(amp_hbm, amp_buf, amp_sem, step)
         out_ref[...] = jnp.zeros_like(out_ref)
         swap[...] = swap_matrix(deep)
 
-    @pl.when(step + 1 < steps)
-    def _():
-        start(step + 1)
+    @pl.when((step > 0) & (step + 1 < steps))
+    def _():
+        start(amp_hbm, amp_buf, amp_sem, step + 1)
+        start(factor_hbm, factor_buf, factor_sem, step + 1)
 
     def later(jobs):
         store = None
@@ -297,6 +299,15 @@
         later(
             functools.partial(reorder, k) for k in range(q * size, (q + 1) * size, 2 * deep)
         )
+
+    @pl.when(step == 0)
+    def _():
+        start(factor_hbm, factor_buf, factor_sem, step)
+
+    @pl.when((step == 0) & (steps > 1))
+    def _():
+        start(amp_hbm, amp_buf, amp_sem, step + 1)
+        start(factor_hbm, factor_buf, factor_sem, step + 1)
 
     row = jnp.concatenate([row_ref[k] for k in range(count)], axis=1)
 

time: 127 us -> 128 us (level)
  Pallas kernels: 86.3 us -> 87.6 us
    pallas_call x1, Pallas kernels: 70 us -> 71.3 us  [ladder_partial(): pl.pallas_call(functools.partial(ladder_kernel, sides), grid=(slab // dee...]
  transfers between devices with their start and end apart: 11 -> 11, of which waited for: 6 -> 6; matrix products, arithmetic and copies ran while one was open for 3% -> 3% of each run, Pallas kernels for 68% -> 69%
where the time goes in v8:
time: 128 us
  Pallas kernels  87.6 us (68%)
  starting transfers between devices  23.5 us (18%)
  waiting for transfers between devices  7.66 us (6%)
  other arithmetic  4.73 us (4%)
  local copies, waits for them, and re-layouts  3.06 us (2%)
    pallas_call x1, Pallas kernels, ladder_partial(): pl.pallas_call(functools.partial(ladder_kernel, sides), grid=(slab // dee...  71.3 us
    ppermute x7, starting transfers between devices, scatter_sum(): total = total + lax.ppermute(piece, axes, pairs).astype(f32)  10.4 us
    pallas_call x1, Pallas kernels, cycle_partial(): pl.pallas_call(functools.partial(cycle_kernel, shares, len(amps)), grid=(...  9.86 us
    pallas_call x1, Pallas kernels, own_row(): pl.pallas_call(row_kernel, grid=(chol // LANES, steps), in_specs=[side(q)...  6.43 us
    all_to_all x1, starting transfers between devices, local(): row = lax.all_to_all(row, 'vir', 0, 0)  6.29 us
    all_to_all x1, waiting for transfers between devices, local(): row = lax.all_to_all(row, 'vir', 0, 0)  4.03 us
    all_to_all x1, starting transfers between devices, local(): lax.all_to_all(cycle_partial(amps, codes, ov_slots), ('vir', 'ph', 'vec')...  3.68 us
    ppermute x7, waiting for transfers between devices, scatter_sum(): total = total + lax.ppermute(piece, axes, pairs).astype(f32)  3.63 us
  transfers between devices with their start and end apart: 11, of which 6 were waited for; matrix products, arithmetic and copies ran while one was open for 3% of the time, Pallas kernels for 69%

profile of v8, /device:TPU:0, one launch (start us, length us, event | category | flops | bytes accessed | tf_op | source)
XLA Modules:
  0.0 127.6 jit_solution(11553228368850726157)
XLA Ops:
  0.6 1.1 fusion.14
  1.8 0.1 pad_maximum_fusion.refs_2_
  1.9 3.0 %collective-permute-start = (bf16[32,32,128]{2,1,0:T(8,128)(2,1)S(1)}, bf16[32,32,128]{2,1,0:T(8,128)(2,1)S(1)}, u32[]{:S(2)}, u32[]{:S(2)}) collective-permute-start(bf16[32,32,128]{2,1,0:T(8,128)(2,1)S(1)} %pad_maximum_fusion.refs_2_), channel_id=1, source_target_pairs={{0,2},{2,0},{1,3},{3,1},{4,6},{6,4},{5,7},{7,5},{8,10},{10,8},{9,1... | collective-permute-start | bytes 786440 | tf_op jit(solution)/shard_map/ppermute | solution.py:93
  5.0 0.7 multiply_add_fusion.refs_0_
  5.7 6.4 %shard_map.104 = bf16[8,256,128]{2,1,0:T(8,128)(2,1)} custom-call(bf16[256,128,1024]{2,1,0:T(8,128)(2,1)} %factor_hbm.1, bf16[256,128,1024]{2,1,0:T(8,128)(2,1)} %factor_hbm.1, bf16[256,128,1024]{2,1,0:T(8,128)(2,1)} %factor_hbm.1, bf16[256,128,1024]{2,1,0:T(8,128)(2,1)} %factor_hbm.1), custom_call_target="tpu_custom_call" | custom-call | flops 8388608 | bytes 8388608 | tf_op jit(solution)/shard_map/pallas_call | solution.py:134
  12.2 6.3 %all-to-all-start = ((bf16[8,256,128]{2,1,0:T(8,128)(2,1)}), bf16[8,256,128]{2,1,0:T(8,128)(2,1)S(1)}, u32[]{:S(2)}, u32[]{:S(2)}) async-start(bf16[8,256,128]{2,1,0:T(8,128)(2,1)} %shard_map.104), calls=%async_computation | async-start | bytes 1048576 | tf_op jit(solution)/shard_map/all_to_all | solution.py:423
  18.5 0.1 broadcast_bitcast_fusion
  18.5 9.9 %shard_map.106 = f32[32,32,256]{2,1,0:T(8,128)} custom-call(s32[1]{0:T(128)} %bitcast.2.place_ref, s32[64]{0:T(128)} %copy-done.5, s32[64]{0:T(128)} %copy-done.6, bf16[32,32,128]{2,1,0:T(8,128)(2,1)} %copy-done.2, bf16[32,32,128]{2,1,0:T(8,128)(2,1)} %copy-done.3, bf16[128,64,1024]{2,1,0:T(8,128)(2,1)} %bitcast.60, bf16[128,64,1024]{2,1,0:T(8,128)(2,1)} %bitcast.61, ...), custom_call_target="tpu_custom_call" | custom-call | flops 536870912 | bytes 16777216 | tf_op jit(solution)/shard_map/pallas_call | solution.py:214
  28.4 4.0 %all-to-all-done.row_ref = bf16[8,256,128]{2,1,0:T(8,128)(2,1)S(1)} async-done(((bf16[8,256,128]{2,1,0:T(8,128)(2,1)}), bf16[8,256,128]{2,1,0:T(8,128)(2,1)S(1)}, u32[]{:S(2)}, u32[]{:S(2)}) %all-to-all-start) | async-done | bytes 524320 | tf_op jit(solution)/shard_map/all_to_all | solution.py:423
  32.4 3.7 %all-to-all-start.1 = ((f32[32,32,256]{2,1,0:T(8,128)}), f32[32,32,256]{2,1,0:T(8,128)S(1)}, u32[]{:S(2)}, u32[]{:S(2)}) async-start(f32[32,32,256]{2,1,0:T(8,128)} %shard_map.106), calls=%async_computation.1 | async-start | bytes 2097152 | tf_op jit(solution)/shard_map/all_to_all | solution.py:424
  36.1 71.3 %shard_map.105 = f32[256,1024]{1,0:T(8,128)} custom-call(bf16[8,256,128]{2,1,0:T(8,128)(2,1)} %copy-done.1, bf16[1024,128,256]{2,1,0:T(8,128)(2,1)} %amp_hbm.1, bf16[256,128,1024]{2,1,0:T(8,128)(2,1)} %factor_hbm.1), custom_call_target="tpu_custom_call" | custom-call | flops 34359738368 | bytes 134217728 | tf_op jit(solution)/shard_map/pallas_call | solution.py:360
  107.6 0.2 fusion
  107.7 0.1 copy.24
  107.9 0.2 broadcast_in_dim.62
  108.1 1.4 %select_add_fusion = f32[2,2,64,1024]{3,2,1,0:T(8,128)S(1)} fusion(f32[2,2,64,1024]{3,2,1,0:T(8,128)} %bitcast.64, f32[2,2,64,1024]{3,2,1,0:T(8,128)S(1)} %broadcast_in_dim.62, pred[1024]{0:T(1024)(128)(4,1)S(1)} %broadcast_bitcast_fusion), kind=kLoop, calls=%fused_computation | loop fusion | flops 524288 | bytes 3146752 | tf_op jit(solution)/shard_map/add | solution.py:434
  109.5 0.3 collective-permute-start.2
  109.8 1.2 slice.3
  111.2 0.1 copy.20
  111.3 0.1 copy.19
  111.5 1.8 %collective-permute-start.3 = (bf16[4,64,128]{2,1,0:T(8,128)(2,1)S(1)}, bf16[4,64,128]{2,1,0:T(8,128)(2,1)S(1)}, u32[]{:S(2)}, u32[]{:S(2)}) collective-permute-start(bf16[4,64,128]{2,1,0:T(8,128)(2,1)S(1)} %get-tuple-element.20), channel_id=1, source_target_pairs={{0,2},{2,4},{4,6},{6,0},{8,10},{10,12},{12,14},{14,8},{16,18},{18,... | collective-permute-start | bytes 196616 | tf_op jit(solution)/shard_map/ppermute | solution.py:405
  113.4 1.5 %collective-permute-start.4 = (bf16[4,64,128]{2,1,0:T(8,128)(2,1)S(1)}, bf16[4,64,128]{2,1,0:T(8,128)(2,1)S(1)}, u32[]{:S(2)}, u32[]{:S(2)}) collective-permute-start(bf16[4,64,128]{2,1,0:T(8,128)(2,1)S(1)} %get-tuple-element.22), channel_id=1, source_target_pairs={{0,4},{2,6},{4,0},{6,2},{8,12},{10,14},{12,8},{14,10},{16,20},{18,... | collective-permute-start | bytes 196616 | tf_op jit(solution)/shard_map/ppermute | solution.py:405
  114.8 1.5 %collective-permute-start.5 = (bf16[4,64,128]{2,1,0:T(8,128)(2,1)S(1)}, bf16[4,64,128]{2,1,0:T(8,128)(2,1)S(1)}, u32[]{:S(2)}, u32[]{:S(2)}) collective-permute-start(bf16[4,64,128]{2,1,0:T(8,128)(2,1)S(1)} %get-tuple-element.21), channel_id=1, source_target_pairs={{0,6},{2,0},{4,2},{6,4},{8,14},{10,8},{12,10},{14,12},{16,22},{18,... | collective-permute-start | bytes 196616 | tf_op jit(solution)/shard_map/ppermute | solution.py:405
  116.3 0.2 select_reduce_fusion.1
  116.5 0.3 collective-permute-done.3
  116.8 1.5 %collective-permute-done.4 = bf16[4,64,128]{2,1,0:T(8,128)(2,1)S(1)} collective-permute-done((bf16[4,64,128]{2,1,0:T(8,128)(2,1)S(1)}, bf16[4,64,128]{2,1,0:T(8,128)(2,1)S(1)}, u32[]{:S(2)}, u32[]{:S(2)}) %collective-permute-start.4) | collective-permute-done | bytes 65568 | tf_op jit(solution)/shard_map/ppermute | solution.py:405
  118.3 0.8 collective-permute-done.5
  119.2 1.5 %collective-permute-start.6 = (bf16[64,128]{1,0:T(8,128)(2,1)S(1)}, bf16[64,128]{1,0:T(8,128)(2,1)S(1)}, u32[]{:S(2)}, u32[]{:S(2)}) collective-permute-start(bf16[64,128]{1,0:T(8,128)(2,1)S(1)} %get-tuple-element.23), channel_id=1, source_target_pairs={{0,8},{2,10},{4,12},{6,14},{8,16},{10,18},{12,20},{14,22},{16,24},... | collective-permute-start | bytes 49160 | tf_op jit(solution)/shard_map/ppermute | solution.py:405
  120.7 2.5 %collective-permute-start.7 = (bf16[64,128]{1,0:T(8,128)(2,1)S(1)}, bf16[64,128]{1,0:T(8,128)(2,1)S(1)}, u32[]{:S(2)}, u32[]{:S(2)}) collective-permute-start(bf16[64,128]{1,0:T(8,128)(2,1)S(1)} %get-tuple-element.25), channel_id=1, source_target_pairs={{0,16},{2,18},{4,20},{6,22},{8,24},{10,26},{12,28},{14,30},{16,0},... | collective-permute-start | bytes 49160 | tf_op jit(solution)/shard_map/ppermute | solution.py:405
  123.1 1.4 %collective-permute-start.8 = (bf16[64,128]{1,0:T(8,128)(2,1)S(1)}, bf16[64,128]{1,0:T(8,128)(2,1)S(1)}, u32[]{:S(2)}, u32[]{:S(2)}) collective-permute-start(bf16[64,128]{1,0:T(8,128)(2,1)S(1)} %get-tuple-element.24), channel_id=1, source_target_pairs={{0,24},{2,26},{4,28},{6,30},{8,0},{10,2},{12,4},{14,6},{16,8},{18,... | collective-permute-start | bytes 49160 | tf_op jit(solution)/shard_map/ppermute | solution.py:405
  124.5 1.4 %dynamic-slice_add_fusion = f32[128]{0:T(128)S(1)} fusion(f32[1024]{0:T(1024)} %param.16, s32[]{:T(128)S(6)} %select_n.165, f32[]{:T(128)} %bitcast.19), kind=kLoop, calls=%fused_computation.37 | loop fusion | flops 128 | bytes 1032 | tf_op jit(solution)/shard_map/add | solution.py:452
  125.9 0.9 collective-permute-done.8
  126.9 0.7 subtract_divide_fusion
  (32 shorter events, 0.6 us)
Async XLA Ops:
  0.6 106.9 %copy-start = (bf16[256,8,128]{2,1,0:T(8,128)(2,1)S(1)}, bf16[256,8,128]{2,1,0:T(8,128)(2,1)}, u32[]{:S(2)}) copy-start(bf16[256,8,128]{2,1,0:T(8,128)(2,1)} %param.15) | copy-start | bytes 1572868
  1.9 10.2 %copy-start.2 = (bf16[32,32,128]{2,1,0:T(8,128)(2,1)}, bf16[32,32,128]{2,1,0:T(8,128)(2,1)S(1)}, u32[]{:S(2)}) copy-start(bf16[32,32,128]{2,1,0:T(8,128)(2,1)S(1)} %pad_maximum_fusion.refs_2_) | copy-start | bytes 786436
  1.9 10.2 %collective-permute-start = (bf16[32,32,128]{2,1,0:T(8,128)(2,1)S(1)}, bf16[32,32,128]{2,1,0:T(8,128)(2,1)S(1)}, u32[]{:S(2)}, u32[]{:S(2)}) collective-permute-start(bf16[32,32,128]{2,1,0:T(8,128)(2,1)S(1)} %pad_maximum_fusion.refs_2_), channel_id=1, source_target_pairs={{0,2},{2,0},{1,3},{3,1},{4,6},{6,4},{5,7},{7,5},{8,10},{10,8},{9,1... | collective-permute-start | bytes 786440 | tf_op jit(solution)/shard_map/ppermute | solution.py:93
  5.6 6.5 %copy-start.5 = (s32[64]{0:T(128)}, s32[64]{0:T(128)S(1)}, u32[]{:S(2)}) copy-start(s32[64]{0:T(128)S(1)} %multiply_add_fusion.refs_0_) | copy-start | bytes 772
  5.6 6.5 %collective-permute-start.1 = (s32[64]{0:T(128)S(1)}, s32[64]{0:T(128)S(1)}, u32[]{:S(2)}, u32[]{:S(2)}) collective-permute-start(s32[64]{0:T(128)S(1)} %multiply_add_fusion.refs_0_), channel_id=1, source_target_pairs={{0,2},{2,0},{1,3},{3,1},{4,6},{6,4},{5,7},{7,5},{8,10},{10,8},{9,1... | collective-permute-start | bytes 776 | tf_op jit(solution)/shard_map/ppermute | solution.py:93
  12.1 6.4 %copy-start.6 = (s32[64]{0:T(128)}, s32[64]{0:T(128)S(1)}, u32[]{:S(2)}) copy-start(s32[64]{0:T(128)S(1)} %collective-permute-done.1.refs_1_) | copy-start | bytes 772
  12.1 6.4 %copy-start.3 = (bf16[32,32,128]{2,1,0:T(8,128)(2,1)}, bf16[32,32,128]{2,1,0:T(8,128)(2,1)S(1)}, u32[]{:S(2)}) copy-start(bf16[32,32,128]{2,1,0:T(8,128)(2,1)S(1)} %collective-permute-done.refs_3_) | copy-start | bytes 786436
  12.2 20.3 %all-to-all-start = ((bf16[8,256,128]{2,1,0:T(8,128)(2,1)}), bf16[8,256,128]{2,1,0:T(8,128)(2,1)S(1)}, u32[]{:S(2)}, u32[]{:S(2)}) async-start(bf16[8,256,128]{2,1,0:T(8,128)(2,1)} %shard_map.104), calls=%async_computation | async-start | bytes 1048576 | tf_op jit(solution)/shard_map/all_to_all | solution.py:423
  32.4 3.7 %copy-start.1 = (bf16[8,256,128]{2,1,0:T(8,128)(2,1)}, bf16[8,256,128]{2,1,0:T(8,128)(2,1)S(1)}, u32[]{:S(2)}) copy-start(bf16[8,256,128]{2,1,0:T(8,128)(2,1)S(1)} %all-to-all-done.row_ref) | copy-start | bytes 1572868
  32.4 75.0 %all-to-all-start.1 = ((f32[32,32,256]{2,1,0:T(8,128)}), f32[32,32,256]{2,1,0:T(8,128)S(1)}, u32[]{:S(2)}, u32[]{:S(2)}) async-start(f32[32,32,256]{2,1,0:T(8,128)} %shard_map.106), calls=%async_computation.1 | async-start | bytes 2097152 | tf_op jit(solution)/shard_map/all_to_all | solution.py:424
  36.1 80.2 %copy-start.4 = (f32[128]{0:T(128)S(1)}, f32[128]{0:T(128)}, u32[]{:S(2)}) copy-start(f32[128]{0:T(128)} %param.17) | copy-start | bytes 1540
  109.5 1.6 %collective-permute-start.2 = (bf16[2,64,1024]{2,1,0:T(8,128)(2,1)S(1)}, bf16[2,64,1024]{2,1,0:T(8,128)(2,1)S(1)}, u32[]{:S(2)}, u32[]{:S(2)}) collective-permute-start(bf16[2,64,1024]{2,1,0:T(8,128)(2,1)S(1)} %fusion.2), channel_id=1, source_target_pairs={{0,1},{1,0},{2,3},{3,2},{4,5},{5,4},{6,7},{7,6},{8,9},{9,8},{10,11... | collective-permute-start | bytes 786440 | tf_op jit(solution)/shard_map/ppermute | solution.py:405
  111.5 5.2 %collective-permute-start.3 = (bf16[4,64,128]{2,1,0:T(8,128)(2,1)S(1)}, bf16[4,64,128]{2,1,0:T(8,128)(2,1)S(1)}, u32[]{:S(2)}, u32[]{:S(2)}) collective-permute-start(bf16[4,64,128]{2,1,0:T(8,128)(2,1)S(1)} %get-tuple-element.20), channel_id=1, source_target_pairs={{0,2},{2,4},{4,6},{6,0},{8,10},{10,12},{12,14},{14,8},{16,18},{18,... | collective-permute-start | bytes 196616 | tf_op jit(solution)/shard_map/ppermute | solution.py:405
  113.4 4.9 %collective-permute-start.4 = (bf16[4,64,128]{2,1,0:T(8,128)(2,1)S(1)}, bf16[4,64,128]{2,1,0:T(8,128)(2,1)S(1)}, u32[]{:S(2)}, u32[]{:S(2)}) collective-permute-start(bf16[4,64,128]{2,1,0:T(8,128)(2,1)S(1)} %get-tuple-element.22), channel_id=1, source_target_pairs={{0,4},{2,6},{4,0},{6,2},{8,12},{10,14},{12,8},{14,10},{16,20},{18,... | collective-permute-start | bytes 196616 | tf_op jit(solution)/shard_map/ppermute | solution.py:405
  114.8 4.3 %collective-permute-start.5 = (bf16[4,64,128]{2,1,0:T(8,128)(2,1)S(1)}, bf16[4,64,128]{2,1,0:T(8,128)(2,1)S(1)}, u32[]{:S(2)}, u32[]{:S(2)}) collective-permute-start(bf16[4,64,128]{2,1,0:T(8,128)(2,1)S(1)} %get-tuple-element.21), channel_id=1, source_target_pairs={{0,6},{2,0},{4,2},{6,4},{8,14},{10,8},{12,10},{14,12},{16,22},{18,... | collective-permute-start | bytes 196616 | tf_op jit(solution)/shard_map/ppermute | solution.py:405
  119.2 6.8 %collective-permute-start.6 = (bf16[64,128]{1,0:T(8,128)(2,1)S(1)}, bf16[64,128]{1,0:T(8,128)(2,1)S(1)}, u32[]{:S(2)}, u32[]{:S(2)}) collective-permute-start(bf16[64,128]{1,0:T(8,128)(2,1)S(1)} %get-tuple-element.23), channel_id=1, source_target_pairs={{0,8},{2,10},{4,12},{6,14},{8,16},{10,18},{12,20},{14,22},{16,24},... | collective-permute-start | bytes 49160 | tf_op jit(solution)/shard_map/ppermute | solution.py:405
  120.7 5.3 %collective-permute-start.7 = (bf16[64,128]{1,0:T(8,128)(2,1)S(1)}, bf16[64,128]{1,0:T(8,128)(2,1)S(1)}, u32[]{:S(2)}, u32[]{:S(2)}) collective-permute-start(bf16[64,128]{1,0:T(8,128)(2,1)S(1)} %get-tuple-element.25), channel_id=1, source_target_pairs={{0,16},{2,18},{4,20},{6,22},{8,24},{10,26},{12,28},{14,30},{16,0},... | collective-permute-start | bytes 49160 | tf_op jit(solution)/shard_map/ppermute | solution.py:405
  123.1 3.7 %collective-permute-start.8 = (bf16[64,128]{1,0:T(8,128)(2,1)S(1)}, bf16[64,128]{1,0:T(8,128)(2,1)S(1)}, u32[]{:S(2)}, u32[]{:S(2)}) collective-permute-start(bf16[64,128]{1,0:T(8,128)(2,1)S(1)} %get-tuple-element.24), channel_id=1, source_target_pairs={{0,24},{2,26},{4,28},{6,30},{8,0},{10,2},{12,4},{14,6},{16,8},{18,... | collective-permute-start | bytes 49160 | tf_op jit(solution)/shard_map/ppermute | solution.py:405

commit v9 on v8

--- a/solution.py
+++ b/solution.py
@@ -307,7 +307,6 @@
     @pl.when((step == 0) & (steps > 1))
     def _():
         start(amp_hbm, amp_buf, amp_sem, step + 1)
-        start(factor_hbm, factor_buf, factor_sem, step + 1)
 
     row = jnp.concatenate([row_ref[k] for k in range(count)], axis=1)
 
@@ -321,6 +320,10 @@
         return store
 
     later(functools.partial(halves, d) for d in range(0, deep, 2))
+
+    @pl.when((step == 0) & (steps > 1))
+    def _():
+        start(factor_hbm, factor_buf, factor_sem, step + 1)
 
     def flatten(first):
         parts = range(first, first + 4 * deep, deep)

time: 128 us -> 128 us (level)
  no operation moved by 1% of the time
where the time goes in v9:
time: 128 us
  Pallas kernels  87.5 us (68%)
  starting transfers between devices  23.5 us (18%)
  waiting for transfers between devices  7.66 us (6%)
  other arithmetic  4.73 us (4%)
  local copies, waits for them, and re-layouts  3.06 us (2%)
    pallas_call x1, Pallas kernels, ladder_partial(): pl.pallas_call(functools.partial(ladder_kernel, sides), grid=(slab // dee...  71.2 us
    ppermute x7, starting transfers between devices, scatter_sum(): total = total + lax.ppermute(piece, axes, pairs).astype(f32)  10.4 us
    pallas_call x1, Pallas kernels, cycle_partial(): pl.pallas_call(functools.partial(cycle_kernel, shares, len(amps)), grid=(...  9.86 us
    pallas_call x1, Pallas kernels, own_row(): pl.pallas_call(row_kernel, grid=(chol // LANES, steps), in_specs=[side(q)...  6.43 us
    all_to_all x1, starting transfers between devices, local(): row = lax.all_to_all(row, 'vir', 0, 0)  6.29 us
    all_to_all x1, waiting for transfers between devices, local(): row = lax.all_to_all(row, 'vir', 0, 0)  4.02 us
    all_to_all x1, starting transfers between devices, local(): lax.all_to_all(cycle_partial(amps, codes, ov_slots), ('vir', 'ph', 'vec')...  3.68 us
    ppermute x7, waiting for transfers between devices, scatter_sum(): total = total + lax.ppermute(piece, axes, pairs).astype(f32)  3.63 us
  transfers between devices with their start and end apart: 11, of which 6 were waited for; matrix products, arithmetic and copies ran while one was open for 3% of the time, Pallas kernels for 69%

profile of v9, /device:TPU:0, one launch (start us, length us, event | category | flops | bytes accessed | tf_op | source)
XLA Modules:
  0.0 127.5 jit_solution(13642576010849542200)
XLA Ops:
  0.6 1.1 fusion.14
  1.8 0.1 pad_maximum_fusion.refs_2_
  1.9 3.0 %collective-permute-start = (bf16[32,32,128]{2,1,0:T(8,128)(2,1)S(1)}, bf16[32,32,128]{2,1,0:T(8,128)(2,1)S(1)}, u32[]{:S(2)}, u32[]{:S(2)}) collective-permute-start(bf16[32,32,128]{2,1,0:T(8,128)(2,1)S(1)} %pad_maximum_fusion.refs_2_), channel_id=1, source_target_pairs={{0,2},{2,0},{1,3},{3,1},{4,6},{6,4},{5,7},{7,5},{8,10},{10,8},{9,1... | collective-permute-start | bytes 786440 | tf_op jit(solution)/shard_map/ppermute | solution.py:93
  5.0 0.7 multiply_add_fusion.refs_0_
  5.7 6.4 %shard_map.104 = bf16[8,256,128]{2,1,0:T(8,128)(2,1)} custom-call(bf16[256,128,1024]{2,1,0:T(8,128)(2,1)} %factor_hbm.1, bf16[256,128,1024]{2,1,0:T(8,128)(2,1)} %factor_hbm.1, bf16[256,128,1024]{2,1,0:T(8,128)(2,1)} %factor_hbm.1, bf16[256,128,1024]{2,1,0:T(8,128)(2,1)} %factor_hbm.1), custom_call_target="tpu_custom_call" | custom-call | flops 8388608 | bytes 8388608 | tf_op jit(solution)/shard_map/pallas_call | solution.py:134
  12.2 6.3 %all-to-all-start = ((bf16[8,256,128]{2,1,0:T(8,128)(2,1)}), bf16[8,256,128]{2,1,0:T(8,128)(2,1)S(1)}, u32[]{:S(2)}, u32[]{:S(2)}) async-start(bf16[8,256,128]{2,1,0:T(8,128)(2,1)} %shard_map.104), calls=%async_computation | async-start | bytes 1048576 | tf_op jit(solution)/shard_map/all_to_all | solution.py:426
  18.5 0.1 broadcast_bitcast_fusion
  18.5 9.9 %shard_map.106 = f32[32,32,256]{2,1,0:T(8,128)} custom-call(s32[1]{0:T(128)} %bitcast.2.place_ref, s32[64]{0:T(128)} %copy-done.5, s32[64]{0:T(128)} %copy-done.6, bf16[32,32,128]{2,1,0:T(8,128)(2,1)} %copy-done.2, bf16[32,32,128]{2,1,0:T(8,128)(2,1)} %copy-done.3, bf16[128,64,1024]{2,1,0:T(8,128)(2,1)} %bitcast.60, bf16[128,64,1024]{2,1,0:T(8,128)(2,1)} %bitcast.61, ...), custom_call_target="tpu_custom_call" | custom-call | flops 536870912 | bytes 16777216 | tf_op jit(solution)/shard_map/pallas_call | solution.py:214
  28.4 4.0 %all-to-all-done.row_ref = bf16[8,256,128]{2,1,0:T(8,128)(2,1)S(1)} async-done(((bf16[8,256,128]{2,1,0:T(8,128)(2,1)}), bf16[8,256,128]{2,1,0:T(8,128)(2,1)S(1)}, u32[]{:S(2)}, u32[]{:S(2)}) %all-to-all-start) | async-done | bytes 524320 | tf_op jit(solution)/shard_map/all_to_all | solution.py:426
  32.4 3.7 %all-to-all-start.1 = ((f32[32,32,256]{2,1,0:T(8,128)}), f32[32,32,256]{2,1,0:T(8,128)S(1)}, u32[]{:S(2)}, u32[]{:S(2)}) async-start(f32[32,32,256]{2,1,0:T(8,128)} %shard_map.106), calls=%async_computation.1 | async-start | bytes 2097152 | tf_op jit(solution)/shard_map/all_to_all | solution.py:427
  36.1 71.2 %shard_map.105 = f32[256,1024]{1,0:T(8,128)} custom-call(bf16[8,256,128]{2,1,0:T(8,128)(2,1)} %copy-done.1, bf16[1024,128,256]{2,1,0:T(8,128)(2,1)} %amp_hbm.1, bf16[256,128,1024]{2,1,0:T(8,128)(2,1)} %factor_hbm.1), custom_call_target="tpu_custom_call" | custom-call | flops 34359738368 | bytes 134217728 | tf_op jit(solution)/shard_map/pallas_call | solution.py:363
  107.5 0.2 fusion
  107.7 0.1 copy.24
  107.8 0.2 broadcast_in_dim.62
  108.0 1.4 %select_add_fusion = f32[2,2,64,1024]{3,2,1,0:T(8,128)S(1)} fusion(f32[2,2,64,1024]{3,2,1,0:T(8,128)} %bitcast.64, f32[2,2,64,1024]{3,2,1,0:T(8,128)S(1)} %broadcast_in_dim.62, pred[1024]{0:T(1024)(128)(4,1)S(1)} %broadcast_bitcast_fusion), kind=kLoop, calls=%fused_computation | loop fusion | flops 524288 | bytes 3146752 | tf_op jit(solution)/shard_map/add | solution.py:437
  109.4 0.3 collective-permute-start.2
  109.8 1.2 slice.3
  111.1 0.1 copy.20
  111.3 0.1 copy.19
  111.5 1.8 %collective-permute-start.3 = (bf16[4,64,128]{2,1,0:T(8,128)(2,1)S(1)}, bf16[4,64,128]{2,1,0:T(8,128)(2,1)S(1)}, u32[]{:S(2)}, u32[]{:S(2)}) collective-permute-start(bf16[4,64,128]{2,1,0:T(8,128)(2,1)S(1)} %get-tuple-element.20), channel_id=1, source_target_pairs={{0,2},{2,4},{4,6},{6,0},{8,10},{10,12},{12,14},{14,8},{16,18},{18,... | collective-permute-start | bytes 196616 | tf_op jit(solution)/shard_map/ppermute | solution.py:408
  113.3 1.5 %collective-permute-start.4 = (bf16[4,64,128]{2,1,0:T(8,128)(2,1)S(1)}, bf16[4,64,128]{2,1,0:T(8,128)(2,1)S(1)}, u32[]{:S(2)}, u32[]{:S(2)}) collective-permute-start(bf16[4,64,128]{2,1,0:T(8,128)(2,1)S(1)} %get-tuple-element.22), channel_id=1, source_target_pairs={{0,4},{2,6},{4,0},{6,2},{8,12},{10,14},{12,8},{14,10},{16,20},{18,... | collective-permute-start | bytes 196616 | tf_op jit(solution)/shard_map/ppermute | solution.py:408
  114.7 1.5 %collective-permute-start.5 = (bf16[4,64,128]{2,1,0:T(8,128)(2,1)S(1)}, bf16[4,64,128]{2,1,0:T(8,128)(2,1)S(1)}, u32[]{:S(2)}, u32[]{:S(2)}) collective-permute-start(bf16[4,64,128]{2,1,0:T(8,128)(2,1)S(1)} %get-tuple-element.21), channel_id=1, source_target_pairs={{0,6},{2,0},{4,2},{6,4},{8,14},{10,8},{12,10},{14,12},{16,22},{18,... | collective-permute-start | bytes 196616 | tf_op jit(solution)/shard_map/ppermute | solution.py:408
  116.2 0.2 select_reduce_fusion.1
  116.4 0.3 collective-permute-done.3
  116.7 1.5 %collective-permute-done.4 = bf16[4,64,128]{2,1,0:T(8,128)(2,1)S(1)} collective-permute-done((bf16[4,64,128]{2,1,0:T(8,128)(2,1)S(1)}, bf16[4,64,128]{2,1,0:T(8,128)(2,1)S(1)}, u32[]{:S(2)}, u32[]{:S(2)}) %collective-permute-start.4) | collective-permute-done | bytes 65568 | tf_op jit(solution)/shard_map/ppermute | solution.py:408
  118.2 0.8 collective-permute-done.5
  119.1 1.5 %collective-permute-start.6 = (bf16[64,128]{1,0:T(8,128)(2,1)S(1)}, bf16[64,128]{1,0:T(8,128)(2,1)S(1)}, u32[]{:S(2)}, u32[]{:S(2)}) collective-permute-start(bf16[64,128]{1,0:T(8,128)(2,1)S(1)} %get-tuple-element.23), channel_id=1, source_target_pairs={{0,8},{2,10},{4,12},{6,14},{8,16},{10,18},{12,20},{14,22},{16,24},... | collective-permute-start | bytes 49160 | tf_op jit(solution)/shard_map/ppermute | solution.py:408
  120.6 2.5 %collective-permute-start.7 = (bf16[64,128]{1,0:T(8,128)(2,1)S(1)}, bf16[64,128]{1,0:T(8,128)(2,1)S(1)}, u32[]{:S(2)}, u32[]{:S(2)}) collective-permute-start(bf16[64,128]{1,0:T(8,128)(2,1)S(1)} %get-tuple-element.25), channel_id=1, source_target_pairs={{0,16},{2,18},{4,20},{6,22},{8,24},{10,26},{12,28},{14,30},{16,0},... | collective-permute-start | bytes 49160 | tf_op jit(solution)/shard_map/ppermute | solution.py:408
  123.1 1.4 %collective-permute-start.8 = (bf16[64,128]{1,0:T(8,128)(2,1)S(1)}, bf16[64,128]{1,0:T(8,128)(2,1)S(1)}, u32[]{:S(2)}, u32[]{:S(2)}) collective-permute-start(bf16[64,128]{1,0:T(8,128)(2,1)S(1)} %get-tuple-element.24), channel_id=1, source_target_pairs={{0,24},{2,26},{4,28},{6,30},{8,0},{10,2},{12,4},{14,6},{16,8},{18,... | collective-permute-start | bytes 49160 | tf_op jit(solution)/shard_map/ppermute | solution.py:408
  124.5 1.4 %dynamic-slice_add_fusion = f32[128]{0:T(128)S(1)} fusion(f32[1024]{0:T(1024)} %param.16, s32[]{:T(128)S(6)} %select_n.165, f32[]{:T(128)} %bitcast.19), kind=kLoop, calls=%fused_computation.37 | loop fusion | flops 128 | bytes 1032 | tf_op jit(solution)/shard_map/add | solution.py:455
  125.9 0.9 collective-permute-done.8
  126.8 0.7 subtract_divide_fusion
  (32 shorter events, 0.6 us)
Async XLA Ops:
  0.6 106.8 %copy-start = (bf16[256,8,128]{2,1,0:T(8,128)(2,1)S(1)}, bf16[256,8,128]{2,1,0:T(8,128)(2,1)}, u32[]{:S(2)}) copy-start(bf16[256,8,128]{2,1,0:T(8,128)(2,1)} %param.15) | copy-start | bytes 1572868
  1.9 10.2 %copy-start.2 = (bf16[32,32,128]{2,1,0:T(8,128)(2,1)}, bf16[32,32,128]{2,1,0:T(8,128)(2,1)S(1)}, u32[]{:S(2)}) copy-start(bf16[32,32,128]{2,1,0:T(8,128)(2,1)S(1)} %pad_maximum_fusion.refs_2_) | copy-start | bytes 786436
  1.9 10.2 %collective-permute-start = (bf16[32,32,128]{2,1,0:T(8,128)(2,1)S(1)}, bf16[32,32,128]{2,1,0:T(8,128)(2,1)S(1)}, u32[]{:S(2)}, u32[]{:S(2)}) collective-permute-start(bf16[32,32,128]{2,1,0:T(8,128)(2,1)S(1)} %pad_maximum_fusion.refs_2_), channel_id=1, source_target_pairs={{0,2},{2,0},{1,3},{3,1},{4,6},{6,4},{5,7},{7,5},{8,10},{10,8},{9,1... | collective-permute-start | bytes 786440 | tf_op jit(solution)/shard_map/ppermute | solution.py:93
  5.6 6.5 %copy-start.5 = (s32[64]{0:T(128)}, s32[64]{0:T(128)S(1)}, u32[]{:S(2)}) copy-start(s32[64]{0:T(128)S(1)} %multiply_add_fusion.refs_0_) | copy-start | bytes 772
  5.6 6.5 %collective-permute-start.1 = (s32[64]{0:T(128)S(1)}, s32[64]{0:T(128)S(1)}, u32[]{:S(2)}, u32[]{:S(2)}) collective-permute-start(s32[64]{0:T(128)S(1)} %multiply_add_fusion.refs_0_), channel_id=1, source_target_pairs={{0,2},{2,0},{1,3},{3,1},{4,6},{6,4},{5,7},{7,5},{8,10},{10,8},{9,1... | collective-permute-start | bytes 776 | tf_op jit(solution)/shard_map/ppermute | solution.py:93
  12.1 6.4 %copy-start.6 = (s32[64]{0:T(128)}, s32[64]{0:T(128)S(1)}, u32[]{:S(2)}) copy-start(s32[64]{0:T(128)S(1)} %collective-permute-done.1.refs_1_) | copy-start | bytes 772
  12.1 6.4 %copy-start.3 = (bf16[32,32,128]{2,1,0:T(8,128)(2,1)}, bf16[32,32,128]{2,1,0:T(8,128)(2,1)S(1)}, u32[]{:S(2)}) copy-start(bf16[32,32,128]{2,1,0:T(8,128)(2,1)S(1)} %collective-permute-done.refs_3_) | copy-start | bytes 786436
  12.2 20.3 %all-to-all-start = ((bf16[8,256,128]{2,1,0:T(8,128)(2,1)}), bf16[8,256,128]{2,1,0:T(8,128)(2,1)S(1)}, u32[]{:S(2)}, u32[]{:S(2)}) async-start(bf16[8,256,128]{2,1,0:T(8,128)(2,1)} %shard_map.104), calls=%async_computation | async-start | bytes 1048576 | tf_op jit(solution)/shard_map/all_to_all | solution.py:426
  32.4 3.7 %copy-start.1 = (bf16[8,256,128]{2,1,0:T(8,128)(2,1)}, bf16[8,256,128]{2,1,0:T(8,128)(2,1)S(1)}, u32[]{:S(2)}) copy-start(bf16[8,256,128]{2,1,0:T(8,128)(2,1)S(1)} %all-to-all-done.row_ref) | copy-start | bytes 1572868
  32.4 75.0 %all-to-all-start.1 = ((f32[32,32,256]{2,1,0:T(8,128)}), f32[32,32,256]{2,1,0:T(8,128)S(1)}, u32[]{:S(2)}, u32[]{:S(2)}) async-start(f32[32,32,256]{2,1,0:T(8,128)} %shard_map.106), calls=%async_computation.1 | async-start | bytes 2097152 | tf_op jit(solution)/shard_map/all_to_all | solution.py:427
  36.1 80.1 %copy-start.4 = (f32[128]{0:T(128)S(1)}, f32[128]{0:T(128)}, u32[]{:S(2)}) copy-start(f32[128]{0:T(128)} %param.17) | copy-start | bytes 1540
  109.4 1.6 %collective-permute-start.2 = (bf16[2,64,1024]{2,1,0:T(8,128)(2,1)S(1)}, bf16[2,64,1024]{2,1,0:T(8,128)(2,1)S(1)}, u32[]{:S(2)}, u32[]{:S(2)}) collective-permute-start(bf16[2,64,1024]{2,1,0:T(8,128)(2,1)S(1)} %fusion.2), channel_id=1, source_target_pairs={{0,1},{1,0},{2,3},{3,2},{4,5},{5,4},{6,7},{7,6},{8,9},{9,8},{10,11... | collective-permute-start | bytes 786440 | tf_op jit(solution)/shard_map/ppermute | solution.py:408
  111.5 5.2 %collective-permute-start.3 = (bf16[4,64,128]{2,1,0:T(8,128)(2,1)S(1)}, bf16[4,64,128]{2,1,0:T(8,128)(2,1)S(1)}, u32[]{:S(2)}, u32[]{:S(2)}) collective-permute-start(bf16[4,64,128]{2,1,0:T(8,128)(2,1)S(1)} %get-tuple-element.20), channel_id=1, source_target_pairs={{0,2},{2,4},{4,6},{6,0},{8,10},{10,12},{12,14},{14,8},{16,18},{18,... | collective-permute-start | bytes 196616 | tf_op jit(solution)/shard_map/ppermute | solution.py:408
  113.3 4.9 %collective-permute-start.4 = (bf16[4,64,128]{2,1,0:T(8,128)(2,1)S(1)}, bf16[4,64,128]{2,1,0:T(8,128)(2,1)S(1)}, u32[]{:S(2)}, u32[]{:S(2)}) collective-permute-start(bf16[4,64,128]{2,1,0:T(8,128)(2,1)S(1)} %get-tuple-element.22), channel_id=1, source_target_pairs={{0,4},{2,6},{4,0},{6,2},{8,12},{10,14},{12,8},{14,10},{16,20},{18,... | collective-permute-start | bytes 196616 | tf_op jit(solution)/shard_map/ppermute | solution.py:408
  114.7 4.3 %collective-permute-start.5 = (bf16[4,64,128]{2,1,0:T(8,128)(2,1)S(1)}, bf16[4,64,128]{2,1,0:T(8,128)(2,1)S(1)}, u32[]{:S(2)}, u32[]{:S(2)}) collective-permute-start(bf16[4,64,128]{2,1,0:T(8,128)(2,1)S(1)} %get-tuple-element.21), channel_id=1, source_target_pairs={{0,6},{2,0},{4,2},{6,4},{8,14},{10,8},{12,10},{14,12},{16,22},{18,... | collective-permute-start | bytes 196616 | tf_op jit(solution)/shard_map/ppermute | solution.py:408
  119.1 6.8 %collective-permute-start.6 = (bf16[64,128]{1,0:T(8,128)(2,1)S(1)}, bf16[64,128]{1,0:T(8,128)(2,1)S(1)}, u32[]{:S(2)}, u32[]{:S(2)}) collective-permute-start(bf16[64,128]{1,0:T(8,128)(2,1)S(1)} %get-tuple-element.23), channel_id=1, source_target_pairs={{0,8},{2,10},{4,12},{6,14},{8,16},{10,18},{12,20},{14,22},{16,24},... | collective-permute-start | bytes 49160 | tf_op jit(solution)/shard_map/ppermute | solution.py:408
  120.6 5.3 %collective-permute-start.7 = (bf16[64,128]{1,0:T(8,128)(2,1)S(1)}, bf16[64,128]{1,0:T(8,128)(2,1)S(1)}, u32[]{:S(2)}, u32[]{:S(2)}) collective-permute-start(bf16[64,128]{1,0:T(8,128)(2,1)S(1)} %get-tuple-element.25), channel_id=1, source_target_pairs={{0,16},{2,18},{4,20},{6,22},{8,24},{10,26},{12,28},{14,30},{16,0},... | collective-permute-start | bytes 49160 | tf_op jit(solution)/shard_map/ppermute | solution.py:408
  123.1 3.7 %collective-permute-start.8 = (bf16[64,128]{1,0:T(8,128)(2,1)S(1)}, bf16[64,128]{1,0:T(8,128)(2,1)S(1)}, u32[]{:S(2)}, u32[]{:S(2)}) collective-permute-start(bf16[64,128]{1,0:T(8,128)(2,1)S(1)} %get-tuple-element.24), channel_id=1, source_target_pairs={{0,24},{2,26},{4,28},{6,30},{8,0},{10,2},{12,4},{14,6},{16,8},{18,... | collective-permute-start | bytes 49160 | tf_op jit(solution)/shard_map/ppermute | solution.py:408

commit v10 on v8

--- a/solution.py
+++ b/solution.py
@@ -256,20 +256,21 @@
             hbm.at[rows, block], buf.at[slot, rows], sem.at[slot, side]
         )
 
-    def start(hbm, buf, sem, step):
+    def start(step):
         for q in range(sides):
-            arriving(hbm, buf, sem, step, q).start()
+            arriving(amp_hbm, amp_buf, amp_sem, step, q).start()
+        for q in range(sides):
+            arriving(factor_hbm, factor_buf, factor_sem, step, q).start()
 
     @pl.when(step == 0)
     def _():
-        start(amp_hbm, amp_buf, amp_sem, step)
+        start(step)
         out_ref[...] = jnp.zeros_like(out_ref)
         swap[...] = swap_matrix(deep)
 
-    @pl.when((step > 0) & (step + 1 < steps))
-    def _():
-        start(amp_hbm, amp_buf, amp_sem, step + 1)
-        start(factor_hbm, factor_buf, factor_sem, step + 1)
+    @pl.when(step + 1 < steps)
+    def _():
+        start(step + 1)
 
     def later(jobs):
         store = None
@@ -295,19 +296,7 @@
 
     for q in range(sides):
         arriving(amp_hbm, amp_buf, amp_sem, step, q).wait()
-        size = virtuals // sides
-        later(
-            functools.partial(reorder, k) for k in range(q * size, (q + 1) * size, 2 * deep)
-        )
-
-    @pl.when(step == 0)
-    def _():
-        start(factor_hbm, factor_buf, factor_sem, step)
-
-    @pl.when((step == 0) & (steps > 1))
-    def _():
-        start(amp_hbm, amp_buf, amp_sem, step + 1)
-        start(factor_hbm, factor_buf, factor_sem, step + 1)
+    later(functools.partial(reorder, k) for k in range(0, virtuals, 2 * deep))
 
     row = jnp.concatenate([row_ref[k] for k in range(count)], axis=1)
 
@@ -335,9 +324,9 @@
 
         return store
 
-    later(functools.partial(flatten, k) for k in range(0, chol, 4 * deep))
     for q in range(sides):
         arriving(factor_hbm, factor_buf, factor_sem, step, q).wait()
+    later(functools.partial(flatten, k) for k in range(0, chol, 4 * deep))
     columns = 512
 
     def ladder(first):

time: 128 us -> 124 us (0.969)
  Pallas kernels: 87.6 us -> 83.8 us
    pallas_call x1, Pallas kernels: 71.3 us -> 67.5 us  [ladder_partial(): pl.pallas_call(functools.partial(ladder_kernel, sides), grid=(slab // dee...]
  transfers between devices with their start and end apart: 11 -> 11, of which waited for: 6 -> 6; matrix products, arithmetic and copies ran while one was open for 3% -> 3% of each run, Pallas kernels for 69% -> 68%
where the time goes in v10:
time: 124 us
  Pallas kernels  83.8 us (68%)
  starting transfers between devices  23.5 us (19%)
  waiting for transfers between devices  7.66 us (6%)
  other arithmetic  4.73 us (4%)
  local copies, waits for them, and re-layouts  3.07 us (2%)
    pallas_call x1, Pallas kernels, ladder_partial(): pl.pallas_call(functools.partial(ladder_kernel, sides), grid=(slab // dee...  67.5 us
    ppermute x7, starting transfers between devices, scatter_sum(): total = total + lax.ppermute(piece, axes, pairs).astype(f32)  10.4 us
    pallas_call x1, Pallas kernels, cycle_partial(): pl.pallas_call(functools.partial(cycle_kernel, shares, len(amps)), grid=(...  9.86 us
    pallas_call x1, Pallas kernels, own_row(): pl.pallas_call(row_kernel, grid=(chol // LANES, steps), in_specs=[side(q)...  6.43 us
    all_to_all x1, starting transfers between devices, local(): row = lax.all_to_all(row, 'vir', 0, 0)  6.29 us
    all_to_all x1, waiting for transfers between devices, local(): row = lax.all_to_all(row, 'vir', 0, 0)  4.02 us
    all_to_all x1, starting transfers between devices, local(): lax.all_to_all(cycle_partial(amps, codes, ov_slots), ('vir', 'ph', 'vec')...  3.68 us
    ppermute x7, waiting for transfers between devices, scatter_sum(): total = total + lax.ppermute(piece, axes, pairs).astype(f32)  3.63 us
  transfers between devices with their start and end apart: 11, of which 6 were waited for; matrix products, arithmetic and copies ran while one was open for 3% of the time, Pallas kernels for 68%

profile of v10, /device:TPU:0, one launch (start us, length us, event | category | flops | bytes accessed | tf_op | source)
XLA Modules:
  0.0 123.7 jit_solution(10880132656528829383)
XLA Ops:
  0.6 1.1 fusion.14
  1.8 0.1 pad_maximum_fusion.refs_2_
  1.9 3.0 %collective-permute-start = (bf16[32,32,128]{2,1,0:T(8,128)(2,1)S(1)}, bf16[32,32,128]{2,1,0:T(8,128)(2,1)S(1)}, u32[]{:S(2)}, u32[]{:S(2)}) collective-permute-start(bf16[32,32,128]{2,1,0:T(8,128)(2,1)S(1)} %pad_maximum_fusion.refs_2_), channel_id=1, source_target_pairs={{0,2},{2,0},{1,3},{3,1},{4,6},{6,4},{5,7},{7,5},{8,10},{10,8},{9,1... | collective-permute-start | bytes 786440 | tf_op jit(solution)/shard_map/ppermute | solution.py:93
  5.0 0.7 multiply_add_fusion.refs_0_
  5.7 6.4 %shard_map.104 = bf16[8,256,128]{2,1,0:T(8,128)(2,1)} custom-call(bf16[256,128,1024]{2,1,0:T(8,128)(2,1)} %factor_hbm.1, bf16[256,128,1024]{2,1,0:T(8,128)(2,1)} %factor_hbm.1, bf16[256,128,1024]{2,1,0:T(8,128)(2,1)} %factor_hbm.1, bf16[256,128,1024]{2,1,0:T(8,128)(2,1)} %factor_hbm.1), custom_call_target="tpu_custom_call" | custom-call | flops 8388608 | bytes 8388608 | tf_op jit(solution)/shard_map/pallas_call | solution.py:134
  12.2 6.3 %all-to-all-start = ((bf16[8,256,128]{2,1,0:T(8,128)(2,1)}), bf16[8,256,128]{2,1,0:T(8,128)(2,1)S(1)}, u32[]{:S(2)}, u32[]{:S(2)}) async-start(bf16[8,256,128]{2,1,0:T(8,128)(2,1)} %shard_map.104), calls=%async_computation | async-start | bytes 1048576 | tf_op jit(solution)/shard_map/all_to_all | solution.py:412
  18.5 9.9 %shard_map.106 = f32[32,32,256]{2,1,0:T(8,128)} custom-call(s32[1]{0:T(128)} %bitcast.2.place_ref, s32[64]{0:T(128)} %copy-done.5, s32[64]{0:T(128)} %copy-done.6, bf16[32,32,128]{2,1,0:T(8,128)(2,1)} %copy-done.2, bf16[32,32,128]{2,1,0:T(8,128)(2,1)} %copy-done.3, bf16[128,64,1024]{2,1,0:T(8,128)(2,1)} %bitcast.60, bf16[128,64,1024]{2,1,0:T(8,128)(2,1)} %bitcast.61, ...), custom_call_target="tpu_custom_call" | custom-call | flops 536870912 | bytes 16777216 | tf_op jit(solution)/shard_map/pallas_call | solution.py:214
  28.4 4.0 %all-to-all-done.row_ref = bf16[8,256,128]{2,1,0:T(8,128)(2,1)S(1)} async-done(((bf16[8,256,128]{2,1,0:T(8,128)(2,1)}), bf16[8,256,128]{2,1,0:T(8,128)(2,1)S(1)}, u32[]{:S(2)}, u32[]{:S(2)}) %all-to-all-start) | async-done | bytes 524320 | tf_op jit(solution)/shard_map/all_to_all | solution.py:412
  32.4 3.7 %all-to-all-start.1 = ((f32[32,32,256]{2,1,0:T(8,128)}), f32[32,32,256]{2,1,0:T(8,128)S(1)}, u32[]{:S(2)}, u32[]{:S(2)}) async-start(f32[32,32,256]{2,1,0:T(8,128)} %shard_map.106), calls=%async_computation.1 | async-start | bytes 2097152 | tf_op jit(solution)/shard_map/all_to_all | solution.py:413
  36.1 67.5 %shard_map.105 = f32[256,1024]{1,0:T(8,128)} custom-call(bf16[8,256,128]{2,1,0:T(8,128)(2,1)} %copy-done.1, bf16[1024,128,256]{2,1,0:T(8,128)(2,1)} %amp_hbm.1, bf16[256,128,1024]{2,1,0:T(8,128)(2,1)} %factor_hbm.1), custom_call_target="tpu_custom_call" | custom-call | flops 34359738368 | bytes 134217728 | tf_op jit(solution)/shard_map/pallas_call | solution.py:349
  103.7 0.2 fusion
  103.9 0.1 copy.24
  104.1 0.2 broadcast_in_dim.62
  104.2 1.4 %select_add_fusion = f32[2,2,64,1024]{3,2,1,0:T(8,128)S(1)} fusion(f32[2,2,64,1024]{3,2,1,0:T(8,128)} %bitcast.64, f32[2,2,64,1024]{3,2,1,0:T(8,128)S(1)} %broadcast_in_dim.62, pred[1024]{0:T(1024)(128)(4,1)S(1)} %broadcast_bitcast_fusion), kind=kLoop, calls=%fused_computation | loop fusion | flops 524288 | bytes 3146752 | tf_op jit(solution)/shard_map/add | solution.py:423
  105.7 0.3 collective-permute-start.2
  106.0 1.2 slice.3
  107.2 0.1 collective-permute-done.2
  107.4 0.1 copy.20
  107.5 0.1 copy.19
  107.7 1.8 %collective-permute-start.3 = (bf16[4,64,128]{2,1,0:T(8,128)(2,1)S(1)}, bf16[4,64,128]{2,1,0:T(8,128)(2,1)S(1)}, u32[]{:S(2)}, u32[]{:S(2)}) collective-permute-start(bf16[4,64,128]{2,1,0:T(8,128)(2,1)S(1)} %get-tuple-element.20), channel_id=1, source_target_pairs={{0,2},{2,4},{4,6},{6,0},{8,10},{10,12},{12,14},{14,8},{16,18},{18,... | collective-permute-start | bytes 196616 | tf_op jit(solution)/shard_map/ppermute | solution.py:394
  109.5 1.5 %collective-permute-start.4 = (bf16[4,64,128]{2,1,0:T(8,128)(2,1)S(1)}, bf16[4,64,128]{2,1,0:T(8,128)(2,1)S(1)}, u32[]{:S(2)}, u32[]{:S(2)}) collective-permute-start(bf16[4,64,128]{2,1,0:T(8,128)(2,1)S(1)} %get-tuple-element.22), channel_id=1, source_target_pairs={{0,4},{2,6},{4,0},{6,2},{8,12},{10,14},{12,8},{14,10},{16,20},{18,... | collective-permute-start | bytes 196616 | tf_op jit(solution)/shard_map/ppermute | solution.py:394
  111.0 1.5 %collective-permute-start.5 = (bf16[4,64,128]{2,1,0:T(8,128)(2,1)S(1)}, bf16[4,64,128]{2,1,0:T(8,128)(2,1)S(1)}, u32[]{:S(2)}, u32[]{:S(2)}) collective-permute-start(bf16[4,64,128]{2,1,0:T(8,128)(2,1)S(1)} %get-tuple-element.21), channel_id=1, source_target_pairs={{0,6},{2,0},{4,2},{6,4},{8,14},{10,8},{12,10},{14,12},{16,22},{18,... | collective-permute-start | bytes 196616 | tf_op jit(solution)/shard_map/ppermute | solution.py:394
  112.4 0.2 select_reduce_fusion.1
  112.6 0.3 collective-permute-done.3
  112.9 1.5 %collective-permute-done.4 = bf16[4,64,128]{2,1,0:T(8,128)(2,1)S(1)} collective-permute-done((bf16[4,64,128]{2,1,0:T(8,128)(2,1)S(1)}, bf16[4,64,128]{2,1,0:T(8,128)(2,1)S(1)}, u32[]{:S(2)}, u32[]{:S(2)}) %collective-permute-start.4) | collective-permute-done | bytes 65568 | tf_op jit(solution)/shard_map/ppermute | solution.py:394
  114.4 0.8 collective-permute-done.5
  115.3 1.5 %collective-permute-start.6 = (bf16[64,128]{1,0:T(8,128)(2,1)S(1)}, bf16[64,128]{1,0:T(8,128)(2,1)S(1)}, u32[]{:S(2)}, u32[]{:S(2)}) collective-permute-start(bf16[64,128]{1,0:T(8,128)(2,1)S(1)} %get-tuple-element.23), channel_id=1, source_target_pairs={{0,8},{2,10},{4,12},{6,14},{8,16},{10,18},{12,20},{14,22},{16,24},... | collective-permute-start | bytes 49160 | tf_op jit(solution)/shard_map/ppermute | solution.py:394
  116.8 2.5 %collective-permute-start.7 = (bf16[64,128]{1,0:T(8,128)(2,1)S(1)}, bf16[64,128]{1,0:T(8,128)(2,1)S(1)}, u32[]{:S(2)}, u32[]{:S(2)}) collective-permute-start(bf16[64,128]{1,0:T(8,128)(2,1)S(1)} %get-tuple-element.25), channel_id=1, source_target_pairs={{0,16},{2,18},{4,20},{6,22},{8,24},{10,26},{12,28},{14,30},{16,0},... | collective-permute-start | bytes 49160 | tf_op jit(solution)/shard_map/ppermute | solution.py:394
  119.3 1.4 %collective-permute-start.8 = (bf16[64,128]{1,0:T(8,128)(2,1)S(1)}, bf16[64,128]{1,0:T(8,128)(2,1)S(1)}, u32[]{:S(2)}, u32[]{:S(2)}) collective-permute-start(bf16[64,128]{1,0:T(8,128)(2,1)S(1)} %get-tuple-element.24), channel_id=1, source_target_pairs={{0,24},{2,26},{4,28},{6,30},{8,0},{10,2},{12,4},{14,6},{16,8},{18,... | collective-permute-start | bytes 49160 | tf_op jit(solution)/shard_map/ppermute | solution.py:394
  120.7 1.4 %dynamic-slice_add_fusion = f32[128]{0:T(128)S(1)} fusion(f32[1024]{0:T(1024)} %param.16, s32[]{:T(128)S(6)} %select_n.165, f32[]{:T(128)} %bitcast.19), kind=kLoop, calls=%fused_computation.37 | loop fusion | flops 128 | bytes 1032 | tf_op jit(solution)/shard_map/add | solution.py:441
  122.1 0.9 collective-permute-done.8
  123.0 0.7 subtract_divide_fusion
  (32 shorter events, 0.6 us)
Async XLA Ops:
  0.6 103.1 %copy-start = (bf16[256,8,128]{2,1,0:T(8,128)(2,1)S(1)}, bf16[256,8,128]{2,1,0:T(8,128)(2,1)}, u32[]{:S(2)}) copy-start(bf16[256,8,128]{2,1,0:T(8,128)(2,1)} %param.15) | copy-start | bytes 1572868
  1.9 10.2 %copy-start.2 = (bf16[32,32,128]{2,1,0:T(8,128)(2,1)}, bf16[32,32,128]{2,1,0:T(8,128)(2,1)S(1)}, u32[]{:S(2)}) copy-start(bf16[32,32,128]{2,1,0:T(8,128)(2,1)S(1)} %pad_maximum_fusion.refs_2_) | copy-start | bytes 786436
  1.9 10.2 %collective-permute-start = (bf16[32,32,128]{2,1,0:T(8,128)(2,1)S(1)}, bf16[32,32,128]{2,1,0:T(8,128)(2,1)S(1)}, u32[]{:S(2)}, u32[]{:S(2)}) collective-permute-start(bf16[32,32,128]{2,1,0:T(8,128)(2,1)S(1)} %pad_maximum_fusion.refs_2_), channel_id=1, source_target_pairs={{0,2},{2,0},{1,3},{3,1},{4,6},{6,4},{5,7},{7,5},{8,10},{10,8},{9,1... | collective-permute-start | bytes 786440 | tf_op jit(solution)/shard_map/ppermute | solution.py:93
  5.6 6.5 %copy-start.5 = (s32[64]{0:T(128)}, s32[64]{0:T(128)S(1)}, u32[]{:S(2)}) copy-start(s32[64]{0:T(128)S(1)} %multiply_add_fusion.refs_0_) | copy-start | bytes 772
  5.6 6.5 %collective-permute-start.1 = (s32[64]{0:T(128)S(1)}, s32[64]{0:T(128)S(1)}, u32[]{:S(2)}, u32[]{:S(2)}) collective-permute-start(s32[64]{0:T(128)S(1)} %multiply_add_fusion.refs_0_), channel_id=1, source_target_pairs={{0,2},{2,0},{1,3},{3,1},{4,6},{6,4},{5,7},{7,5},{8,10},{10,8},{9,1... | collective-permute-start | bytes 776 | tf_op jit(solution)/shard_map/ppermute | solution.py:93
  12.1 6.4 %copy-start.6 = (s32[64]{0:T(128)}, s32[64]{0:T(128)S(1)}, u32[]{:S(2)}) copy-start(s32[64]{0:T(128)S(1)} %collective-permute-done.1.refs_1_) | copy-start | bytes 772
  12.1 6.4 %copy-start.3 = (bf16[32,32,128]{2,1,0:T(8,128)(2,1)}, bf16[32,32,128]{2,1,0:T(8,128)(2,1)S(1)}, u32[]{:S(2)}) copy-start(bf16[32,32,128]{2,1,0:T(8,128)(2,1)S(1)} %collective-permute-done.refs_3_) | copy-start | bytes 786436
  12.2 20.3 %all-to-all-start = ((bf16[8,256,128]{2,1,0:T(8,128)(2,1)}), bf16[8,256,128]{2,1,0:T(8,128)(2,1)S(1)}, u32[]{:S(2)}, u32[]{:S(2)}) async-start(bf16[8,256,128]{2,1,0:T(8,128)(2,1)} %shard_map.104), calls=%async_computation | async-start | bytes 1048576 | tf_op jit(solution)/shard_map/all_to_all | solution.py:412
  32.4 3.7 %copy-start.1 = (bf16[8,256,128]{2,1,0:T(8,128)(2,1)}, bf16[8,256,128]{2,1,0:T(8,128)(2,1)S(1)}, u32[]{:S(2)}) copy-start(bf16[8,256,128]{2,1,0:T(8,128)(2,1)S(1)} %all-to-all-done.row_ref) | copy-start | bytes 1572868
  32.4 71.2 %all-to-all-start.1 = ((f32[32,32,256]{2,1,0:T(8,128)}), f32[32,32,256]{2,1,0:T(8,128)S(1)}, u32[]{:S(2)}, u32[]{:S(2)}) async-start(f32[32,32,256]{2,1,0:T(8,128)} %shard_map.106), calls=%async_computation.1 | async-start | bytes 2097152 | tf_op jit(solution)/shard_map/all_to_all | solution.py:413
  36.1 76.3 %copy-start.4 = (f32[128]{0:T(128)S(1)}, f32[128]{0:T(128)}, u32[]{:S(2)}) copy-start(f32[128]{0:T(128)} %param.17) | copy-start | bytes 1540
  105.7 1.6 %collective-permute-start.2 = (bf16[2,64,1024]{2,1,0:T(8,128)(2,1)S(1)}, bf16[2,64,1024]{2,1,0:T(8,128)(2,1)S(1)}, u32[]{:S(2)}, u32[]{:S(2)}) collective-permute-start(bf16[2,64,1024]{2,1,0:T(8,128)(2,1)S(1)} %fusion.2), channel_id=1, source_target_pairs={{0,1},{1,0},{2,3},{3,2},{4,5},{5,4},{6,7},{7,6},{8,9},{9,8},{10,11... | collective-permute-start | bytes 786440 | tf_op jit(solution)/shard_map/ppermute | solution.py:394
  107.7 5.2 %collective-permute-start.3 = (bf16[4,64,128]{2,1,0:T(8,128)(2,1)S(1)}, bf16[4,64,128]{2,1,0:T(8,128)(2,1)S(1)}, u32[]{:S(2)}, u32[]{:S(2)}) collective-permute-start(bf16[4,64,128]{2,1,0:T(8,128)(2,1)S(1)} %get-tuple-element.20), channel_id=1, source_target_pairs={{0,2},{2,4},{4,6},{6,0},{8,10},{10,12},{12,14},{14,8},{16,18},{18,... | collective-permute-start | bytes 196616 | tf_op jit(solution)/shard_map/ppermute | solution.py:394
  109.5 4.9 %collective-permute-start.4 = (bf16[4,64,128]{2,1,0:T(8,128)(2,1)S(1)}, bf16[4,64,128]{2,1,0:T(8,128)(2,1)S(1)}, u32[]{:S(2)}, u32[]{:S(2)}) collective-permute-start(bf16[4,64,128]{2,1,0:T(8,128)(2,1)S(1)} %get-tuple-element.22), channel_id=1, source_target_pairs={{0,4},{2,6},{4,0},{6,2},{8,12},{10,14},{12,8},{14,10},{16,20},{18,... | collective-permute-start | bytes 196616 | tf_op jit(solution)/shard_map/ppermute | solution.py:394
  111.0 4.3 %collective-permute-start.5 = (bf16[4,64,128]{2,1,0:T(8,128)(2,1)S(1)}, bf16[4,64,128]{2,1,0:T(8,128)(2,1)S(1)}, u32[]{:S(2)}, u32[]{:S(2)}) collective-permute-start(bf16[4,64,128]{2,1,0:T(8,128)(2,1)S(1)} %get-tuple-element.21), channel_id=1, source_target_pairs={{0,6},{2,0},{4,2},{6,4},{8,14},{10,8},{12,10},{14,12},{16,22},{18,... | collective-permute-start | bytes 196616 | tf_op jit(solution)/shard_map/ppermute | solution.py:394
  115.3 6.8 %collective-permute-start.6 = (bf16[64,128]{1,0:T(8,128)(2,1)S(1)}, bf16[64,128]{1,0:T(8,128)(2,1)S(1)}, u32[]{:S(2)}, u32[]{:S(2)}) collective-permute-start(bf16[64,128]{1,0:T(8,128)(2,1)S(1)} %get-tuple-element.23), channel_id=1, source_target_pairs={{0,8},{2,10},{4,12},{6,14},{8,16},{10,18},{12,20},{14,22},{16,24},... | collective-permute-start | bytes 49160 | tf_op jit(solution)/shard_map/ppermute | solution.py:394
  116.8 5.3 %collective-permute-start.7 = (bf16[64,128]{1,0:T(8,128)(2,1)S(1)}, bf16[64,128]{1,0:T(8,128)(2,1)S(1)}, u32[]{:S(2)}, u32[]{:S(2)}) collective-permute-start(bf16[64,128]{1,0:T(8,128)(2,1)S(1)} %get-tuple-element.25), channel_id=1, source_target_pairs={{0,16},{2,18},{4,20},{6,22},{8,24},{10,26},{12,28},{14,30},{16,0},... | collective-permute-start | bytes 49160 | tf_op jit(solution)/shard_map/ppermute | solution.py:394
  119.3 3.7 %collective-permute-start.8 = (bf16[64,128]{1,0:T(8,128)(2,1)S(1)}, bf16[64,128]{1,0:T(8,128)(2,1)S(1)}, u32[]{:S(2)}, u32[]{:S(2)}) collective-permute-start(bf16[64,128]{1,0:T(8,128)(2,1)S(1)} %get-tuple-element.24), channel_id=1, source_target_pairs={{0,24},{2,26},{4,28},{6,30},{8,0},{10,2},{12,4},{14,6},{16,8},{18,... | collective-permute-start | bytes 49160 | tf_op jit(solution)/shard_map/ppermute | solution.py:394
